TPU v7x, 32 devices: a whole 2x2x4 slice. The times are simulated.
32 devices in a mesh: dom: 8 (over z, x), face: 4 (over y, core).
Axes of the slice: x: 2, y: 2, z: 4, core: 2. Of those that a mesh axis runs over, the one named last changes fastest.
Arguments:
- start: float32 [64, 4096], P(None, ('dom', 'face')), may hold values from -6 to 6
- rhs: float32 [64, 4096], P(None, ('dom', 'face')), may hold values from -6 to 6
- diag_block: bfloat16 [64, 64, 4096], P(None, None, ('dom', 'face'))
- precond: bfloat16 [64, 64, 4096], P(None, None, ('dom', 'face'))
- lift: float32 [6, 16, 64], replicated, may hold values from -0.625 to 0.625
- neighbour: int32 [6, 4096], P(None, ('dom', 'face')), may hold values from 0 to 831, as said below
- orient: int32 [6, 4096], P(None, ('dom', 'face')), may hold values from 0 to 7
- owner: int32 [4096], P(('dom', 'face')), may hold values from 0 to 7, as said below
- slot: int32 [4096], P(('dom', 'face')), may hold values from 0 to 63
Outputs:
- solution: float32 [64, 4096], P(None, ('dom', 'face'))
- coarse_op: float32 [729, 2048], P(None, ('dom', 'face'))
- coarse_rhs: float32 [27, 2048], P(None, ('dom', 'face'))
Inputs may be any that keep to these rules, and one draw needn't show every extreme that they name: neighbour of face 2 of local element e < 32 is 768 + e; of face 3 of local element 128 - 32 + j it is 800 + j; every other face f points to a face-(f xor 1) trace of a local element, below 768. Local elements 0 .. 31 of a device are owned by its own dom index, all others by another dom index; from the elements of one device at most 28 go to one owner, and some owner receives exactly 28 from each device.
All inputs are finite; a program needn't handle non-finite values.
Results may differ from a plain program's by a relative error of at most 0.0029.
Values may be sent and summed in bfloat16 or wider, within the bound.
No kernel may reach another device: no remote copies, remote signals or barrier semaphores. Data moves between devices by JAX's collectives and lax.ppermute only.
A program may use at most 64 MiB of HBM per device.

v0:
```python
import jax
import jax.numpy as jnp
import numpy as np
from jax import lax
from jax.sharding import PartitionSpec as P

SWEEPS = 2


def with_halo(cells, sides, width):
    for axis, dim in sides:
        count = lax.axis_size(axis)
        ends = count - 1
        head = lax.slice_in_dim(cells, 0, width, axis=dim)
        tail = lax.slice_in_dim(cells, cells.shape[dim] - width, cells.shape[dim], axis=dim)
        cells = jnp.concatenate(
            [
                lax.ppermute(tail, axis, [(i, (i + 1) % count) for i in range(ends)]),
                cells,
                lax.ppermute(head, axis, [((i + 1) % count, i) for i in range(ends)]),
            ],
            axis=dim,
        )
    return cells


def turn_table():
    square = np.arange(16).reshape(4, 4)
    tables = []
    for turn in range(8):
        layout = square.T if turn & 4 else square
        if turn & 1:
            layout = layout[::-1, :]
        if turn & 2:
            layout = layout[:, ::-1]
        tables.append(layout.reshape(16))
    return np.stack(tables)


def restrict_table():
    fine_nodes = np.array([-1.0, -1.0 / np.sqrt(5.0), 1.0 / np.sqrt(5.0), 1.0])
    coarse_nodes = np.array([-1.0, 0.0, 1.0])
    basis = np.ones((4, 3))
    for column in range(3):
        for other in range(3):
            if other != column:
                basis[:, column] *= (fine_nodes - coarse_nodes[other]) / (
                    coarse_nodes[column] - coarse_nodes[other]
                )
    prolong = (
        basis[:, None, None, :, None, None]
        * basis[None, :, None, None, :, None]
        * basis[None, None, :, None, None, :]
    ).reshape(64, 27)
    return prolong.T.astype(np.float32)


def face_traces(values):
    cube = values.reshape(4, 4, 4, -1)
    planes = [cube[0], cube[3], cube[:, 0], cube[:, 3], cube[:, :, 0], cube[:, :, 3]]
    return jnp.stack([plane.reshape(16, -1) for plane in planes])


def couple(face_vals, low_in, high_in, neighbour, orient, lift):
    local_count = face_vals.shape[2]
    pool = jnp.concatenate(
        [face_vals.transpose(1, 0, 2).reshape(16, 6 * local_count), low_in, high_in], 1
    )
    picked = jnp.take(pool, neighbour.reshape(-1), axis=1).reshape(16, 6, local_count)
    tables = turn_table()
    turned = jnp.zeros_like(picked)
    for turn in range(8):
        turned = turned + jnp.where(orient[None, :, :] == turn, picked[tables[turn]], 0.0)
    return jnp.einsum("kfn,fke->ne", lift, turned, precision=lax.Precision.HIGHEST)


def galerkin(blocks, rtab):
    half = jnp.einsum(
        "cn,nms->cms",
        rtab,
        blocks,
        precision=lax.Precision.HIGHEST,
        preferred_element_type=jnp.float32,
    )
    return jnp.einsum("cms,dm->cds", half, rtab, precision=lax.Precision.HIGHEST)


def restrict(values, rtab):
    return jnp.einsum(
        "cn,ne->ce",
        rtab,
        values,
        precision=lax.Precision.HIGHEST,
        preferred_element_type=jnp.float32,
    )


def per_device(start, rhs, diag_block, precond, lift, neighbour, orient, owner, slot):
    local_count = start.shape[1]
    edge_width = local_count // 4
    staying = local_count // 4
    aggregates_here = local_count // 2
    rtab = jnp.asarray(restrict_table(), dtype=jnp.float32)

    def residual_of(values):
        face_vals = face_traces(values)
        rim_traces = jnp.concatenate(
            [face_vals[2][:, :edge_width], face_vals[3][:, local_count - edge_width :]], 1
        )
        extended = with_halo(rim_traces, (("face", 1),), edge_width)
        product = jnp.einsum(
            "nme,me->ne",
            diag_block,
            values,
            precision=lax.Precision.HIGHEST,
            preferred_element_type=jnp.float32,
        )
        coupled = couple(
            face_vals,
            extended[:, :edge_width],
            extended[:, 3 * edge_width :],
            neighbour,
            orient,
            lift,
        )
        return rhs - (product - coupled)

    solution = start
    for sweep_idx in range(SWEEPS):
        resid = residual_of(solution)
        solution = solution + jnp.einsum(
            "nme,me->ne",
            precond,
            resid,
            precision=lax.Precision.HIGHEST,
            preferred_element_type=jnp.float32,
        )
    resid = residual_of(solution)
    resid_low = lax.optimization_barrier(resid.astype(jnp.bfloat16))
    owner_count = lax.axis_size("dom")
    movers = local_count - staying
    capacity = 2 * ((movers + owner_count - 2) // (owner_count - 1))
    total_slots = owner_count * capacity
    positions = jnp.arange(local_count, dtype=jnp.int32)
    moving = positions >= staying
    hits = (
        (owner[:, None] == jnp.arange(owner_count, dtype=jnp.int32)[None, :]) & moving[:, None]
    ).astype(jnp.int32)
    earlier = jnp.cumsum(hits, 0) - hits
    rank_of = jnp.sum(earlier * hits, 1)
    target = jnp.where(moving, owner * capacity + rank_of, total_slots)
    slot_send = (
        jnp.full((1, total_slots), -1, jnp.int32).at[:, target].set(slot[None, :], mode="drop")
    )
    slot_send = slot_send.reshape(1, owner_count, capacity)
    local_op = galerkin(diag_block, rtab).reshape(729, local_count)
    local_rhs = restrict(resid_low, rtab)
    op_send = (
        jnp.zeros((729, total_slots), jnp.float32)
        .at[:, target]
        .set(local_op, mode="drop")
        .reshape(729, owner_count, capacity)
    )
    rhs_send = (
        jnp.zeros((27, total_slots), jnp.float32)
        .at[:, target]
        .set(local_rhs, mode="drop")
        .reshape(27, owner_count, capacity)
    )
    got_op, got_rhs, got_slot = (
        lax.all_to_all(op_send, "dom", split_axis=1, concat_axis=1, tiled=True),
        lax.all_to_all(rhs_send, "dom", split_axis=1, concat_axis=1, tiled=True),
        lax.all_to_all(slot_send, "dom", split_axis=1, concat_axis=1, tiled=True),
    )
    stay_op = local_op[:, :staying]
    stay_rhs = local_rhs[:, :staying]
    columns_op = jnp.concatenate([got_op.reshape(729, total_slots), stay_op], 1)
    columns_rhs = jnp.concatenate([got_rhs.reshape(27, total_slots), stay_rhs], 1)
    slot_ids = jnp.concatenate([got_slot.reshape(total_slots), slot[:staying]])
    slot_ids = jnp.where(slot_ids < 0, aggregates_here, slot_ids)
    coarse_op = (
        jnp.zeros((729, aggregates_here), jnp.float32).at[:, slot_ids].add(columns_op, mode="drop")
    )
    coarse_rhs = (
        jnp.zeros((27, aggregates_here), jnp.float32).at[:, slot_ids].add(columns_rhs, mode="drop")
    )
    return (solution, coarse_op, coarse_rhs)


def solution(mesh):
    return jax.shard_map(
        per_device,
        mesh=mesh,
        in_specs=(
            P(None, ("dom", "face")),
            P(None, ("dom", "face")),
            P(None, None, ("dom", "face")),
            P(None, None, ("dom", "face")),
            P(),
            P(None, ("dom", "face")),
            P(None, ("dom", "face")),
            P(("dom", "face")),
            P(("dom", "face")),
        ),
        out_specs=(P(None, ("dom", "face")), P(None, ("dom", "face")), P(None, ("dom", "face"))),
        check_vma=False,
    )
```

profile of v0, /device:TPU:0, one launch (start us, length us, event | category | flops | bytes accessed | tf_op | source)
XLA Modules:
  0.0 121.7 jit_solution(6721870433222111880)
XLA Ops:
  0.7 0.8 fusion.43
  1.6 2.3 %collective-permute-start = (f32[16,32]{1,0:T(8,128)S(1)}, f32[16,32]{1,0:T(8,128)S(1)}, u32[]{:S(2)}, u32[]{:S(2)}) collective-permute-start(f32[16,32]{1,0:T(8,128)S(1)} %slice.172), channel_id=1, source_target_pairs={{0,1},{1,2},{2,3},{4,5},{5,6},{6,7},{8,9},{9,10},{10,11},{12,13},{... | collective-permute-start | bytes 6152 | tf_op jit(solution)/shard_map/ppermute | solution.py:18
  3.9 1.3 %collective-permute-start.1 = (f32[16,32]{1,0:T(8,128)S(1)}, f32[16,32]{1,0:T(8,128)S(1)}, u32[]{:S(2)}, u32[]{:S(2)}) collective-permute-start(f32[16,32]{1,0:T(8,128)S(1)} %bitcast.223), channel_id=1, source_target_pairs={{1,0},{2,1},{3,2},{5,4},{6,5},{7,6},{9,8},{10,9},{11,10},{13,12},{... | collective-permute-start | bytes 6152 | tf_op jit(solution)/shard_map/ppermute | solution.py:20
  5.2 0.8 fusion.28
  6.2 0.8 select_reduce_fusion
  7.7 1.1 scatter_custom_fusion
  9.4 6.6 %all-to-all-start = ((s32[1,8,28]{2,0,1:T(1,128)}), s32[1,8,28]{2,0,1:T(1,128)}, u32[]{:S(2)}, u32[]{:S(2)}) async-start(s32[1,8,28]{2,0,1:T(1,128)} %reshape.168), calls=%async_computation | async-start | bytes 8192 | tf_op jit(solution)/shard_map/all_to_all | solution.py:173
  17.5 0.8 fusion.42
  19.0 1.3 %broadcast_compare_fusion.7 = (pred[6,128]{1,0:T(8,128)(4,1)}, pred[6,128]{1,0:T(8,128)(4,1)}, pred[6,128]{1,0:T(8,128)(4,1)}, pred[6,128]{1,0:T(8,128)(4,1)}, p...) fusion(s32[6,128]{1,0:T(8,128)} %param.66), kind=kLoop, calls=%fused_computation.138 | loop fusion | flops 6144 | bytes 9216 | tf_op jit(solution)/shard_map/eq | solution.py:73
  21.0 1.6 %fusion.2 = f32[128,64]{0,1:T(8,128)S(1)} fusion(f32[128,64]{0,1:T(8,128)} %bitcast.211, bf16[64,64,128]{2,1,0:T(8,128)(2,1)} %param.62), kind=kLoop, calls=%fused_computation.39 | loop fusion | flops 1564672 | bytes 1114112 | tf_op jit(solution)/shard_map/nme,me->ne/dot_general | solution.py:111
  22.7 1.1 fusion.17
  24.9 1.6 %gather_fusion.24 = f32[768,16]{1,0:T(8,128)S(1)} fusion(f32[16,832]{0,1:T(8,128)S(1)} %copy.186, s32[1024]{0:T(1024)S(1)} %pad_clamp_fusion.8), kind=kCustom, calls=%fused_computation.clone | custom fusion | bytes 101376 | tf_op jit(solution)/shard_map/jit(_take)/gather | solution.py:69
  28.6 1.2 gather_fusion.4
  29.8 1.2 gather_fusion.3
  31.0 1.2 gather_fusion.2
  32.2 1.2 gather_fusion.1
  33.4 1.4 %gather_fusion = f32[16,6,128]{2,1,0:T(8,128)} fusion(f32[16,6,128]{2,1,0:T(8,128)S(1)} %copy.187, s32[1024]{0:T(1024)} %get-tuple-element.43), kind=kCustom, calls=%fused_computation.3 | custom fusion | bytes 98368 | tf_op jit(solution)/shard_map/gather | solution.py:73
  34.8 1.0 select_add_fusion.2
  36.7 4.0 %collective-permute-start.2 = (f32[16,32]{1,0:T(8,128)S(1)}, f32[16,32]{1,0:T(8,128)S(1)}, u32[]{:S(2)}, u32[]{:S(2)}) collective-permute-start(f32[16,32]{1,0:T(8,128)S(1)} %slice.180), channel_id=1, source_target_pairs={{0,1},{1,2},{2,3},{4,5},{5,6},{6,7},{8,9},{9,10},{10,11},{12,13},{... | collective-permute-start | bytes 6152 | tf_op jit(solution)/shard_map/ppermute | solution.py:18
  40.7 1.3 %collective-permute-start.3 = (f32[16,32]{1,0:T(8,128)S(1)}, f32[16,32]{1,0:T(8,128)S(1)}, u32[]{:S(2)}, u32[]{:S(2)}) collective-permute-start(f32[16,32]{1,0:T(8,128)S(1)} %bitcast.225), channel_id=1, source_target_pairs={{1,0},{2,1},{3,2},{5,4},{6,5},{7,6},{9,8},{10,9},{11,10},{13,12},{... | collective-permute-start | bytes 6152 | tf_op jit(solution)/shard_map/ppermute | solution.py:20
  42.5 2.9 %collective-permute-done.3 = f32[16,32]{1,0:T(8,128)S(1)} collective-permute-done((f32[16,32]{1,0:T(8,128)S(1)}, f32[16,32]{1,0:T(8,128)S(1)}, u32[]{:S(2)}, u32[]{:S(2)}) %collective-permute-start.3) | collective-permute-done | bytes 2080 | tf_op jit(solution)/shard_map/ppermute | solution.py:20
  45.4 1.0 copy.199
  46.4 3.3 %gather_fusion.25 = f32[768,16]{1,0:T(8,128)} fusion(f32[16,832]{0,1:T(8,128)} %copy.199, s32[1024]{0:T(1024)S(1)} %copy-done.10), kind=kCustom, calls=%fused_computation.1.clone | custom fusion | bytes 101376 | tf_op jit(solution)/shard_map/jit(_take)/gather | solution.py:69
  49.6 1.9 %broadcast_select_fusion.1 = f32[768,16]{1,0:T(8,128)} fusion(f32[768,16]{1,0:T(8,128)} %gather_fusion.25, pred[768]{0:T(1024)(128)(4,1)S(1)} %copy-done.21), kind=kLoop, calls=%fused_computation.69 | loop fusion | flops 12288 | bytes 99072 | tf_op jit(solution)/shard_map/jit(_take)/select_n | solution.py:69
  51.6 1.2 copy.200
  54.8 1.3 %gather_fusion.12 = f32[16,6,128]{2,1,0:T(8,128)} fusion(f32[16,6,128]{2,1,0:T(8,128)S(1)} %copy.200, s32[1024]{0:T(1024)} %copy-done.27), kind=kCustom, calls=%fused_computation.15 | custom fusion | bytes 98368 | tf_op jit(solution)/shard_map/gather | solution.py:73
  56.1 1.3 %gather_fusion.11 = f32[16,6,128]{2,1,0:T(8,128)} fusion(f32[16,6,128]{2,1,0:T(8,128)S(1)} %copy.200, s32[1024]{0:T(1024)} %copy-done.26), kind=kCustom, calls=%fused_computation.14 | custom fusion | bytes 98368 | tf_op jit(solution)/shard_map/gather | solution.py:73
  57.4 1.3 %gather_fusion.10 = f32[16,6,128]{2,1,0:T(8,128)} fusion(f32[16,6,128]{2,1,0:T(8,128)S(1)} %copy.200, s32[1024]{0:T(1024)} %copy-done.25), kind=kCustom, calls=%fused_computation.13 | custom fusion | bytes 98368 | tf_op jit(solution)/shard_map/gather | solution.py:73
  58.7 1.3 %gather_fusion.9 = f32[16,6,128]{2,1,0:T(8,128)} fusion(f32[16,6,128]{2,1,0:T(8,128)S(1)} %copy.200, s32[1024]{0:T(1024)} %copy-done.24), kind=kCustom, calls=%fused_computation.12 | custom fusion | bytes 98368 | tf_op jit(solution)/shard_map/gather | solution.py:73
  60.1 1.3 %gather_fusion.8 = f32[16,6,128]{2,1,0:T(8,128)} fusion(f32[16,6,128]{2,1,0:T(8,128)S(1)} %copy.200, s32[1024]{0:T(1024)} %get-tuple-element.43), kind=kCustom, calls=%fused_computation.11 | custom fusion | bytes 98368 | tf_op jit(solution)/shard_map/gather | solution.py:73
  61.4 1.0 select_add_fusion.1
  63.2 4.3 %collective-permute-start.4 = (f32[16,32]{1,0:T(8,128)S(1)}, f32[16,32]{1,0:T(8,128)S(1)}, u32[]{:S(2)}, u32[]{:S(2)}) collective-permute-start(f32[16,32]{1,0:T(8,128)S(1)} %slice.189), channel_id=1, source_target_pairs={{0,1},{1,2},{2,3},{4,5},{5,6},{6,7},{8,9},{9,10},{10,11},{12,13},{... | collective-permute-start | bytes 6152 | tf_op jit(solution)/shard_map/ppermute | solution.py:18
  67.5 1.3 %collective-permute-start.5 = (f32[16,32]{1,0:T(8,128)S(1)}, f32[16,32]{1,0:T(8,128)S(1)}, u32[]{:S(2)}, u32[]{:S(2)}) collective-permute-start(f32[16,32]{1,0:T(8,128)S(1)} %bitcast.227), channel_id=1, source_target_pairs={{1,0},{2,1},{3,2},{5,4},{6,5},{7,6},{9,8},{10,9},{11,10},{13,12},{... | collective-permute-start | bytes 6152 | tf_op jit(solution)/shard_map/ppermute | solution.py:20
  69.2 1.3 %collective-permute-done.5 = f32[16,32]{1,0:T(8,128)S(1)} collective-permute-done((f32[16,32]{1,0:T(8,128)S(1)}, f32[16,32]{1,0:T(8,128)S(1)}, u32[]{:S(2)}, u32[]{:S(2)}) %collective-permute-start.5) | collective-permute-done | bytes 2080 | tf_op jit(solution)/shard_map/ppermute | solution.py:20
  70.8 1.6 %gather_fusion.26 = f32[768,16]{1,0:T(8,128)S(1)} fusion(f32[16,832]{0,1:T(8,128)S(1)} %copy.216, s32[1024]{0:T(1024)S(1)} %copy-done.11), kind=kCustom, calls=%fused_computation.2.clone | custom fusion | bytes 101376 | tf_op jit(solution)/shard_map/jit(_take)/gather | solution.py:69
  76.3 0.8 gather_fusion.18
  79.2 1.0 scatter_custom_fusion.3
  80.4 0.7 reshape.483
  81.1 6.0 %all-to-all-start.2 = ((f32[8,1,756]{2,1,0:T(1,128)}), f32[8,1,756]{2,1,0:T(1,128)S(1)}, u32[]{:S(2)}, u32[]{:S(2)}) async-start(f32[8,1,756]{2,1,0:T(1,128)} %reshape.483), calls=%async_computation.2 | async-start | bytes 49152 | tf_op jit(solution)/shard_map/all_to_all | solution.py:172
  87.1 1.1 convolution_bitcast_fusion
  88.5 1.3 %scatter_custom_fusion.1 = f32[729,224]{0,1:T(8,128)S(1)} fusion(s32[128]{0:T(128)} %copy-done.39, f32[729,128]{0,1:T(8,128)S(1)} %copy.211, f32[]{:T(128)} %constant.34.clone.1), kind=kCustom, calls=%fused_computation.65 | custom fusion | bytes 1026944 | tf_op jit(solution)/shard_map/scatter | solution.py:161
  89.8 1.0 reshape.170
  90.8 3.0 %all-to-all-done.2 = f32[8,1,756]{2,1,0:T(1,128)S(1)} async-done(((f32[8,1,756]{2,1,0:T(1,128)}), f32[8,1,756]{2,1,0:T(1,128)S(1)}, u32[]{:S(2)}, u32[]{:S(2)}) %all-to-all-start.2) | async-done | bytes 24224 | tf_op jit(solution)/shard_map/all_to_all | solution.py:172
  93.8 3.7 %all-to-all-start.1 = ((f32[729,8,28]{0,2,1:T(8,128)}), f32[729,8,28]{0,2,1:T(8,128)S(1)}, u32[]{:S(2)}, u32[]{:S(2)}) async-start(f32[729,8,28]{0,2,1:T(8,128)} %reshape.170), calls=%async_computation.1 | async-start | bytes 1572864 | tf_op jit(solution)/shard_map/all_to_all | solution.py:171
  98.0 1.3 %reduce.13 = s32[8,28]{1,0:T(8,128)S(1)} reduce(s32[1,8,28]{2,0,1:T(1,128)} %all-to-all-done, s32[]{:T(128)} %broadcast.220), dimensions={0}, to_apply=%all_to_all.9.reduce_sub_computation.3 | reduce | bytes 1796 | tf_op jit(solution)/shard_map/all_to_all | solution.py:173
  101.3 1.4 %scatter_custom_fusion.4 = f32[27,64]{0,1:T(8,128)S(1)} fusion(s32[256]{0:T(256)S(1)} %bitcast.235, f32[256,27]{1,0:T(8,128)S(1)} %copy.230, f32[]{:T(128)} %constant.34.clone.1), kind=kCustom, calls=%fused_computation.111 | custom fusion | flops 6912 | bytes 6916 | tf_op jit(solution)/shard_map/scatter-add | solution.py:185
  103.4 15.3 %all-to-all-done.1 = f32[729,8,28]{0,2,1:T(8,128)S(1)} async-done(((f32[729,8,28]{0,2,1:T(8,128)}), f32[729,8,28]{0,2,1:T(8,128)S(1)}, u32[]{:S(2)}, u32[]{:S(2)}) %all-to-all-start.1) | async-done | bytes 653216 | tf_op jit(solution)/shard_map/all_to_all | solution.py:171
  118.8 2.9 %scatter_custom_fusion.2 = f32[729,64]{0,1:T(8,128)} fusion(s32[256]{0:T(256)S(1)} %bitcast.236, f32[729,32]{0,1:T(8,128)S(1)} %slice-done, f32[]{:T(128)} %constant.118, f32[729,224]{0,1:T(8,128)S(1)} %reshape.171, f32[]{:T(128)} %constant.34.clone.1), kind=kCustom, calls=%fused_computation.62 | custom fusion | flops 373248 | bytes 973064 | tf_op jit(solution)/shard_map/scatter-add | solution.py:182
  (178 shorter events, 21.2 us)
Async XLA Ops:
  0.6 35.3 %copy-start = (f32[6,16,64]{2,1,0:T(8,128)S(1)}, f32[6,16,64]{2,1,0:T(8,128)}, u32[]{:S(2)}) copy-start(f32[6,16,64]{2,1,0:T(8,128)} %param.64) | copy-start | bytes 73732
  0.6 22.0 %copy-start.7 = (f32[27,64,1]{1,0,2:T(8,128)S(1)}, f32[27,64,1]{1,0,2:T(8,128)}, u32[]{:S(2)}) copy-start(f32[27,64,1]{1,0,2:T(8,128)} %constant.115) | copy-start | bytes 20740
  0.7 22.0 %copy-start.1 = (bf16[64,64,128]{2,1,0:T(8,128)(2,1)S(1)}, bf16[64,64,128]{2,1,0:T(8,128)(2,1)}, u32[]{:S(2)}) copy-start(bf16[64,64,128]{2,1,0:T(8,128)(2,1)} %param.62) | copy-start | bytes 3145732
  1.6 23.1 %collective-permute-start = (f32[16,32]{1,0:T(8,128)S(1)}, f32[16,32]{1,0:T(8,128)S(1)}, u32[]{:S(2)}, u32[]{:S(2)}) collective-permute-start(f32[16,32]{1,0:T(8,128)S(1)} %slice.172), channel_id=1, source_target_pairs={{0,1},{1,2},{2,3},{4,5},{5,6},{6,7},{8,9},{9,10},{10,11},{12,13},{... | collective-permute-start | bytes 6152 | tf_op jit(solution)/shard_map/ppermute | solution.py:18
  3.9 20.7 %collective-permute-start.1 = (f32[16,32]{1,0:T(8,128)S(1)}, f32[16,32]{1,0:T(8,128)S(1)}, u32[]{:S(2)}, u32[]{:S(2)}) collective-permute-start(f32[16,32]{1,0:T(8,128)S(1)} %bitcast.223), channel_id=1, source_target_pairs={{1,0},{2,1},{3,2},{5,4},{6,5},{7,6},{9,8},{10,9},{11,10},{13,12},{... | collective-permute-start | bytes 6152 | tf_op jit(solution)/shard_map/ppermute | solution.py:20
  7.7 9.8 %copy-start.39 = (s32[128]{0:T(128)}, s32[128]{0:T(128)S(1)}, u32[]{:S(2)}) copy-start(s32[128]{0:T(128)S(1)} %compare_select_fusion.3) | copy-start | bytes 1540
  9.4 71.7 %all-to-all-start = ((s32[1,8,28]{2,0,1:T(1,128)}), s32[1,8,28]{2,0,1:T(1,128)}, u32[]{:S(2)}, u32[]{:S(2)}) async-start(s32[1,8,28]{2,0,1:T(1,128)} %reshape.168), calls=%async_computation | async-start | bytes 8192 | tf_op jit(solution)/shard_map/all_to_all | solution.py:173
  16.8 9.7 %copy-start.20 = (pred[768]{0:T(1024)(128)(4,1)}, pred[768]{0:T(1024)(128)(4,1)S(1)}, u32[]{:S(2)}) copy-start(pred[768]{0:T(1024)(128)(4,1)S(1)} %compare_and_fusion) | copy-start | bytes 2308
  22.7 1.8 %copy-start.35 = (s32[16]{0:T(128)S(1)}, s32[16]{0:T(128)}, u32[]{:S(2)}) copy-start(s32[16]{0:T(128)} %constant.91) | copy-start | bytes 196
  22.7 1.8 %copy-start.36 = (s32[16]{0:T(128)S(1)}, s32[16]{0:T(128)}, u32[]{:S(2)}) copy-start(s32[16]{0:T(128)} %constant.90) | copy-start | bytes 196
  22.7 1.8 %copy-start.33 = (s32[16]{0:T(128)S(1)}, s32[16]{0:T(128)}, u32[]{:S(2)}) copy-start(s32[16]{0:T(128)} %constant.93) | copy-start | bytes 196
  22.7 1.8 %copy-start.31 = (s32[16]{0:T(128)S(1)}, s32[16]{0:T(128)}, u32[]{:S(2)}) copy-start(s32[16]{0:T(128)} %constant.95) | copy-start | bytes 196
  22.7 1.8 %copy-start.32 = (s32[16]{0:T(128)S(1)}, s32[16]{0:T(128)}, u32[]{:S(2)}) copy-start(s32[16]{0:T(128)} %constant.94) | copy-start | bytes 196
  24.4 7.8 %copy-start.24 = (s32[1024]{0:T(1024)}, s32[1024]{0:T(1024)S(1)}, u32[]{:S(2)}) copy-start(s32[1024]{0:T(1024)S(1)} %get-tuple-element.42) | copy-start | bytes 12292
  24.5 5.3 %copy-start.26 = (s32[1024]{0:T(1024)}, s32[1024]{0:T(1024)S(1)}, u32[]{:S(2)}) copy-start(s32[1024]{0:T(1024)S(1)} %get-tuple-element.40) | copy-start | bytes 12292
  24.5 6.5 %copy-start.25 = (s32[1024]{0:T(1024)}, s32[1024]{0:T(1024)S(1)}, u32[]{:S(2)}) copy-start(s32[1024]{0:T(1024)S(1)} %get-tuple-element.41) | copy-start | bytes 12292
  24.5 3.5 %copy-start.28 = (s32[1024]{0:T(1024)}, s32[1024]{0:T(1024)S(1)}, u32[]{:S(2)}) copy-start(s32[1024]{0:T(1024)S(1)} %get-tuple-element.38) | copy-start | bytes 12292
  24.5 4.1 %copy-start.27 = (s32[1024]{0:T(1024)}, s32[1024]{0:T(1024)S(1)}, u32[]{:S(2)}) copy-start(s32[1024]{0:T(1024)S(1)} %get-tuple-element.39) | copy-start | bytes 12292
  24.6 2.3 %copy-start.30 = (s32[1024]{0:T(1024)}, s32[1024]{0:T(1024)S(1)}, u32[]{:S(2)}) copy-start(s32[1024]{0:T(1024)S(1)} %get-tuple-element.36) | copy-start | bytes 12292
  24.6 2.9 %copy-start.29 = (s32[1024]{0:T(1024)}, s32[1024]{0:T(1024)S(1)}, u32[]{:S(2)}) copy-start(s32[1024]{0:T(1024)S(1)} %get-tuple-element.37) | copy-start | bytes 12292
  24.6 2.1 %copy-start.9 = (s32[1024]{0:T(1024)}, s32[1024]{0:T(1024)S(1)}, u32[]{:S(2)}) copy-start(s32[1024]{0:T(1024)S(1)} %pad_clamp_fusion.8) | copy-start | bytes 12292
  26.7 9.2 %copy-start.6 = (f32[64,128]{1,0:T(8,128)S(1)}, f32[64,128]{1,0:T(8,128)}, u32[]{:S(2)}) copy-start(f32[64,128]{1,0:T(8,128)} %param.61) | copy-start | bytes 98308
  26.9 9.3 %copy-start.2 = (bf16[64,64,128]{2,1,0:T(8,128)(2,1)S(1)}, bf16[64,64,128]{2,1,0:T(8,128)(2,1)}, u32[]{:S(2)}) copy-start(bf16[64,64,128]{2,1,0:T(8,128)(2,1)} %param.63) | copy-start | bytes 3145732
  33.4 3.1 %copy-start.4 = (f32[64,128]{1,0:T(8,128)S(1)}, f32[64,128]{1,0:T(8,128)}, u32[]{:S(2)}) copy-start(f32[64,128]{1,0:T(8,128)} %param.60) | copy-start | bytes 98308
  36.5 9.8 %copy-start.10 = (s32[1024]{0:T(1024)S(1)}, s32[1024]{0:T(1024)}, u32[]{:S(2)}) copy-start(s32[1024]{0:T(1024)} %copy-done.9) | copy-start | bytes 12292
  36.7 5.8 %collective-permute-start.2 = (f32[16,32]{1,0:T(8,128)S(1)}, f32[16,32]{1,0:T(8,128)S(1)}, u32[]{:S(2)}, u32[]{:S(2)}) collective-permute-start(f32[16,32]{1,0:T(8,128)S(1)} %slice.180), channel_id=1, source_target_pairs={{0,1},{1,2},{2,3},{4,5},{5,6},{6,7},{8,9},{9,10},{10,11},{12,13},{... | collective-permute-start | bytes 6152 | tf_op jit(solution)/shard_map/ppermute | solution.py:18
  40.7 4.6 %collective-permute-start.3 = (f32[16,32]{1,0:T(8,128)S(1)}, f32[16,32]{1,0:T(8,128)S(1)}, u32[]{:S(2)}, u32[]{:S(2)}) collective-permute-start(f32[16,32]{1,0:T(8,128)S(1)} %bitcast.225), channel_id=1, source_target_pairs={{1,0},{2,1},{3,2},{5,4},{6,5},{7,6},{9,8},{10,9},{11,10},{13,12},{... | collective-permute-start | bytes 6152 | tf_op jit(solution)/shard_map/ppermute | solution.py:20
  42.1 7.5 %copy-start.21 = (pred[768]{0:T(1024)(128)(4,1)S(1)}, pred[768]{0:T(1024)(128)(4,1)}, u32[]{:S(2)}) copy-start(pred[768]{0:T(1024)(128)(4,1)} %copy-done.20) | copy-start | bytes 2308
  63.0 7.8 %copy-start.11 = (s32[1024]{0:T(1024)S(1)}, s32[1024]{0:T(1024)}, u32[]{:S(2)}) copy-start(s32[1024]{0:T(1024)} %copy-done.9) | copy-start | bytes 12292
  63.0 9.4 %copy-start.5 = (f32[64,128]{1,0:T(8,128)}, f32[64,128]{1,0:T(8,128)S(1)}, u32[]{:S(2)}) copy-start(f32[64,128]{1,0:T(8,128)S(1)} %bitcast_add_fusion) | copy-start | bytes 98308
  63.2 6.0 %collective-permute-start.4 = (f32[16,32]{1,0:T(8,128)S(1)}, f32[16,32]{1,0:T(8,128)S(1)}, u32[]{:S(2)}, u32[]{:S(2)}) collective-permute-start(f32[16,32]{1,0:T(8,128)S(1)} %slice.189), channel_id=1, source_target_pairs={{0,1},{1,2},{2,3},{4,5},{5,6},{6,7},{8,9},{9,10},{10,11},{12,13},{... | collective-permute-start | bytes 6152 | tf_op jit(solution)/shard_map/ppermute | solution.py:18
  67.5 3.1 %collective-permute-start.5 = (f32[16,32]{1,0:T(8,128)S(1)}, f32[16,32]{1,0:T(8,128)S(1)}, u32[]{:S(2)}, u32[]{:S(2)}) collective-permute-start(f32[16,32]{1,0:T(8,128)S(1)} %bitcast.227), channel_id=1, source_target_pairs={{1,0},{2,1},{3,2},{5,4},{6,5},{7,6},{9,8},{10,9},{11,10},{13,12},{... | collective-permute-start | bytes 6152 | tf_op jit(solution)/shard_map/ppermute | solution.py:20
  68.8 3.6 %copy-start.22 = (pred[768]{0:T(1024)(128)(4,1)S(1)}, pred[768]{0:T(1024)(128)(4,1)}, u32[]{:S(2)}) copy-start(pred[768]{0:T(1024)(128)(4,1)} %copy-done.20) | copy-start | bytes 2308
  72.4 6.2 %copy-start.12 = (pred[6,128]{1,0:T(8,128)(4,1)S(1)}, pred[6,128]{1,0:T(8,128)(4,1)}, u32[]{:S(2)}) copy-start(pred[6,128]{1,0:T(8,128)(4,1)} %get-tuple-element.28) | copy-start | bytes 2308
  72.4 6.2 %copy-start.13 = (pred[6,128]{1,0:T(8,128)(4,1)S(1)}, pred[6,128]{1,0:T(8,128)(4,1)}, u32[]{:S(2)}) copy-start(pred[6,128]{1,0:T(8,128)(4,1)} %get-tuple-element.29) | copy-start | bytes 2308
  72.4 6.2 %copy-start.14 = (pred[6,128]{1,0:T(8,128)(4,1)S(1)}, pred[6,128]{1,0:T(8,128)(4,1)}, u32[]{:S(2)}) copy-start(pred[6,128]{1,0:T(8,128)(4,1)} %get-tuple-element.30) | copy-start | bytes 2308
  72.4 6.2 %copy-start.15 = (pred[6,128]{1,0:T(8,128)(4,1)S(1)}, pred[6,128]{1,0:T(8,128)(4,1)}, u32[]{:S(2)}) copy-start(pred[6,128]{1,0:T(8,128)(4,1)} %get-tuple-element.31) | copy-start | bytes 2308
  72.5 6.2 %copy-start.16 = (pred[6,128]{1,0:T(8,128)(4,1)S(1)}, pred[6,128]{1,0:T(8,128)(4,1)}, u32[]{:S(2)}) copy-start(pred[6,128]{1,0:T(8,128)(4,1)} %get-tuple-element.32) | copy-start | bytes 2308
  72.5 6.2 %copy-start.17 = (pred[6,128]{1,0:T(8,128)(4,1)S(1)}, pred[6,128]{1,0:T(8,128)(4,1)}, u32[]{:S(2)}) copy-start(pred[6,128]{1,0:T(8,128)(4,1)} %get-tuple-element.33) | copy-start | bytes 2308
  72.5 6.2 %copy-start.18 = (pred[6,128]{1,0:T(8,128)(4,1)S(1)}, pred[6,128]{1,0:T(8,128)(4,1)}, u32[]{:S(2)}) copy-start(pred[6,128]{1,0:T(8,128)(4,1)} %get-tuple-element.34) | copy-start | bytes 2308
  72.5 6.2 %copy-start.19 = (pred[6,128]{1,0:T(8,128)(4,1)S(1)}, pred[6,128]{1,0:T(8,128)(4,1)}, u32[]{:S(2)}) copy-start(pred[6,128]{1,0:T(8,128)(4,1)} %get-tuple-element.35) | copy-start | bytes 2308
  72.7 6.3 %copy-start.23 = (f32[27,64]{1,0:T(8,128)S(1)}, f32[27,64]{1,0:T(8,128)}, u32[]{:S(2)}) copy-start(f32[27,64]{1,0:T(8,128)} %constant.23.clone) | copy-start | bytes 20740
  76.3 10.8 %copy-start.8 = (f32[27,64,1]{1,0,2:T(8,128)S(1)}, f32[27,64,1]{1,0,2:T(8,128)}, u32[]{:S(2)}) copy-start(f32[27,64,1]{1,0,2:T(8,128)} %constant.115) | copy-start | bytes 20740
  81.1 12.6 %all-to-all-start.2 = ((f32[8,1,756]{2,1,0:T(1,128)}), f32[8,1,756]{2,1,0:T(1,128)S(1)}, u32[]{:S(2)}, u32[]{:S(2)}) async-start(f32[8,1,756]{2,1,0:T(1,128)} %reshape.483), calls=%async_computation.2 | async-start | bytes 49152 | tf_op jit(solution)/shard_map/all_to_all | solution.py:172
  88.5 9.0 %copy-start.3 = (f32[729,128]{0,1:T(8,128)}, f32[729,128]{0,1:T(8,128)S(1)}, u32[]{:S(2)}) copy-start(f32[729,128]{0,1:T(8,128)S(1)} %copy.211) | copy-start | bytes 1119748
  90.8 6.7 %copy-start.38 = (s32[128]{0:T(128)S(1)}, s32[128]{0:T(128)}, u32[]{:S(2)}) copy-start(s32[128]{0:T(128)} %param.68) | copy-start | bytes 1540
  93.8 24.9 %all-to-all-start.1 = ((f32[729,8,28]{0,2,1:T(8,128)}), f32[729,8,28]{0,2,1:T(8,128)S(1)}, u32[]{:S(2)}, u32[]{:S(2)}) async-start(f32[729,8,28]{0,2,1:T(8,128)} %reshape.170), calls=%async_computation.1 | async-start | bytes 1572864 | tf_op jit(solution)/shard_map/all_to_all | solution.py:171
  100.9 17.9 %slice-start = ((f32[729,128]{0,1:T(8,128)}), f32[729,32]{0,1:T(8,128)S(1)}, s32[]{:S(2)}) async-start(f32[729,128]{0,1:T(8,128)} %copy-done.3), calls=%async_computation.3 | async-start | bytes 196608 | tf_op jit(solution)/shard_map/slice | solution.py:175
  (2 other events, 2.9 us)
where the time goes:
time: 123 us; the launch traced here: 122 us
  local copies, waits for them, and re-layouts  43.6 us (35%)
  starting transfers between devices  30.9 us (25%)
  waiting for transfers between devices  22.4 us (18%)
  other arithmetic  19.8 us (16%)
  matrix products  3.08 us (3%)
  between operations  1.85 us (2%)
    gather x24, local copies, waits for them, and re-layouts, couple(): picked[tables[turn]]  22.2 us
    all_to_all x1, waiting for transfers between devices, per_device(): lax.all_to_all(op_send, 'dom', split_axis=1, concat_axis=1, tiled=True)  15.3 us
    ppermute x3, starting transfers between devices, with_halo(): lax.ppermute(tail, axis, [(i, (i + 1) % count) for i in range(ends)])  10.7 us
    all_to_all x1, starting transfers between devices, per_device(): lax.all_to_all(slot_send, 'dom', split_axis=1, concat_axis=1, tiled=True)  6.63 us
    gather x3, local copies, waits for them, and re-layouts, couple(): jnp.take(pool, neighbour.reshape(-1), axis=1).reshape(16, 6, local_count)  6.42 us
    all_to_all x1, starting transfers between devices, per_device(): lax.all_to_all(rhs_send, 'dom', split_axis=1, concat_axis=1, tiled=True)  5.99 us
    ppermute x3, waiting for transfers between devices, with_halo(): lax.ppermute(head, axis, [((i + 1) % count, i) for i in range(ends)])  4.19 us
    ppermute x3, starting transfers between devices, with_halo(): lax.ppermute(head, axis, [((i + 1) % count, i) for i in range(ends)])  3.88 us
  transfers between devices with their start and end apart: 9, of which 4 were waited for; matrix products, arithmetic and copies ran while one was open for 51% of the time, Pallas kernels for 0%

commit v1 on v0

v1 whole, which is shorter than its diff:
```python
import jax
import jax.numpy as jnp
import numpy as np
from jax import lax
from jax.experimental import pallas as pl
from jax.experimental.pallas import tpu as pltpu
from jax.sharding import PartitionSpec as P

SWEEPS = 2
NODES = 64
COARSE = 27
FACES = 6
GROUP = 4
F32 = jnp.float32
BF16 = jnp.bfloat16
VMEM_LIMIT = 24 * 1024 * 1024

NN = (((1,), (0,)), ((), ()))
NT = (((1,), (1,)), ((), ()))
TN = (((0,), (0,)), ((), ()))


def restrict_line():
    fine = np.array([-1.0, -1.0 / np.sqrt(5.0), 1.0 / np.sqrt(5.0), 1.0])
    coarse = np.array([-1.0, 0.0, 1.0])
    basis = np.ones((4, 3))
    for column in range(3):
        for other in range(3):
            if other != column:
                basis[:, column] *= (fine - coarse[other]) / (coarse[column] - coarse[other])
    return basis.T


def restrict_table():
    line = restrict_line()
    return np.kron(np.kron(line, line), line)


def split_table(table):
    table = table.astype(np.float32)
    high = table.astype(BF16)
    low = (table - high.astype(np.float32)).astype(BF16)
    return high, low


def ceil_to(value, step):
    return -(-value // step) * step


def halves(values):
    high = values.astype(BF16)
    low = (values - high.astype(F32)).astype(BF16)
    return high, low


def dot(left, right, dims):
    return lax.dot_general(left, right, dims, preferred_element_type=F32)


def dot_split(left, right, dims):
    left_high, left_low = left
    right_high, right_low = right
    return (
        dot(left_high, right_high, dims)
        + dot(left_low, right_high, dims)
        + dot(left_high, right_low, dims)
    )


def lanes(shape):
    return lax.broadcasted_iota(jnp.int32, shape, 1)


def rows(shape):
    return lax.broadcasted_iota(jnp.int32, shape, 0)


def face_traces(ref):
    return [
        ref[0:16],
        ref[48:64],
        jnp.concatenate([ref[16 * i : 16 * i + 4] for i in range(4)], 0),
        jnp.concatenate([ref[16 * i + 12 : 16 * i + 16] for i in range(4)], 0),
        ref[pl.ds(0, 16, stride=4)],
        ref[pl.ds(3, 16, stride=4)],
    ]


def take(values, index, axis):
    return jnp.take_along_axis(values, index, axis=axis, mode="promise_in_bounds")


def turn(values, orient_row):
    shape = values.shape
    orient = jnp.broadcast_to(orient_row, shape)
    place = rows(shape)
    first = (place >> 2) ^ ((orient & 1) * 3)
    second = (place & 3) ^ (((orient >> 1) & 1) * 3)
    flip = (orient & 4) > 0
    source = jnp.where(flip, 4 * second + first, 4 * first + second)
    out = []
    for half in (source[:8], source[8:]):
        within = half & 7
        out.append(jnp.where(half >= 8, take(values[8:], within, 0), take(values[:8], within, 0)))
    return jnp.concatenate(out, 0)


def pick(traces, neighbour_ref, face):
    values = traces[face ^ 1]
    count = values.shape[1]
    index = jnp.clip(neighbour_ref[face : face + 1] - (face ^ 1) * count, 0, count - 1)
    return take(values, jnp.broadcast_to(index, values.shape), 1)


def apply_blocks(ref, values):
    out = []
    for group in range(NODES // 8):
        block = ref[8 * group : 8 * group + 8].astype(F32) * values[None]
        out.append(jnp.sum(block, axis=1))
    return jnp.concatenate(out, 0)


def pack_rim(traces):
    shape = traces[2].shape
    return jnp.where(lanes(shape) < shape[1] // 2, traces[2], traces[3])


def halo_of(pos_ref, gathered_ref):
    slabs, _, count = gathered_ref.shape
    pos = pos_ref[0]
    below = gathered_ref[jnp.maximum(pos - 1, 0)]
    above = gathered_ref[jnp.minimum(pos + 1, slabs - 1)]
    below = jnp.where(pos > 0, pltpu.roll(below, count // 4, 1), 0.0)
    above = jnp.where(pos < slabs - 1, pltpu.roll(above, count - count // 4, 1), 0.0)
    return below, above


def coupling(traces, below, above, neighbour_ref, orient_ref, lift_ref):
    count = below.shape[1]
    edge = count // 4
    turned = []
    for face in range(FACES):
        values = pick(traces, neighbour_ref, face)
        if face == 2:
            values = jnp.where(lanes(values.shape) < edge, below, values)
        if face == 3:
            values = jnp.where(lanes(values.shape) >= count - edge, above, values)
        turned.append(turn(values, orient_ref[face : face + 1]))
    turned = jnp.concatenate(turned, 0)
    lift = lift_ref[...].reshape(FACES * 16, NODES)
    return dot_split(halves(lift), halves(turned), TN)


def rim_kernel(start_ref, rim_ref):
    rim_ref[...] = pack_rim(face_traces(start_ref))


def residual(pos_ref, gathered_ref, sol_ref, rhs_ref, diag_ref, lift_ref, neighbour_ref, orient_ref):
    traces = face_traces(sol_ref)
    below, above = halo_of(pos_ref, gathered_ref)
    coupled = coupling(traces, below, above, neighbour_ref, orient_ref, lift_ref)
    return rhs_ref[...] - (apply_blocks(diag_ref, sol_ref[...]) - coupled)


def sweep_kernel(
    pos_ref, gathered_ref, sol_ref, rhs_ref, diag_ref, precond_ref, lift_ref, neighbour_ref, orient_ref,
    out_ref, rim_ref,
):
    resid = residual(pos_ref, gathered_ref, sol_ref, rhs_ref, diag_ref, lift_ref, neighbour_ref, orient_ref)
    out_ref[...] = sol_ref[...] + apply_blocks(precond_ref, resid)
    rim_ref[...] = pack_rim(face_traces(out_ref))


def targets(owner_row, staying, owner_count, capacity):
    count = owner_row.shape[1]
    shape = (owner_count, count)
    hits = (rows(shape) == owner_row) & (lanes(shape) >= staying)
    hits = jnp.where(hits, 1.0, 0.0)
    before = jnp.where(rows((count, count)) < lanes((count, count)), 1.0, 0.0)
    earlier = dot(hits.astype(BF16), before.astype(BF16), NN)
    rank = jnp.sum(hits * earlier, axis=0, keepdims=True).astype(jnp.int32)
    return jnp.where(lanes(owner_row.shape) >= staying, owner_row * capacity + rank, -1)


def one_hot(condition):
    return jnp.where(condition, 1.0, 0.0).astype(BF16)


def contract(four, line):
    first, second = float(line[0, 1]), float(line[0, 2])
    middle = float(line[1, 1])
    return [
        four[0] + first * four[1] + second * four[2],
        middle * (four[1] + four[2]),
        four[3] + second * four[1] + first * four[2],
    ]


def galerkin_kernel(
    staying, owner_count, capacity,
    diag_ref, owner_ref, slot_ref, table_ref,
    send_ref, local_ref, target_ref, high_ref, low_ref, full_ref,
):
    line = restrict_line()
    count = diag_ref.shape[2]
    chunk = 16

    def step(part, carry):
        at = pl.ds(pl.multiple_of(part * chunk, chunk), chunk)
        planes = []
        for i in range(4):
            bars = []
            for j in range(4):
                four = [diag_ref[16 * i + 4 * j + k, at].astype(F32) for k in range(4)]
                bars.append(contract(four, line))
            sheet = [contract([bars[j][k] for j in range(4)], line) for k in range(3)]
            planes.append([sheet[k][j] for j in range(3) for k in range(3)])
        for rest in range(9):
            made = contract([planes[i][rest] for i in range(4)], line)
            for i in range(3):
                high, low = halves(made[i])
                high_ref[9 * i + rest, at] = high
                low_ref[9 * i + rest, at] = low
        return carry

    lax.fori_loop(0, NODES // chunk, step, 0)
    high_ref[COARSE] = jnp.zeros((NODES, count), BF16)
    low_ref[COARSE] = jnp.zeros((NODES, count), BF16)
    full_ref[...] = jnp.zeros(full_ref.shape, F32)
    padded = table_ref.shape[0] // 2
    table = table_ref[...]
    for part in range(high_ref.shape[0] // GROUP):
        high = high_ref[GROUP * part : GROUP * part + GROUP].reshape(GROUP * NODES, count)
        low = low_ref[GROUP * part : GROUP * part + GROUP].reshape(GROUP * NODES, count)
        both = dot(table, high, NN)
        made = both[:padded] + both[padded:] + dot(table[:padded], low, NN)
        full_ref[GROUP * COARSE * part : GROUP * COARSE * part + padded] = made
    full_ref[COARSE * COARSE : COARSE * COARSE + 1] = (slot_ref[...] + 1).astype(F32)
    local = full_ref[...].astype(BF16)
    local_ref[...] = local
    target = targets(owner_ref[...], staying, owner_count, capacity)
    target_ref[...] = target
    shape = (owner_count * capacity, count)
    send_ref[...] = dot(one_hot(rows(shape) == target), local, NT).astype(BF16)


def slot_hits(got_ref, aggregates):
    ids = got_ref[:, COARSE * COARSE : COARSE * COARSE + 1].astype(F32)
    shape = (ids.shape[0], aggregates)
    return one_hot(ids == (lanes(shape) + 1).astype(F32))


def stay_hits(slot_ref, staying, aggregates):
    shape = (aggregates, slot_ref.shape[1])
    return one_hot((rows(shape) == slot_ref[...]) & (lanes(shape) < staying))


def gather_op_kernel(staying, got_ref, local_ref, slot_ref, out_ref):
    aggregates = out_ref.shape[1]
    total = dot(slot_hits(got_ref, aggregates), got_ref[...], TN)
    total = total + dot(stay_hits(slot_ref, staying, aggregates), local_ref[...], NT)
    out_ref[...] = total.T[: COARSE * COARSE]


def last_kernel(
    pos_ref, gathered_ref, sol_ref, rhs_ref, diag_ref, lift_ref, neighbour_ref, orient_ref, target_ref,
    low_ref, send_ref,
):
    resid = residual(pos_ref, gathered_ref, sol_ref, rhs_ref, diag_ref, lift_ref, neighbour_ref, orient_ref)
    low = resid.astype(BF16)
    low_ref[...] = low
    shape = (send_ref.shape[0], low.shape[1])
    send_ref[...] = dot(one_hot(rows(shape) == target_ref[...]), low, NT).astype(BF16)


def gather_rhs_kernel(staying, got_ref, ids_ref, low_ref, slot_ref, table_ref, out_ref):
    aggregates = out_ref.shape[1]
    total = dot(got_ref[...], slot_hits(ids_ref, aggregates), TN)
    total = total + dot(low_ref[...], stay_hits(slot_ref, staying, aggregates), NT)
    padded = table_ref.shape[0] // 2
    high, low = halves(total)
    both = dot(table_ref[...], high, NN)
    made = both[:padded] + both[padded:] + dot(table_ref[:padded], low, NN)
    out_ref[...] = made[:COARSE]


def call(kernel, outs, args, scratch=(), flops=0, scalars=0):
    bytes_in = sum(a.size * a.dtype.itemsize for a in args)
    bytes_out = sum(o.size * o.dtype.itemsize for o in outs)
    specs = [
        pl.BlockSpec(memory_space=pltpu.SMEM if i < scalars else pltpu.VMEM) for i in range(len(args))
    ]
    return pl.pallas_call(
        kernel,
        out_shape=tuple(outs),
        in_specs=specs,
        out_specs=tuple(pl.BlockSpec(memory_space=pltpu.VMEM) for _ in outs),
        scratch_shapes=list(scratch),
        compiler_params=pltpu.CompilerParams(vmem_limit_bytes=VMEM_LIMIT),
        cost_estimate=pl.CostEstimate(
            flops=flops, bytes_accessed=bytes_in + bytes_out, transcendentals=0
        ),
    )(*args)


def struct(shape, dtype):
    return jax.ShapeDtypeStruct(shape, dtype)


def block_table(table, copies, row_step):
    out = []
    for part in split_table(table):
        full = np.zeros((ceil_to(copies * table.shape[0], row_step), copies * table.shape[1]), BF16)
        for copy in range(copies):
            full[
                copy * table.shape[0] : (copy + 1) * table.shape[0],
                copy * table.shape[1] : (copy + 1) * table.shape[1],
            ] = part
        out.append(full)
    return np.concatenate(out, 0)


def per_device(start, rhs, diag_block, precond, lift, neighbour, orient, owner, slot):
    count = start.shape[1]
    staying = count // 4
    aggregates = count // 2
    owner_count = lax.axis_size("dom")
    movers = count - staying
    capacity = ceil_to(2 * ((movers + owner_count - 2) // (owner_count - 1)), 16)
    total = owner_count * capacity
    entries = ceil_to(COARSE * COARSE + 1, 128)
    groups = -(-COARSE // GROUP)
    pos = jnp.reshape(lax.axis_index("face"), (1,)).astype(jnp.int32)
    owner = owner.reshape(1, count)
    slot = slot.reshape(1, count)
    table = jnp.asarray(block_table(restrict_table(), GROUP, 16))
    small = jnp.asarray(block_table(restrict_table(), 1, 16))

    (rim,) = call(rim_kernel, [struct((16, count), F32)], [start])
    op_send, local_op, target = call(
        lambda *refs: galerkin_kernel(staying, owner_count, capacity, *refs),
        [
            struct((total, entries), BF16),
            struct((entries, count), BF16),
            struct((1, count), jnp.int32),
        ],
        [diag_block, owner, slot, table],
        scratch=[
            pltpu.VMEM((groups * GROUP, NODES, count), BF16),
            pltpu.VMEM((groups * GROUP, NODES, count), BF16),
            pltpu.VMEM((entries, count), F32),
        ],
        flops=200_000_000,
    )
    op_got = lax.all_to_all(op_send, "dom", split_axis=0, concat_axis=0, tiled=True)

    sol = start
    for _ in range(SWEEPS):
        gathered = lax.all_gather(rim, "face")
        sol, rim = call(
            sweep_kernel,
            [struct((NODES, count), F32), struct((16, count), F32)],
            [pos, gathered, sol, rhs, diag_block, precond, lift, neighbour, orient],
            flops=100_000_000,
            scalars=1,
        )
    gathered = lax.all_gather(rim, "face")
    low, rhs_send = call(
        last_kernel,
        [struct((NODES, count), BF16), struct((total, NODES), BF16)],
        [pos, gathered, sol, rhs, diag_block, lift, neighbour, orient, target],
        flops=100_000_000,
        scalars=1,
    )
    rhs_got = lax.all_to_all(rhs_send, "dom", split_axis=0, concat_axis=0, tiled=True)
    (coarse_op,) = call(
        lambda *refs: gather_op_kernel(staying, *refs),
        [struct((COARSE * COARSE, aggregates), F32)],
        [op_got, local_op, slot],
        flops=100_000_000,
    )
    (coarse_rhs,) = call(
        lambda *refs: gather_rhs_kernel(staying, *refs),
        [struct((COARSE, aggregates), F32)],
        [rhs_got, op_got, low, slot, small],
        flops=10_000_000,
    )
    return (sol, coarse_op, coarse_rhs)


def solution(mesh):
    return jax.shard_map(
        per_device,
        mesh=mesh,
        in_specs=(
            P(None, ("dom", "face")),
            P(None, ("dom", "face")),
            P(None, None, ("dom", "face")),
            P(None, None, ("dom", "face")),
            P(),
            P(None, ("dom", "face")),
            P(None, ("dom", "face")),
            P(("dom", "face")),
            P(("dom", "face")),
        ),
        out_specs=(P(None, ("dom", "face")), P(None, ("dom", "face")), P(None, ("dom", "face"))),
        check_vma=False,
    )
```

time: 123 us -> 56.1 us (0.46)
  local copies, waits for them, and re-layouts: 43.6 us -> 4.96 us
  blocking collectives: 0 us -> 29.3 us
  starting transfers between devices: 30.9 us -> 3.45 us
  other arithmetic: 19.8 us -> 0 us
  waiting for transfers between devices: 22.4 us -> 10.8 us
  Pallas kernels: 0 us -> 6.36 us
  matrix products: 3.08 us -> 0 us
    gather x27 -> x0, local copies, waits for them, and re-layouts: 28.6 us -> none  [the longest x24 22.2 us: couple(): picked[tables[turn]]]
    all_gather x0 -> x3, blocking collectives: none -> 16.8 us  [per_device(): gathered = lax.all_gather(rim, 'face')]
    ppermute x6 -> x0, starting transfers between devices: 14.6 us -> none  [the longest x3 10.7 us: with_halo(): lax.ppermute(tail, axis, [(i, (i + 1) % count) for i in range(ends)])]
    all_to_all x3 -> x1, starting transfers between devices: 16.4 us -> 3.45 us  [per_device(): lax.all_to_all(op_send, 'dom', split_axis=0, concat_axis=0, tiled=True)]
    all_to_all x0 -> x1, blocking collectives: none -> 12.5 us  [per_device(): lax.all_to_all(rhs_send, 'dom', split_axis=0, concat_axis=0, tiled=True)]
    all_to_all x3 -> x1, waiting for transfers between devices: 18.2 us -> 10.8 us  [per_device(): lax.all_to_all(op_send, 'dom', split_axis=0, concat_axis=0, tiled=True)]
    pallas_call x0 -> x7, Pallas kernels: none -> 6.36 us  [call(): pl.pallas_call(kernel, out_shape=tuple(outs), in_specs=specs, out_specs=t...]
    scatter-add x2 -> x0, other arithmetic: 4.35 us -> none  [the longest x1 2.91 us: per_device(): jnp.zeros((729, aggregates_here), jnp.float32).at[:, slot_ids]]
  transfers between devices with their start and end apart: 9 -> 1, of which waited for: 4 -> 1; matrix products, arithmetic and copies ran while one was open for 51% -> 0% of each run, Pallas kernels for 0% -> 0%
where the time goes in v1:
time: 56.1 us; the launch traced here: 55.6 us
  blocking collectives  29.3 us (52%)
  waiting for transfers between devices  10.8 us (19%)
  Pallas kernels  6.36 us (11%)
  local copies, waits for them, and re-layouts  4.96 us (9%)
  starting transfers between devices  3.45 us (6%)
  between operations  0.73 us (1%)
    all_gather x3, blocking collectives, per_device(): gathered = lax.all_gather(rim, 'face')  16.8 us
    all_to_all x1, blocking collectives, per_device(): lax.all_to_all(rhs_send, 'dom', split_axis=0, concat_axis=0, tiled=True)  12.5 us
    all_to_all x1, waiting for transfers between devices, per_device(): lax.all_to_all(op_send, 'dom', split_axis=0, concat_axis=0, tiled=True)  10.8 us
    pallas_call x7, Pallas kernels, call(): pl.pallas_call(kernel, out_shape=tuple(outs), in_specs=specs, out_specs=t...  6.36 us
    unnamed x31, local copies, waits for them, and re-layouts  4.96 us
    all_to_all x1, starting transfers between devices, per_device(): lax.all_to_all(op_send, 'dom', split_axis=0, concat_axis=0, tiled=True)  3.45 us
  transfers between devices with their start and end apart: 1, of which 1 were waited for; matrix products, arithmetic and copies ran while one was open for 0% of the time, Pallas kernels for 0%

profile of v1, /device:TPU:0, one launch (start us, length us, event | category | flops | bytes accessed | tf_op | source)
XLA Modules:
  0.0 55.6 jit_solution(7341396120408915352)
XLA Ops:
  0.6 0.0 copy-start.4
  0.6 0.0 copy-start.6
  0.7 0.8 %copy-done.6 = f32[64,128]{1,0:T(8,128)S(1)} copy-done((f32[64,128]{1,0:T(8,128)S(1)}, f32[64,128]{1,0:T(8,128)}, u32[]{:S(2)}) %copy-start.6) | copy-done | bytes 32792
  1.4 0.0 copy-start.5
  1.4 0.0 copy-start.8
  1.4 0.0 copy-start.9
  1.4 6.2 %all-gather = f32[64,128]{1,0:T(8,128)S(1)} all-gather(f32[16,128]{1,0:T(8,128)S(1)} %shard_map.130), channel_id=2, replica_groups=mesh['dom'=8,'face'=4] {'face'}, dimensions={0}, use_global_device_ids=true | all-gather | bytes 40960 | tf_op jit(solution)/shard_map/all_gather | solution.py:359
  7.7 0.0 copy-done.4
  7.7 0.0 copy-done.5
  7.7 0.0 copy-done.8
  7.7 0.0 copy-done.9
  7.7 0.0 copy-start
  7.7 1.2 %copy-done = bf16[64,64,128]{2,1,0:T(8,128)(2,1)S(1)} copy-done((bf16[64,64,128]{2,1,0:T(8,128)(2,1)S(1)}, bf16[64,64,128]{2,1,0:T(8,128)(2,1)}, u32[]{:S(2)}) %copy-start) | copy-done | bytes 1048600
  8.9 0.0 copy-start.2
  8.9 1.2 %copy-done.2 = bf16[64,64,128]{2,1,0:T(8,128)(2,1)S(1)} copy-done((bf16[64,64,128]{2,1,0:T(8,128)(2,1)S(1)}, bf16[64,64,128]{2,1,0:T(8,128)(2,1)}, u32[]{:S(2)}) %copy-start.2) | copy-done | bytes 1048600
  10.1 0.0 copy-start.1
  10.1 0.0 copy-start.3
  10.1 0.8 %shard_map.131 = (f32[64,128]{1,0:T(8,128)S(1)}, f32[16,128]{1,0:T(8,128)S(1)}) custom-call(s32[1]{0:T(128)} %bitcast.pos_ref, f32[4,16,128]{2,1,0:T(8,128)S(1)} %bitcast.14, f32[64,128]{1,0:T(8,128)S(1)} %copy-done.6, f32[64,128]{1,0:T(8,128)S(1)} %copy-done.5, bf16[64,64,128]{2,1,0:T(8,128)(2,1)S(1)} %copy-done, bf16[64,64,128]{2,1,0:T(8,128)(2,1)S(1)} %copy-done.2, ...), custom_call_target="tpu_custom_call" | custom-call | flops 100000000 | bytes 2267140 | tf_op jit(solution)/shard_map/pallas_call | solution.py:293
  10.9 5.4 %all-gather.1 = f32[64,128]{1,0:T(8,128)S(1)} all-gather(f32[16,128]{1,0:T(8,128)S(1)} %get-tuple-element.12), channel_id=3, replica_groups=mesh['dom'=8,'face'=4] {'face'}, dimensions={0}, use_global_device_ids=true | all-gather | bytes 40960 | tf_op jit(solution)/shard_map/all_gather | solution.py:359
  16.4 0.0 copy-done.1
  16.4 0.0 copy-done.3
  16.4 0.0 copy-start.7
  16.4 1.5 %shard_map.132 = (f32[64,128]{1,0:T(8,128)}, f32[16,128]{1,0:T(8,128)S(1)}) custom-call(s32[1]{0:T(128)} %bitcast.pos_ref, f32[4,16,128]{2,1,0:T(8,128)S(1)} %bitcast.13, f32[64,128]{1,0:T(8,128)S(1)} %get-tuple-element.13.sol_ref, f32[64,128]{1,0:T(8,128)S(1)} %copy-done.5, bf16[64,64,128]{2,1,0:T(8,128)(2,1)S(1)} %copy-done.1, ...), custom_call_target="tpu_custom_call" | custom-call | flops 100000000 | bytes 2267140 | tf_op jit(solution)/shard_map/pallas_call | solution.py:293
  17.8 5.2 %all-gather.2 = f32[64,128]{1,0:T(8,128)S(1)} all-gather(f32[16,128]{1,0:T(8,128)S(1)} %get-tuple-element.17), channel_id=4, replica_groups=mesh['dom'=8,'face'=4] {'face'}, dimensions={0}, use_global_device_ids=true | all-gather | bytes 40960 | tf_op jit(solution)/shard_map/all_gather | solution.py:367
  23.0 0.0 copy-start.12
  23.0 0.0 copy-start.13
  23.0 0.0 copy-done.7
  23.0 0.6 %copy-done.12 = s32[128]{0:T(128)S(1)} copy-done((s32[128]{0:T(128)S(1)}, s32[128]{0:T(128)}, u32[]{:S(2)}) %copy-start.12) | copy-done | bytes 536
  23.7 0.0 copy-done.13
  23.7 0.0 copy-start.10
  23.7 2.1 %shard_map.133 = (bf16[256,768]{1,0:T(8,128)(2,1)}, bf16[768,128]{1,0:T(8,128)(2,1)S(1)}, s32[1,128]{1,0:T(1,128)S(1)}) custom-call(bf16[64,64,128]{2,1,0:T(8,128)(2,1)S(1)} %copy-done.1, s32[1,128]{1,0:T(1,128)S(1)} %bitcast.20, s32[1,128]{1,0:T(1,128)S(1)} %bitcast.17, bf16[224,256]{1,0:T(8,128)(2,1)S(1)} %copy-done.7), custom_call_target="tpu_custom_call" | custom-call | flops 200000000 | bytes 1754624 | tf_op jit(solution)/shard_map/pallas_call | solution.py:293
  25.8 0.0 copy-done.10
  25.8 0.6 %shard_map.135 = (bf16[64,128]{1,0:T(8,128)(2,1)S(1)}, bf16[256,64]{1,0:T(8,128)(2,1)S(1)}) custom-call(s32[1]{0:T(128)} %bitcast.pos_ref, f32[4,16,128]{2,1,0:T(8,128)S(1)} %bitcast.15, f32[64,128]{1,0:T(8,128)S(1)} %copy-done.10, f32[64,128]{1,0:T(8,128)S(1)} %copy-done.5, bf16[64,64,128]{2,1,0:T(8,128)(2,1)S(1)} %copy-done.1, f32[6,16,64]{2,1,0:T(8,128)S(1)} %copy-done.4, ...), custom_call_target="tpu_custom_call" | custom-call | flops 100000000 | bytes 1227268 | tf_op jit(solution)/shard_map/pallas_call | solution.py:293
  26.4 0.1 reshape.25
  26.5 12.5 %all_to_all.22 = bf16[8,2,1024]{2,1,0:T(2,128)(2,1)S(1)} all-to-all(bf16[8,2,1024]{2,1,0:T(2,128)(2,1)S(1)} %reshape.25), channel_id=1, replica_groups=mesh['dom'=8,'face'=4] {'dom'}, dimensions={0} | all-to-all | bytes 65536 | tf_op jit(solution)/shard_map/all_to_all | solution.py:375
  39.0 3.5 %all-to-all-start = ((bf16[8,32,768]{2,1,0:T(8,128)(2,1)}), bf16[8,32,768]{2,1,0:T(8,128)(2,1)S(1)}, u32[]{:S(2)}, u32[]{:S(2)}) async-start(bf16[8,32,768]{2,1,0:T(8,128)(2,1)} %bitcast.5), calls=%async_computation | async-start | bytes 786432 | tf_op jit(solution)/shard_map/all_to_all | solution.py:355
  42.5 0.1 reshape.26
  42.6 10.8 %all-to-all-done = bf16[8,32,768]{2,1,0:T(8,128)(2,1)S(1)} async-done(((bf16[8,32,768]{2,1,0:T(8,128)(2,1)}), bf16[8,32,768]{2,1,0:T(8,128)(2,1)S(1)}, u32[]{:S(2)}, u32[]{:S(2)}) %all-to-all-start) | async-done | bytes 393248 | tf_op jit(solution)/shard_map/all_to_all | solution.py:355
  53.4 0.4 shard_map.134
  53.8 0.0 copy-start.11
  53.8 0.8 %copy.14 = f32[729,64]{0,1:T(8,128)} copy(f32[729,64]{1,0:T(8,128)S(1)} %shard_map.134) | data formatting | bytes 373248
  54.7 0.0 copy-done.11
  54.7 1.0 %shard_map.136 = f32[27,64]{1,0:T(8,128)} custom-call(bf16[256,64]{1,0:T(8,128)(2,1)S(1)} %bitcast.12, bf16[256,768]{1,0:T(8,128)(2,1)S(1)} %bitcast.11, bf16[64,128]{1,0:T(8,128)(2,1)S(1)} %get-tuple-element.20.refs_2_, s32[1,128]{1,0:T(1,128)S(1)} %bitcast.19, bf16[64,64]{1,0:T(8,128)(2,1)S(1)} %copy-done.11), custom_call_target="tpu_custom_call" | custom-call | flops 10000000 | bytes 457984 | tf_op jit(solution)/shard_map/pallas_call | solution.py:293
  (1 shorter events, 0.0 us)
Async XLA Ops:
  0.6 7.0 %copy-start.4 = (f32[6,16,64]{2,1,0:T(8,128)S(1)}, f32[6,16,64]{2,1,0:T(8,128)}, u32[]{:S(2)}) copy-start(f32[6,16,64]{2,1,0:T(8,128)} %lift_ref.5) | copy-start | bytes 73732
  0.6 0.8 %copy-start.6 = (f32[64,128]{1,0:T(8,128)S(1)}, f32[64,128]{1,0:T(8,128)}, u32[]{:S(2)}) copy-start(f32[64,128]{1,0:T(8,128)} %sol_ref.1) | copy-start | bytes 98308
  1.4 6.2 %copy-start.5 = (f32[64,128]{1,0:T(8,128)S(1)}, f32[64,128]{1,0:T(8,128)}, u32[]{:S(2)}) copy-start(f32[64,128]{1,0:T(8,128)} %rhs_ref.5) | copy-start | bytes 98308
  1.4 6.2 %copy-start.8 = (s32[6,128]{1,0:T(8,128)S(1)}, s32[6,128]{1,0:T(8,128)}, u32[]{:S(2)}) copy-start(s32[6,128]{1,0:T(8,128)} %neighbour_ref.5) | copy-start | bytes 9220
  1.4 6.2 %copy-start.9 = (s32[6,128]{1,0:T(8,128)S(1)}, s32[6,128]{1,0:T(8,128)}, u32[]{:S(2)}) copy-start(s32[6,128]{1,0:T(8,128)} %orient_ref.5) | copy-start | bytes 9220
  7.7 1.2 %copy-start = (bf16[64,64,128]{2,1,0:T(8,128)(2,1)S(1)}, bf16[64,64,128]{2,1,0:T(8,128)(2,1)}, u32[]{:S(2)}) copy-start(bf16[64,64,128]{2,1,0:T(8,128)(2,1)} %diag_ref.5) | copy-start | bytes 3145732
  8.9 1.2 %copy-start.2 = (bf16[64,64,128]{2,1,0:T(8,128)(2,1)S(1)}, bf16[64,64,128]{2,1,0:T(8,128)(2,1)}, u32[]{:S(2)}) copy-start(bf16[64,64,128]{2,1,0:T(8,128)(2,1)} %precond_ref.3) | copy-start | bytes 3145732
  10.1 6.2 %copy-start.1 = (bf16[64,64,128]{2,1,0:T(8,128)(2,1)S(1)}, bf16[64,64,128]{2,1,0:T(8,128)(2,1)}, u32[]{:S(2)}) copy-start(bf16[64,64,128]{2,1,0:T(8,128)(2,1)} %diag_ref.5) | copy-start | bytes 3145732
  10.1 6.2 %copy-start.3 = (bf16[64,64,128]{2,1,0:T(8,128)(2,1)S(1)}, bf16[64,64,128]{2,1,0:T(8,128)(2,1)}, u32[]{:S(2)}) copy-start(bf16[64,64,128]{2,1,0:T(8,128)(2,1)} %precond_ref.3) | copy-start | bytes 3145732
  16.4 6.6 %copy-start.7 = (bf16[224,256]{1,0:T(8,128)(2,1)S(1)}, bf16[224,256]{1,0:T(8,128)(2,1)}, u32[]{:S(2)}) copy-start(bf16[224,256]{1,0:T(8,128)(2,1)} %constant.8.clone.refs_3_) | copy-start | bytes 344068
  23.0 0.7 %copy-start.12 = (s32[128]{0:T(128)S(1)}, s32[128]{0:T(128)}, u32[]{:S(2)}) copy-start(s32[128]{0:T(128)} %param.19) | copy-start | bytes 1540
  23.0 0.7 %copy-start.13 = (s32[128]{0:T(128)S(1)}, s32[128]{0:T(128)}, u32[]{:S(2)}) copy-start(s32[128]{0:T(128)} %param.18) | copy-start | bytes 1540
  23.7 2.1 %copy-start.10 = (f32[64,128]{1,0:T(8,128)S(1)}, f32[64,128]{1,0:T(8,128)}, u32[]{:S(2)}) copy-start(f32[64,128]{1,0:T(8,128)} %get-tuple-element.21.sol_ref) | copy-start | bytes 98308
  39.0 14.4 %all-to-all-start = ((bf16[8,32,768]{2,1,0:T(8,128)(2,1)}), bf16[8,32,768]{2,1,0:T(8,128)(2,1)S(1)}, u32[]{:S(2)}, u32[]{:S(2)}) async-start(bf16[8,32,768]{2,1,0:T(8,128)(2,1)} %bitcast.5), calls=%async_computation | async-start | bytes 786432 | tf_op jit(solution)/shard_map/all_to_all | solution.py:355
  53.8 0.8 %copy-start.11 = (bf16[64,64]{1,0:T(8,128)(2,1)S(1)}, bf16[64,64]{1,0:T(8,128)(2,1)}, u32[]{:S(2)}) copy-start(bf16[64,64]{1,0:T(8,128)(2,1)} %constant.9.clone.refs_4_) | copy-start | bytes 24580

commit v2 on v1

--- a/solution.py
+++ b/solution.py
@@ -123,16 +123,6 @@
 def pack_rim(traces):
     shape = traces[2].shape
     return jnp.where(lanes(shape) < shape[1] // 2, traces[2], traces[3])
-
-
-def halo_of(pos_ref, gathered_ref):
-    slabs, _, count = gathered_ref.shape
-    pos = pos_ref[0]
-    below = gathered_ref[jnp.maximum(pos - 1, 0)]
-    above = gathered_ref[jnp.minimum(pos + 1, slabs - 1)]
-    below = jnp.where(pos > 0, pltpu.roll(below, count // 4, 1), 0.0)
-    above = jnp.where(pos < slabs - 1, pltpu.roll(above, count - count // 4, 1), 0.0)
-    return below, above
 
 
 def coupling(traces, below, above, neighbour_ref, orient_ref, lift_ref):
@@ -151,24 +141,115 @@
     return dot_split(halves(lift), halves(turned), TN)
 
 
-def rim_kernel(start_ref, rim_ref):
-    rim_ref[...] = pack_rim(face_traces(start_ref))
-
-
-def residual(pos_ref, gathered_ref, sol_ref, rhs_ref, diag_ref, lift_ref, neighbour_ref, orient_ref):
+def edge_mask(shape):
+    return (lanes(shape) < shape[1] // 4) | (lanes(shape) >= shape[1] - shape[1] // 4)
+
+
+def low_mask(shape):
+    return ((lanes(shape) // (shape[1] // 4)) & 1) == 0
+
+
+def both_halves(shape, low, high):
+    return jnp.where(lanes(shape) < shape[1] // 2, low, high)
+
+
+def response(precond_ref, lift_ref):
+    count = precond_ref.shape[2]
+    parts = []
+    for face in (2, 3):
+        parts.extend(halves(lift_ref[face]))
+    stack = jnp.concatenate(parts, 0)
+    shape = (NODES, count)
+    out = []
+    for spot in range(16):
+        node = 16 * (spot // 4) + spot % 4
+        block = both_halves(shape, precond_ref[node].astype(F32), precond_ref[node + 12].astype(F32))
+        made = dot(stack, block.astype(BF16), NN)
+        out.append(
+            both_halves((16, count), made[0:16] + made[16:32], made[32:48] + made[48:64])
+        )
+    return out
+
+
+def halo_lift(below, above, orient_ref, lift_ref):
+    shape = below.shape
+    edge = shape[1] // 4
+    low = jnp.where(lanes(shape) < edge, turn(below, orient_ref[2:3]), 0.0)
+    high = jnp.where(lanes(shape) >= shape[1] - edge, turn(above, orient_ref[3:4]), 0.0)
+    lift = lift_ref[2:4].reshape(32, NODES)
+    return dot_split(halves(lift), halves(jnp.concatenate([low, high], 0)), TN)
+
+
+def first_kernel(
+    start_ref, rhs_ref, diag_ref, precond_ref, lift_ref, neighbour_ref, orient_ref,
+    partial_ref, message_ref,
+):
+    traces = face_traces(start_ref)
+    shape = traces[2].shape
+    count = shape[1]
+    none = jnp.zeros(shape, F32)
+    coupled = coupling(traces, none, none, neighbour_ref, orient_ref, lift_ref)
+    resid = rhs_ref[...] - (apply_blocks(diag_ref, start_ref[...]) - coupled)
+    partial_ref[...] = start_ref[...] + apply_blocks(precond_ref, resid)
+    direct = edge_mask(shape)
+    later = pack_rim(face_traces(partial_ref))
+    message_ref[0:16] = jnp.where(direct, pack_rim(traces), pltpu.roll(later, count // 2, 1))
+    reply = response(precond_ref, lift_ref)
+    for spot in range(8):
+        message_ref[16 + 16 * spot : 32 + 16 * spot] = jnp.where(
+            direct, reply[spot], pltpu.roll(reply[spot + 8], count // 2, 1)
+        )
+    orient = both_halves((1, count), orient_ref[2:3], orient_ref[3:4])
+    message_ref[144:152] = jnp.broadcast_to(orient.astype(F32), (8, count))
+
+
+def merged(pos_ref, gathered_ref, at):
+    slabs = gathered_ref.shape[0]
+    pos = pos_ref[0]
+    above = gathered_ref[jnp.minimum(pos + 1, slabs - 1), at]
+    below = gathered_ref[jnp.maximum(pos - 1, 0), at]
+    above = jnp.where(pos < slabs - 1, above, 0.0)
+    below = jnp.where(pos > 0, below, 0.0)
+    return jnp.where(low_mask(above.shape), above, below)
+
+
+def aside(values):
+    count = values.shape[1]
+    return pltpu.roll(values, count // 4, 1), pltpu.roll(values, count - count // 4, 1)
+
+
+def middle_kernel(
+    pos_ref, gathered_ref, start_ref, partial_ref, rhs_ref, diag_ref, precond_ref, lift_ref,
+    neighbour_ref, orient_ref,
+    out_ref, rest_ref, rim_ref, sol_ref,
+):
+    own = face_traces(start_ref)
+    shape = own[2].shape
+    count = shape[1]
+    head = merged(pos_ref, gathered_ref, pl.ds(0, 16))
+    orient = merged(pos_ref, gathered_ref, pl.ds(144, 8))[0:1].astype(jnp.int32)
+    sent = both_halves(shape, aside(own[3])[0], aside(own[2])[1])
+    sent = turn(sent, orient)
+    below, above = aside(head)
+    delta = halo_lift(below, above, orient_ref, lift_ref)
+    sol_ref[...] = partial_ref[...] + apply_blocks(precond_ref, delta)
+    later = pltpu.roll(head, count // 2, 1)
+    reply = []
+    for spot in range(8):
+        block = merged(pos_ref, gathered_ref, pl.ds(16 + 16 * spot, 16))
+        reply.append((block, pltpu.roll(block, count // 2, 1)))
+    reply = [pair[0] for pair in reply] + [pair[1] for pair in reply]
+    change = [jnp.sum(block * sent, axis=0, keepdims=True) for block in reply]
+    below, above = aside(later + jnp.concatenate(change, 0))
     traces = face_traces(sol_ref)
-    below, above = halo_of(pos_ref, gathered_ref)
     coupled = coupling(traces, below, above, neighbour_ref, orient_ref, lift_ref)
-    return rhs_ref[...] - (apply_blocks(diag_ref, sol_ref[...]) - coupled)
-
-
-def sweep_kernel(
-    pos_ref, gathered_ref, sol_ref, rhs_ref, diag_ref, precond_ref, lift_ref, neighbour_ref, orient_ref,
-    out_ref, rim_ref,
-):
-    resid = residual(pos_ref, gathered_ref, sol_ref, rhs_ref, diag_ref, lift_ref, neighbour_ref, orient_ref)
+    resid = rhs_ref[...] - (apply_blocks(diag_ref, sol_ref[...]) - coupled)
     out_ref[...] = sol_ref[...] + apply_blocks(precond_ref, resid)
-    rim_ref[...] = pack_rim(face_traces(out_ref))
+    traces = face_traces(out_ref)
+    none = jnp.zeros(shape, F32)
+    coupled = coupling(traces, none, none, neighbour_ref, orient_ref, lift_ref)
+    rest_ref[...] = rhs_ref[...] - (apply_blocks(diag_ref, out_ref[...]) - coupled)
+    rim_ref[...] = pack_rim(traces)
 
 
 def targets(owner_row, staying, owner_count, capacity):
@@ -263,10 +344,11 @@
 
 
 def last_kernel(
-    pos_ref, gathered_ref, sol_ref, rhs_ref, diag_ref, lift_ref, neighbour_ref, orient_ref, target_ref,
+    pos_ref, gathered_ref, rest_ref, lift_ref, orient_ref, target_ref, after_ref,
     low_ref, send_ref,
 ):
-    resid = residual(pos_ref, gathered_ref, sol_ref, rhs_ref, diag_ref, lift_ref, neighbour_ref, orient_ref)
+    below, above = aside(merged(pos_ref, gathered_ref, pl.ds(0, 16)))
+    resid = rest_ref[...] + halo_lift(below, above, orient_ref, lift_ref)
     low = resid.astype(BF16)
     low_ref[...] = low
     shape = (send_ref.shape[0], low.shape[1])
@@ -284,12 +366,11 @@
     out_ref[...] = made[:COARSE]
 
 
-def call(kernel, outs, args, scratch=(), flops=0, scalars=0):
+def call(kernel, outs, args, scratch=(), flops=0, scalars=0, anywhere=0):
     bytes_in = sum(a.size * a.dtype.itemsize for a in args)
     bytes_out = sum(o.size * o.dtype.itemsize for o in outs)
-    specs = [
-        pl.BlockSpec(memory_space=pltpu.SMEM if i < scalars else pltpu.VMEM) for i in range(len(args))
-    ]
+    spaces = [pltpu.SMEM] * scalars + [pltpu.VMEM] * (len(args) - scalars - anywhere) + [pl.ANY] * anywhere
+    specs = [pl.BlockSpec(memory_space=space) for space in spaces]
     return pl.pallas_call(
         kernel,
         out_shape=tuple(outs),
@@ -336,7 +417,6 @@
     table = jnp.asarray(block_table(restrict_table(), GROUP, 16))
     small = jnp.asarray(block_table(restrict_table(), 1, 16))
 
-    (rim,) = call(rim_kernel, [struct((16, count), F32)], [start])
     op_send, local_op, target = call(
         lambda *refs: galerkin_kernel(staying, owner_count, capacity, *refs),
         [
@@ -354,23 +434,29 @@
     )
     op_got = lax.all_to_all(op_send, "dom", split_axis=0, concat_axis=0, tiled=True)
 
-    sol = start
-    for _ in range(SWEEPS):
-        gathered = lax.all_gather(rim, "face")
-        sol, rim = call(
-            sweep_kernel,
-            [struct((NODES, count), F32), struct((16, count), F32)],
-            [pos, gathered, sol, rhs, diag_block, precond, lift, neighbour, orient],
-            flops=100_000_000,
-            scalars=1,
-        )
+    partial, message = call(
+        first_kernel,
+        [struct((NODES, count), F32), struct((152, count), F32)],
+        [start, rhs, diag_block, precond, lift, neighbour, orient],
+        flops=100_000_000,
+    )
+    gathered = lax.all_gather(message, "face")
+    sol, rest, rim = call(
+        middle_kernel,
+        [struct((NODES, count), F32), struct((NODES, count), F32), struct((16, count), F32)],
+        [pos, gathered, start, partial, rhs, diag_block, precond, lift, neighbour, orient],
+        scratch=[pltpu.VMEM((NODES, count), F32)],
+        flops=200_000_000,
+        scalars=1,
+    )
     gathered = lax.all_gather(rim, "face")
     low, rhs_send = call(
         last_kernel,
         [struct((NODES, count), BF16), struct((total, NODES), BF16)],
-        [pos, gathered, sol, rhs, diag_block, lift, neighbour, orient, target],
+        [pos, gathered, rest, lift, orient, target, op_got],
         flops=100_000_000,
         scalars=1,
+        anywhere=1,
     )
     rhs_got = lax.all_to_all(rhs_send, "dom", split_axis=0, concat_axis=0, tiled=True)
     (coarse_op,) = call(

time: 56.1 us -> 44 us (0.78)
  blocking collectives: 29.3 us -> 11.2 us
  starting transfers between devices: 3.45 us -> 13.4 us
  waiting for transfers between devices: 10.8 us -> 5.42 us
  local copies, waits for them, and re-layouts: 4.96 us -> 6.31 us
    all_to_all x1 -> x0, blocking collectives: 12.5 us -> none  [per_device(): lax.all_to_all(rhs_send, 'dom', split_axis=0, concat_axis=0, tiled=True)]
    all_gather x3 -> x1, blocking collectives: 16.8 us -> 5.18 us  [per_device(): gathered = lax.all_gather(rim, 'face')]
    all_to_all x1, waiting for transfers between devices: 10.8 us -> 0.01 us  [per_device(): lax.all_to_all(op_send, 'dom', split_axis=0, concat_axis=0, tiled=True)]
    all_gather x0 -> x1, blocking collectives: none -> 6.04 us  [per_device(): gathered = lax.all_gather(message, 'face')]
    all_to_all x0 -> x1, starting transfers between devices: none -> 6 us  [per_device(): lax.all_to_all(rhs_send, 'dom', split_axis=0, concat_axis=0, tiled=True)]
    all_to_all x0 -> x1, waiting for transfers between devices: none -> 5.42 us  [per_device(): lax.all_to_all(rhs_send, 'dom', split_axis=0, concat_axis=0, tiled=True)]
    all_to_all x1, starting transfers between devices: 3.45 us -> 7.4 us  [per_device(): lax.all_to_all(op_send, 'dom', split_axis=0, concat_axis=0, tiled=True)]
    unnamed x31 -> x27, local copies, waits for them, and re-layouts: 4.96 us -> 6.31 us
  transfers between devices with their start and end apart: 1 -> 2, of which waited for: 1 -> 1; matrix products, arithmetic and copies ran while one was open for 0% -> 2% of each run, Pallas kernels for 0% -> 7%
where the time goes in v2:
time: 44 us; the launch traced here: 43.5 us
  starting transfers between devices  13.4 us (30%)
  blocking collectives  11.2 us (25%)
  Pallas kernels  6.41 us (15%)
  local copies, waits for them, and re-layouts  6.31 us (14%)
  waiting for transfers between devices  5.42 us (12%)
  between operations  0.74 us (2%)
    all_to_all x1, starting transfers between devices, per_device(): lax.all_to_all(op_send, 'dom', split_axis=0, concat_axis=0, tiled=True)  7.4 us
    pallas_call x6, Pallas kernels, call(): pl.pallas_call(kernel, out_shape=tuple(outs), in_specs=specs, out_specs=t...  6.41 us
    unnamed x27, local copies, waits for them, and re-layouts  6.31 us
    all_gather x1, blocking collectives, per_device(): gathered = lax.all_gather(message, 'face')  6.04 us
    all_to_all x1, starting transfers between devices, per_device(): lax.all_to_all(rhs_send, 'dom', split_axis=0, concat_axis=0, tiled=True)  6 us
    all_to_all x1, waiting for transfers between devices, per_device(): lax.all_to_all(rhs_send, 'dom', split_axis=0, concat_axis=0, tiled=True)  5.42 us
    all_gather x1, blocking collectives, per_device(): gathered = lax.all_gather(rim, 'face')  5.18 us
  transfers between devices with their start and end apart: 2, of which 1 were waited for; matrix products, arithmetic and copies ran while one was open for 2% of the time, Pallas kernels for 7%

profile of v2, /device:TPU:0, one launch (start us, length us, event | category | flops | bytes accessed | tf_op | source)
XLA Modules:
  0.0 43.5 jit_solution(17109187321967514381)
XLA Ops:
  0.6 0.0 copy-start.10
  0.6 0.0 copy-start.11
  0.7 0.6 %copy-done.10 = s32[128]{0:T(128)S(1)} copy-done((s32[128]{0:T(128)S(1)}, s32[128]{0:T(128)}, u32[]{:S(2)}) %copy-start.10) | copy-done | bytes 536
  1.3 0.0 copy-done.11
  1.3 0.0 copy-start
  1.3 1.2 %copy-done = bf16[64,64,128]{2,1,0:T(8,128)(2,1)S(1)} copy-done((bf16[64,64,128]{2,1,0:T(8,128)(2,1)S(1)}, bf16[64,64,128]{2,1,0:T(8,128)(2,1)}, u32[]{:S(2)}) %copy-start) | copy-done | bytes 1048600
  2.5 0.0 copy-start.6
  2.5 0.9 %copy-done.6 = bf16[224,256]{1,0:T(8,128)(2,1)S(1)} copy-done((bf16[224,256]{1,0:T(8,128)(2,1)S(1)}, bf16[224,256]{1,0:T(8,128)(2,1)}, u32[]{:S(2)}) %copy-start.6) | copy-done | bytes 114712
  3.4 0.0 copy-start.1
  3.4 2.1 %shard_map.132 = (bf16[256,768]{1,0:T(8,128)(2,1)}, bf16[768,128]{1,0:T(8,128)(2,1)S(1)}, s32[1,128]{1,0:T(1,128)S(1)}) custom-call(bf16[64,64,128]{2,1,0:T(8,128)(2,1)S(1)} %copy-done, s32[1,128]{1,0:T(1,128)S(1)} %bitcast.19, s32[1,128]{1,0:T(1,128)S(1)} %bitcast.16, bf16[224,256]{1,0:T(8,128)(2,1)S(1)} %copy-done.6), custom_call_target="tpu_custom_call" | custom-call | flops 200000000 | bytes 1754624 | tf_op jit(solution)/shard_map/pallas_call | solution.py:374
  5.6 0.0 copy-start.3
  5.6 0.0 copy-start.4
  5.6 0.0 copy-start.5
  5.6 0.0 copy-start.8
  5.6 7.4 %all-to-all-start = ((bf16[8,32,768]{2,1,0:T(8,128)(2,1)}), bf16[8,32,768]{2,1,0:T(8,128)(2,1)S(1)}, u32[]{:S(2)}, u32[]{:S(2)}) async-start(bf16[8,32,768]{2,1,0:T(8,128)(2,1)} %bitcast.4), calls=%async_computation | async-start | bytes 786432 | tf_op jit(solution)/shard_map/all_to_all | solution.py:435
  13.0 0.0 copy-start.7
  13.0 0.0 copy-done.1
  13.0 0.0 copy-done.3
  13.0 0.0 copy-done.4
  13.0 0.0 copy-done.5
  13.0 0.0 copy-done.8
  13.0 0.6 %copy-done.7 = s32[6,128]{1,0:T(8,128)S(1)} copy-done((s32[6,128]{1,0:T(8,128)S(1)}, s32[6,128]{1,0:T(8,128)}, u32[]{:S(2)}) %copy-start.7) | copy-done | bytes 3096
  13.7 0.0 copy-start.2
  13.7 1.2 %copy-done.2 = bf16[64,64,128]{2,1,0:T(8,128)(2,1)S(1)} copy-done((bf16[64,64,128]{2,1,0:T(8,128)(2,1)S(1)}, bf16[64,64,128]{2,1,0:T(8,128)(2,1)}, u32[]{:S(2)}) %copy-start.2) | copy-done | bytes 1048600
  14.9 0.8 %shard_map.130 = (f32[64,128]{1,0:T(8,128)S(1)}, f32[152,128]{1,0:T(8,128)S(1)}) custom-call(f32[64,128]{1,0:T(8,128)S(1)} %copy-done.4, f32[64,128]{1,0:T(8,128)S(1)} %copy-done.5, bf16[64,64,128]{2,1,0:T(8,128)(2,1)S(1)} %copy-done.1, bf16[64,64,128]{2,1,0:T(8,128)(2,1)S(1)} %copy-done.2, f32[6,16,64]{2,1,0:T(8,128)S(1)} %copy-done.3, ...), custom_call_target="tpu_custom_call" | custom-call | flops 100000000 | bytes 2304000 | tf_op jit(solution)/shard_map/pallas_call | solution.py:374
  15.7 6.0 %all-gather = f32[608,128]{1,0:T(8,128)S(1)} all-gather(f32[152,128]{1,0:T(8,128)S(1)} %get-tuple-element.13), channel_id=2, replica_groups=mesh['dom'=8,'face'=4] {'face'}, dimensions={0}, use_global_device_ids=true | all-gather | bytes 389120 | tf_op jit(solution)/shard_map/all_gather | solution.py:443
  21.7 1.7 %shard_map.131 = (f32[64,128]{1,0:T(8,128)}, f32[64,128]{1,0:T(8,128)S(1)}, f32[16,128]{1,0:T(8,128)S(1)}) custom-call(s32[1]{0:T(128)} %bitcast.pos_ref, f32[4,152,128]{2,1,0:T(8,128)S(1)} %bitcast.12, f32[64,128]{1,0:T(8,128)S(1)} %copy-done.4, f32[64,128]{1,0:T(8,128)S(1)} %get-tuple-element.14.partial_ref, f32[64,128]{1,0:T(8,128)S(1)} %copy-done.5, ...), custom_call_target="tpu_custom_call" | custom-call | flops 200000000 | bytes 2611204 | tf_op jit(solution)/shard_map/pallas_call | solution.py:374
  23.4 5.2 %all-gather.1 = f32[64,128]{1,0:T(8,128)S(1)} all-gather(f32[16,128]{1,0:T(8,128)S(1)} %get-tuple-element.18), channel_id=3, replica_groups=mesh['dom'=8,'face'=4] {'face'}, dimensions={0}, use_global_device_ids=true | all-gather | bytes 40960 | tf_op jit(solution)/shard_map/all_gather | solution.py:452
  28.6 0.0 all-to-all-done
  28.6 0.4 shard_map.134
  29.0 0.7 %reshape.24 = bf16[8,2,1024]{2,1,0:T(2,128)(2,1)} reshape(bf16[8,32,64]{2,1,0:T(8,128)(2,1)S(1)} %bitcast.15) | data formatting | bytes 65536
  29.7 6.0 %all-to-all-start.1 = ((bf16[8,2,1024]{2,1,0:T(2,128)(2,1)}), bf16[8,2,1024]{2,1,0:T(2,128)(2,1)S(1)}, u32[]{:S(2)}, u32[]{:S(2)}) async-start(bf16[8,2,1024]{2,1,0:T(2,128)(2,1)} %reshape.24), calls=%async_computation.1 | async-start | bytes 65536 | tf_op jit(solution)/shard_map/all_to_all | solution.py:461
  35.7 0.4 shard_map.133
  36.2 0.8 %copy.14 = f32[729,64]{0,1:T(8,128)} copy(f32[729,64]{1,0:T(8,128)S(1)} %shard_map.133) | data formatting | bytes 373248
  37.0 0.0 copy-start.9
  37.0 5.4 %all-to-all-done.1 = bf16[8,2,1024]{2,1,0:T(2,128)(2,1)S(1)} async-done(((bf16[8,2,1024]{2,1,0:T(2,128)(2,1)}), bf16[8,2,1024]{2,1,0:T(2,128)(2,1)S(1)}, u32[]{:S(2)}, u32[]{:S(2)}) %all-to-all-start.1) | async-done | bytes 32800 | tf_op jit(solution)/shard_map/all_to_all | solution.py:461
  42.4 0.1 reshape.25
  42.5 0.0 copy-done.9
  42.5 1.0 %shard_map.135 = f32[27,64]{1,0:T(8,128)} custom-call(bf16[256,64]{1,0:T(8,128)(2,1)S(1)} %bitcast.13, bf16[256,768]{1,0:T(8,128)(2,1)S(1)} %bitcast.11, bf16[64,128]{1,0:T(8,128)(2,1)S(1)} %get-tuple-element.22.refs_2_, s32[1,128]{1,0:T(1,128)S(1)} %bitcast.18, bf16[64,64]{1,0:T(8,128)(2,1)S(1)} %copy-done.9), custom_call_target="tpu_custom_call" | custom-call | flops 10000000 | bytes 457984 | tf_op jit(solution)/shard_map/pallas_call | solution.py:374
Async XLA Ops:
  0.6 0.7 %copy-start.10 = (s32[128]{0:T(128)S(1)}, s32[128]{0:T(128)}, u32[]{:S(2)}) copy-start(s32[128]{0:T(128)} %param.19) | copy-start | bytes 1540
  0.6 0.7 %copy-start.11 = (s32[128]{0:T(128)S(1)}, s32[128]{0:T(128)}, u32[]{:S(2)}) copy-start(s32[128]{0:T(128)} %param.18) | copy-start | bytes 1540
  1.3 1.2 %copy-start = (bf16[64,64,128]{2,1,0:T(8,128)(2,1)S(1)}, bf16[64,64,128]{2,1,0:T(8,128)(2,1)}, u32[]{:S(2)}) copy-start(bf16[64,64,128]{2,1,0:T(8,128)(2,1)} %refs_0_.1) | copy-start | bytes 3145732
  2.5 0.9 %copy-start.6 = (bf16[224,256]{1,0:T(8,128)(2,1)S(1)}, bf16[224,256]{1,0:T(8,128)(2,1)}, u32[]{:S(2)}) copy-start(bf16[224,256]{1,0:T(8,128)(2,1)} %constant.8.clone.refs_3_) | copy-start | bytes 344068
  3.4 9.6 %copy-start.1 = (bf16[64,64,128]{2,1,0:T(8,128)(2,1)S(1)}, bf16[64,64,128]{2,1,0:T(8,128)(2,1)}, u32[]{:S(2)}) copy-start(bf16[64,64,128]{2,1,0:T(8,128)(2,1)} %refs_0_.1) | copy-start | bytes 3145732
  5.6 7.4 %copy-start.3 = (f32[6,16,64]{2,1,0:T(8,128)S(1)}, f32[6,16,64]{2,1,0:T(8,128)}, u32[]{:S(2)}) copy-start(f32[6,16,64]{2,1,0:T(8,128)} %lift_ref.5) | copy-start | bytes 73732
  5.6 7.4 %copy-start.4 = (f32[64,128]{1,0:T(8,128)S(1)}, f32[64,128]{1,0:T(8,128)}, u32[]{:S(2)}) copy-start(f32[64,128]{1,0:T(8,128)} %start_ref.3) | copy-start | bytes 98308
  5.6 7.4 %copy-start.5 = (f32[64,128]{1,0:T(8,128)S(1)}, f32[64,128]{1,0:T(8,128)}, u32[]{:S(2)}) copy-start(f32[64,128]{1,0:T(8,128)} %rhs_ref.3) | copy-start | bytes 98308
  5.6 7.5 %copy-start.8 = (s32[6,128]{1,0:T(8,128)S(1)}, s32[6,128]{1,0:T(8,128)}, u32[]{:S(2)}) copy-start(s32[6,128]{1,0:T(8,128)} %neighbour_ref.3) | copy-start | bytes 9220
  5.6 23.0 %all-to-all-start = ((bf16[8,32,768]{2,1,0:T(8,128)(2,1)}), bf16[8,32,768]{2,1,0:T(8,128)(2,1)S(1)}, u32[]{:S(2)}, u32[]{:S(2)}) async-start(bf16[8,32,768]{2,1,0:T(8,128)(2,1)} %bitcast.4), calls=%async_computation | async-start | bytes 786432 | tf_op jit(solution)/shard_map/all_to_all | solution.py:435
  13.0 0.7 %copy-start.7 = (s32[6,128]{1,0:T(8,128)S(1)}, s32[6,128]{1,0:T(8,128)}, u32[]{:S(2)}) copy-start(s32[6,128]{1,0:T(8,128)} %orient_ref.5) | copy-start | bytes 9220
  13.7 1.2 %copy-start.2 = (bf16[64,64,128]{2,1,0:T(8,128)(2,1)S(1)}, bf16[64,64,128]{2,1,0:T(8,128)(2,1)}, u32[]{:S(2)}) copy-start(bf16[64,64,128]{2,1,0:T(8,128)(2,1)} %precond_ref.3) | copy-start | bytes 3145732
  29.7 12.7 %all-to-all-start.1 = ((bf16[8,2,1024]{2,1,0:T(2,128)(2,1)}), bf16[8,2,1024]{2,1,0:T(2,128)(2,1)S(1)}, u32[]{:S(2)}, u32[]{:S(2)}) async-start(bf16[8,2,1024]{2,1,0:T(2,128)(2,1)} %reshape.24), calls=%async_computation.1 | async-start | bytes 65536 | tf_op jit(solution)/shard_map/all_to_all | solution.py:461
  37.0 5.5 %copy-start.9 = (bf16[64,64]{1,0:T(8,128)(2,1)S(1)}, bf16[64,64]{1,0:T(8,128)(2,1)}, u32[]{:S(2)}) copy-start(bf16[64,64]{1,0:T(8,128)(2,1)} %constant.9.clone.refs_4_) | copy-start | bytes 24580

commit v3 on v2

--- a/solution.py
+++ b/solution.py
@@ -14,6 +14,7 @@
 F32 = jnp.float32
 BF16 = jnp.bfloat16
 VMEM_LIMIT = 24 * 1024 * 1024
+FIRST_LIMIT = None
 
 NN = (((1,), (0,)), ((), ()))
 NT = (((1,), (1,)), ((), ()))
@@ -65,6 +66,26 @@
         + dot(left_low, right_high, dims)
         + dot(left_high, right_low, dims)
     )
+
+
+def small_table():
+    shape = (32, NODES)
+    line = restrict_line()
+    row, col = rows(shape), lanes(shape)
+    step = 9
+    table = jnp.ones(shape, F32)
+    left = row
+    for digit in range(3):
+        mine = (left >= step).astype(jnp.int32) + (left >= 2 * step).astype(jnp.int32)
+        left = left - step * mine
+        fine = (col >> (4 - 2 * digit)) & 3
+        value = jnp.zeros(shape, F32)
+        for i in range(3):
+            for j in range(4):
+                value = jnp.where((mine == i) & (fine == j), float(line[i, j]), value)
+        table = table * value
+        step //= 3
+    return jnp.where(row < COARSE, table, 0.0)
 
 
 def lanes(shape):
@@ -112,11 +133,28 @@
     return take(values, jnp.broadcast_to(index, values.shape), 1)
 
 
+def fold(parts):
+    place = rows(parts[0].shape)
+    step = 1
+    while len(parts) > 1:
+        even = (place & step) == 0
+        parts = [
+            jnp.where(even, x, y) + pltpu.roll(jnp.where(even, y, x), step, 0)
+            for x, y in zip(parts[::2], parts[1::2])
+        ]
+        step *= 2
+    return parts[0]
+
+
 def apply_blocks(ref, values):
+    count = values.shape[1]
+    tiles = values.reshape(NODES // 8, 8, count)
     out = []
     for group in range(NODES // 8):
-        block = ref[8 * group : 8 * group + 8].astype(F32) * values[None]
-        out.append(jnp.sum(block, axis=1))
+        parts = []
+        for node in range(8 * group, 8 * group + 8):
+            parts.append(jnp.sum(ref[node].astype(F32).reshape(NODES // 8, 8, count) * tiles, axis=0))
+        out.append(fold(parts))
     return jnp.concatenate(out, 0)
 
 
@@ -180,9 +218,9 @@
     return dot_split(halves(lift), halves(jnp.concatenate([low, high], 0)), TN)
 
 
-def first_kernel(
-    start_ref, rhs_ref, diag_ref, precond_ref, lift_ref, neighbour_ref, orient_ref,
-    partial_ref, message_ref,
+def first_half(
+    start_ref, rhs_ref, diag_ref, precond_ref, lift_ref, neighbour_ref, orient_ref, owner_rank,
+    partial_ref, message_ref, wait_precond,
 ):
     traces = face_traces(start_ref)
     shape = traces[2].shape
@@ -190,24 +228,30 @@
     none = jnp.zeros(shape, F32)
     coupled = coupling(traces, none, none, neighbour_ref, orient_ref, lift_ref)
     resid = rhs_ref[...] - (apply_blocks(diag_ref, start_ref[...]) - coupled)
+    wait_precond()
     partial_ref[...] = start_ref[...] + apply_blocks(precond_ref, resid)
     direct = edge_mask(shape)
-    later = pack_rim(face_traces(partial_ref))
-    message_ref[0:16] = jnp.where(direct, pack_rim(traces), pltpu.roll(later, count // 2, 1))
     reply = response(precond_ref, lift_ref)
     for spot in range(8):
-        message_ref[16 + 16 * spot : 32 + 16 * spot] = jnp.where(
+        message_ref[48 + 16 * spot : 64 + 16 * spot] = jnp.where(
             direct, reply[spot], pltpu.roll(reply[spot + 8], count // 2, 1)
-        )
+        ).astype(BF16)
+    later = pack_rim(face_traces(partial_ref))
+    high, low = halves(jnp.where(direct, pack_rim(traces), pltpu.roll(later, count // 2, 1)))
+    message_ref[0:16] = high
+    message_ref[16:32] = low
     orient = both_halves((1, count), orient_ref[2:3], orient_ref[3:4])
-    message_ref[144:152] = jnp.broadcast_to(orient.astype(F32), (8, count))
+    owner, rank = owner_rank
+    place = rows(shape)
+    facts = jnp.where(place < 4, orient, jnp.where(place < 8, owner, rank))
+    message_ref[32:48] = facts.astype(F32).astype(BF16)
 
 
 def merged(pos_ref, gathered_ref, at):
     slabs = gathered_ref.shape[0]
     pos = pos_ref[0]
-    above = gathered_ref[jnp.minimum(pos + 1, slabs - 1), at]
-    below = gathered_ref[jnp.maximum(pos - 1, 0), at]
+    above = gathered_ref[jnp.minimum(pos + 1, slabs - 1), at].astype(F32)
+    below = gathered_ref[jnp.maximum(pos - 1, 0), at].astype(F32)
     above = jnp.where(pos < slabs - 1, above, 0.0)
     below = jnp.where(pos > 0, below, 0.0)
     return jnp.where(low_mask(above.shape), above, below)
@@ -218,16 +262,24 @@
     return pltpu.roll(values, count // 4, 1), pltpu.roll(values, count - count // 4, 1)
 
 
+def target_of(facts, staying, capacity):
+    owner = facts[4:5].astype(jnp.int32)
+    rank = facts[8:9].astype(jnp.int32)
+    return jnp.where(lanes(owner.shape) >= staying, owner * capacity + rank, -1)
+
+
 def middle_kernel(
+    staying, capacity,
     pos_ref, gathered_ref, start_ref, partial_ref, rhs_ref, diag_ref, precond_ref, lift_ref,
-    neighbour_ref, orient_ref,
-    out_ref, rest_ref, rim_ref, sol_ref,
+    neighbour_ref, orient_ref, slot_ref,
+    out_ref, rest_ref, rim_ref, facts_ref, edge_ref, sol_ref, new_ref, sem,
 ):
     own = face_traces(start_ref)
     shape = own[2].shape
     count = shape[1]
-    head = merged(pos_ref, gathered_ref, pl.ds(0, 16))
-    orient = merged(pos_ref, gathered_ref, pl.ds(144, 8))[0:1].astype(jnp.int32)
+    head = merged(pos_ref, gathered_ref, pl.ds(0, 16)) + merged(pos_ref, gathered_ref, pl.ds(16, 16))
+    known = merged(pos_ref, gathered_ref, pl.ds(32, 16))
+    orient = known[0:1].astype(jnp.int32)
     sent = both_halves(shape, aside(own[3])[0], aside(own[2])[1])
     sent = turn(sent, orient)
     below, above = aside(head)
@@ -236,31 +288,94 @@
     later = pltpu.roll(head, count // 2, 1)
     reply = []
     for spot in range(8):
-        block = merged(pos_ref, gathered_ref, pl.ds(16 + 16 * spot, 16))
+        block = merged(pos_ref, gathered_ref, pl.ds(48 + 16 * spot, 16))
         reply.append((block, pltpu.roll(block, count // 2, 1)))
     reply = [pair[0] for pair in reply] + [pair[1] for pair in reply]
-    change = [jnp.sum(block * sent, axis=0, keepdims=True) for block in reply]
-    below, above = aside(later + jnp.concatenate(change, 0))
+    change = [block * sent for block in reply]
+    change = [block[:8] + block[8:] for block in change]
+    change = jnp.concatenate([fold(change[:8]), fold(change[8:])], 0)
+    below, above = aside(later + change)
     traces = face_traces(sol_ref)
     coupled = coupling(traces, below, above, neighbour_ref, orient_ref, lift_ref)
     resid = rhs_ref[...] - (apply_blocks(diag_ref, sol_ref[...]) - coupled)
-    out_ref[...] = sol_ref[...] + apply_blocks(precond_ref, resid)
-    traces = face_traces(out_ref)
+    new_ref[...] = sol_ref[...] + apply_blocks(precond_ref, resid)
+    copy = pltpu.make_async_copy(new_ref, out_ref, sem)
+    copy.start()
+    traces = face_traces(new_ref)
     none = jnp.zeros(shape, F32)
     coupled = coupling(traces, none, none, neighbour_ref, orient_ref, lift_ref)
-    rest_ref[...] = rhs_ref[...] - (apply_blocks(diag_ref, out_ref[...]) - coupled)
+    rest_ref[...] = rhs_ref[...] - (apply_blocks(diag_ref, new_ref[...]) - coupled)
     rim_ref[...] = pack_rim(traces)
-
-
-def targets(owner_row, staying, owner_count, capacity):
+    mine = gathered_ref[pos_ref[0], pl.ds(32, 16)].astype(F32)
+    target = jnp.where(
+        lanes((1, count)) >= count - count // 4, target_of(known, staying, capacity), -1
+    )
+    place = rows((8, count))
+    facts = jnp.where(place == 0, orient, target)
+    facts = jnp.where(place == 2, target_of(mine, staying, capacity), facts)
+    facts = jnp.where(place == 3, orient_ref[2:3], facts)
+    facts_ref[...] = jnp.where(place == 4, slot_ref[...], facts)
+    edge_ref[...] = lift_ref[2:4].reshape(32, NODES)
+    copy.wait()
+
+
+def spread(values, copies):
+    none = jnp.zeros(values.shape, values.dtype)
+    return jnp.concatenate(
+        [
+            jnp.concatenate([values if i == j else none for j in range(copies)], 1)
+            for i in range(copies)
+        ],
+        0,
+    )
+
+
+def packed_by_target(values, target, owners, depth):
+    count = values.shape[1]
+    shape = (owners * depth, count)
+    place = rows(shape)
+    base = (place // depth) * (GROUP * depth) + place % depth
+    hits = jnp.concatenate([one_hot(base + depth * g == target) for g in range(GROUP)], 1)
+    made = dot(hits, spread(values, GROUP), NT)
+    return made.reshape(owners, depth, GROUP * values.shape[0])
+
+
+def send_kernel(pos_ref, rest_ref, rim_ref, facts_ref, after_ref, send_ref):
+    pos = pos_ref[0]
+    count = rest_ref.shape[1]
+    edge = count // 4
+    owners, slabs, depth, _ = send_ref.shape
+    high, low = halves(rest_ref[...])
+    keep = lanes(low.shape) >= count - edge
+    low = jnp.where(keep, low.astype(F32), 0.0).astype(BF16)
+    made = dot_split(halves(small_table()), (high, low), NN)
+    send_ref[...] = jnp.zeros(send_ref.shape, BF16)
+    ours = packed_by_target(made.astype(BF16), facts_ref[2:3], owners, depth)
+    send_ref[:, pl.ds(pos, 1)] = ours.astype(BF16)[:, None]
+    moved_up, moved_down = aside(rim_ref[...])
+
+    @pl.when(pos > 0)
+    def _():
+        turned = turn(moved_down, facts_ref[0:1])
+        turned = jnp.concatenate([turned, jnp.zeros(turned.shape, F32)], 0).astype(BF16)
+        theirs = packed_by_target(turned, facts_ref[1:2], owners, depth)
+        send_ref[:, pl.ds(pos - 1, 1)] = theirs.astype(BF16)[:, None]
+
+    @pl.when(pos < slabs - 1)
+    def _():
+        group = lanes((8, count)) // edge
+        rim = jnp.where(group == 0, moved_up[0:8], pltpu.roll(moved_up[8:16], edge, 1))
+        send_ref[pl.ds(pos_ref[1], 1), pl.ds(pos + 1, 1), 0:8] = rim.astype(BF16)[None, None]
+
+
+def rank_row(owner_row, staying, owner_count):
     count = owner_row.shape[1]
     shape = (owner_count, count)
     hits = (rows(shape) == owner_row) & (lanes(shape) >= staying)
     hits = jnp.where(hits, 1.0, 0.0)
     before = jnp.where(rows((count, count)) < lanes((count, count)), 1.0, 0.0)
     earlier = dot(hits.astype(BF16), before.astype(BF16), NN)
-    rank = jnp.sum(hits * earlier, axis=0, keepdims=True).astype(jnp.int32)
-    return jnp.where(lanes(owner_row.shape) >= staying, owner_row * capacity + rank, -1)
+    return jnp.sum(hits * earlier, axis=0, keepdims=True).astype(jnp.int32)
 
 
 def one_hot(condition):
@@ -277,16 +392,33 @@
     ]
 
 
-def galerkin_kernel(
-    staying, owner_count, capacity,
-    diag_ref, owner_ref, slot_ref, table_ref,
-    send_ref, local_ref, target_ref, high_ref, low_ref, full_ref,
-):
+def first_kernel(staying, owner_count, capacity, *refs):
+    (diag_in, slot_in, owner_in, table_in, start_in, rhs_in, lift_in, neighbour_in, orient_in, precond_in) = refs[:10]
+    (send_out, local_out, partial_out, message_out) = refs[10:14]
+    (diag_ref, slot_ref, owner_ref, table_ref, start_ref, rhs_ref, lift_ref, neighbour_ref) = refs[14:22]
+    (orient_ref, precond_ref, send_ref, local_ref, partial_ref, message_ref) = refs[22:28]
+    (high_ref, low_ref, full_ref, part_sem, sem, out_sem) = refs[28:]
     line = restrict_line()
     count = diag_ref.shape[2]
     chunk = 16
 
+    def part_copy(part):
+        at = pl.ds(pl.multiple_of(part * chunk, chunk), chunk)
+        return pltpu.make_async_copy(diag_in.at[:, at], diag_ref.at[:, at], part_sem.at[part])
+
+    pairs = [
+        (slot_in, slot_ref), (owner_in, owner_ref), (table_in, table_ref), (start_in, start_ref),
+        (rhs_in, rhs_ref), (lift_in, lift_ref), (neighbour_in, neighbour_ref), (orient_in, orient_ref),
+        (precond_in, precond_ref),
+    ]
+    copies = [pltpu.make_async_copy(src, dst, sem.at[i]) for i, (src, dst) in enumerate(pairs)]
+    for part in range(NODES // chunk):
+        part_copy(part).start()
+    for copy in copies:
+        copy.start()
+
     def step(part, carry):
+        part_copy(part).wait()
         at = pl.ds(pl.multiple_of(part * chunk, chunk), chunk)
         planes = []
         for i in range(4):
@@ -308,6 +440,8 @@
     high_ref[COARSE] = jnp.zeros((NODES, count), BF16)
     low_ref[COARSE] = jnp.zeros((NODES, count), BF16)
     full_ref[...] = jnp.zeros(full_ref.shape, F32)
+    for copy in copies[:3]:
+        copy.wait()
     padded = table_ref.shape[0] // 2
     table = table_ref[...]
     for part in range(high_ref.shape[0] // GROUP):
@@ -319,65 +453,93 @@
     full_ref[COARSE * COARSE : COARSE * COARSE + 1] = (slot_ref[...] + 1).astype(F32)
     local = full_ref[...].astype(BF16)
     local_ref[...] = local
-    target = targets(owner_ref[...], staying, owner_count, capacity)
-    target_ref[...] = target
+    owner = owner_ref[...]
+    rank = rank_row(owner, staying, owner_count)
+    target = jnp.where(lanes(owner.shape) >= staying, owner * capacity + rank, -1)
     shape = (owner_count * capacity, count)
     send_ref[...] = dot(one_hot(rows(shape) == target), local, NT).astype(BF16)
-
-
-def slot_hits(got_ref, aggregates):
-    ids = got_ref[:, COARSE * COARSE : COARSE * COARSE + 1].astype(F32)
+    pairs = [(send_ref, send_out), (local_ref, local_out), (partial_ref, partial_out), (message_ref, message_out)]
+    out = [pltpu.make_async_copy(src, dst, out_sem.at[i]) for i, (src, dst) in enumerate(pairs)]
+    out[0].start()
+    out[1].start()
+    for copy in copies[3:8]:
+        copy.wait()
+    first_half(
+        start_ref, rhs_ref, diag_ref, precond_ref, lift_ref, neighbour_ref, orient_ref, (owner, rank),
+        partial_ref, message_ref, copies[8].wait,
+    )
+    out[2].start()
+    out[3].start()
+    for copy in out:
+        copy.wait()
+
+
+def block_sum(made, height, width):
+    total = made[0:height, 0:width]
+    for g in range(1, GROUP):
+        total = total + made[height * g : height * g + height, width * g : width * g + width]
+    return total
+
+
+def operator_kernel(staying, got_ref, local_ref, facts_ref, op_ref, hits_ref):
+    aggregates = op_ref.shape[0]
+    count = local_ref.shape[1]
+    owners, capacity, _ = got_ref.shape
+    got = got_ref[...].reshape(owners * capacity, got_ref.shape[2])
+    ids = got[:, COARSE * COARSE : COARSE * COARSE + 1].astype(F32)
     shape = (ids.shape[0], aggregates)
-    return one_hot(ids == (lanes(shape) + 1).astype(F32))
-
-
-def stay_hits(slot_ref, staying, aggregates):
-    shape = (aggregates, slot_ref.shape[1])
-    return one_hot((rows(shape) == slot_ref[...]) & (lanes(shape) < staying))
-
-
-def gather_op_kernel(staying, got_ref, local_ref, slot_ref, out_ref):
+    hits = jnp.where(ids == (lanes(shape) + 1).astype(F32), 1.0, 0.0)
+    stay = stay_hits(facts_ref, staying, aggregates)
+    total = dot(hits.astype(BF16), got, TN) + dot(stay, local_ref[...], NT)
+    op_ref[...] = total[:, : COARSE * COARSE]
+    depth = capacity // GROUP
+    hits = hits.reshape(owners, GROUP, depth, aggregates)
+    hits_ref[...] = jnp.concatenate(
+        [hits[:, g].reshape(owners * depth, aggregates) for g in range(GROUP)], 1
+    ).astype(BF16)
+
+
+def stay_hits(facts_ref, staying, aggregates):
+    slot = facts_ref[4:5]
+    shape = (aggregates, slot.shape[1])
+    return one_hot((rows(shape) == slot) & (lanes(shape) < staying))
+
+
+def last_kernel(staying, pos_ref, got_ref, hits_ref, rest_ref, facts_ref, edge_ref, out_ref):
+    pos = pos_ref[0]
+    owners, slabs, depth, width = got_ref.shape
     aggregates = out_ref.shape[1]
-    total = dot(slot_hits(got_ref, aggregates), got_ref[...], TN)
-    total = total + dot(stay_hits(slot_ref, staying, aggregates), local_ref[...], NT)
-    out_ref[...] = total.T[: COARSE * COARSE]
-
-
-def last_kernel(
-    pos_ref, gathered_ref, rest_ref, lift_ref, orient_ref, target_ref, after_ref,
-    low_ref, send_ref,
-):
-    below, above = aside(merged(pos_ref, gathered_ref, pl.ds(0, 16)))
-    resid = rest_ref[...] + halo_lift(below, above, orient_ref, lift_ref)
-    low = resid.astype(BF16)
-    low_ref[...] = low
-    shape = (send_ref.shape[0], low.shape[1])
-    send_ref[...] = dot(one_hot(rows(shape) == target_ref[...]), low, NT).astype(BF16)
-
-
-def gather_rhs_kernel(staying, got_ref, ids_ref, low_ref, slot_ref, table_ref, out_ref):
-    aggregates = out_ref.shape[1]
-    total = dot(got_ref[...], slot_hits(ids_ref, aggregates), TN)
-    total = total + dot(low_ref[...], stay_hits(slot_ref, staying, aggregates), NT)
-    padded = table_ref.shape[0] // 2
-    high, low = halves(total)
-    both = dot(table_ref[...], high, NN)
-    made = both[:padded] + both[padded:] + dot(table_ref[:padded], low, NN)
-    out_ref[...] = made[:COARSE]
-
-
-def call(kernel, outs, args, scratch=(), flops=0, scalars=0, anywhere=0):
+    count = rest_ref.shape[1]
+    edge = count // 4
+    hits = hits_ref[...]
+    main = got_ref[:, pl.ds(pos, 1)].astype(F32).reshape(owners * depth, width).astype(BF16)
+    side = got_ref[:, pl.ds(jnp.minimum(pos + 1, slabs - 1), 1)]
+    side = jnp.where(pos < slabs - 1, side.astype(F32).reshape(owners * depth, width), 0.0).astype(BF16)
+    main = block_sum(dot(main, hits, TN), width // GROUP, aggregates)
+    side = block_sum(dot(side, hits, TN), width // GROUP, aggregates)[0:16]
+
+    rim = got_ref[pl.ds(pos_ref[1], 1), pl.ds(jnp.maximum(pos - 1, 0), 1), 0:8]
+    rim = jnp.where(pos > 0, rim.astype(F32).reshape(8, width), 0.0)
+    rim = jnp.concatenate([rim, pltpu.roll(rim, count - edge, 1)], 0)
+    rim = jnp.where(lanes(rim.shape) < edge, turn(rim, facts_ref[3:4]), 0.0)
+    rest = rest_ref[...] + dot_split(halves(edge_ref[0:16]), halves(rim), TN)
+    nodes = dot(rest.astype(BF16), stay_hits(facts_ref, staying, aggregates), NT)
+    nodes = nodes + dot_split(halves(edge_ref[16:32]), halves(side), TN)
+    made = dot_split(halves(small_table()), halves(nodes), NN)
+    out_ref[...] = (made + main)[:COARSE]
+
+
+def call(kernel, outs, args, spaces, out_spaces=None, scratch=(), flops=0, limit=VMEM_LIMIT):
     bytes_in = sum(a.size * a.dtype.itemsize for a in args)
     bytes_out = sum(o.size * o.dtype.itemsize for o in outs)
-    spaces = [pltpu.SMEM] * scalars + [pltpu.VMEM] * (len(args) - scalars - anywhere) + [pl.ANY] * anywhere
-    specs = [pl.BlockSpec(memory_space=space) for space in spaces]
+    out_spaces = out_spaces or [pltpu.VMEM] * len(outs)
     return pl.pallas_call(
         kernel,
         out_shape=tuple(outs),
-        in_specs=specs,
-        out_specs=tuple(pl.BlockSpec(memory_space=pltpu.VMEM) for _ in outs),
+        in_specs=[pl.BlockSpec(memory_space=space) for space in spaces],
+        out_specs=tuple(pl.BlockSpec(memory_space=space) for space in out_spaces),
         scratch_shapes=list(scratch),
-        compiler_params=pltpu.CompilerParams(vmem_limit_bytes=VMEM_LIMIT),
+        compiler_params=pltpu.CompilerParams(vmem_limit_bytes=limit),
         cost_estimate=pl.CostEstimate(
             flops=flops, bytes_accessed=bytes_in + bytes_out, transcendentals=0
         ),
@@ -406,72 +568,95 @@
     staying = count // 4
     aggregates = count // 2
     owner_count = lax.axis_size("dom")
+    slabs = lax.axis_size("face")
     movers = count - staying
-    capacity = ceil_to(2 * ((movers + owner_count - 2) // (owner_count - 1)), 16)
+    capacity = 2 * ((movers + owner_count - 2) // (owner_count - 1))
+    depth = ceil_to(-(-max(capacity, count // 4) // GROUP), 8)
+    capacity = GROUP * depth
     total = owner_count * capacity
     entries = ceil_to(COARSE * COARSE + 1, 128)
     groups = -(-COARSE // GROUP)
-    pos = jnp.reshape(lax.axis_index("face"), (1,)).astype(jnp.int32)
+    pos = jnp.stack([lax.axis_index("face"), lax.axis_index("dom")]).astype(jnp.int32)
     owner = owner.reshape(1, count)
     slot = slot.reshape(1, count)
     table = jnp.asarray(block_table(restrict_table(), GROUP, 16))
-    small = jnp.asarray(block_table(restrict_table(), 1, 16))
-
-    op_send, local_op, target = call(
-        lambda *refs: galerkin_kernel(staying, owner_count, capacity, *refs),
-        [
-            struct((total, entries), BF16),
-            struct((entries, count), BF16),
-            struct((1, count), jnp.int32),
-        ],
-        [diag_block, owner, slot, table],
-        scratch=[
+
+    args = [diag_block, slot, owner, table, start, rhs, lift, neighbour, orient, precond]
+    outs = [
+        struct((total, entries), BF16),
+        struct((entries, count), BF16),
+        struct((NODES, count), F32),
+        struct((176, count), BF16),
+    ]
+    op_send, local_op, partial, message = call(
+        lambda *refs: first_kernel(staying, owner_count, capacity, *refs),
+        outs,
+        args,
+        [pl.ANY] * len(args),
+        [pl.ANY] * len(outs),
+        scratch=[pltpu.VMEM(each.shape, each.dtype) for each in args + outs]
+        + [
             pltpu.VMEM((groups * GROUP, NODES, count), BF16),
             pltpu.VMEM((groups * GROUP, NODES, count), BF16),
             pltpu.VMEM((entries, count), F32),
+            pltpu.SemaphoreType.DMA((NODES // 16,)),
+            pltpu.SemaphoreType.DMA((9,)),
+            pltpu.SemaphoreType.DMA((4,)),
         ],
         flops=200_000_000,
-    )
-    op_got = lax.all_to_all(op_send, "dom", split_axis=0, concat_axis=0, tiled=True)
-
-    partial, message = call(
-        first_kernel,
-        [struct((NODES, count), F32), struct((152, count), F32)],
-        [start, rhs, diag_block, precond, lift, neighbour, orient],
+        limit=FIRST_LIMIT,
+    )
+    op_got = lax.all_to_all(
+        op_send.reshape(owner_count, capacity, entries), "dom", split_axis=0, concat_axis=0, tiled=True
+    )
+    gathered = lax.all_gather(message, "face")
+    sol, rest, rim, facts, edge = call(
+        lambda *refs: middle_kernel(staying, capacity, *refs),
+        [
+            struct((NODES, count), F32),
+            struct((NODES, count), F32),
+            struct((16, count), F32),
+            struct((8, count), jnp.int32),
+            struct((32, NODES), F32),
+        ],
+        [pos, gathered, start, partial, rhs, diag_block, precond, lift, neighbour, orient, slot],
+        [pltpu.SMEM] + [pltpu.VMEM] * 10,
+        [pl.ANY] + [pltpu.VMEM] * 4,
+        scratch=[
+            pltpu.VMEM((NODES, count), F32),
+            pltpu.VMEM((NODES, count), F32),
+            pltpu.SemaphoreType.DMA(()),
+        ],
+        flops=200_000_000,
+    )
+    (send,) = call(
+        send_kernel,
+        [struct((owner_count, slabs, depth, 128), BF16)],
+        [pos, rest, rim, facts, op_got],
+        [pltpu.SMEM] + [pltpu.VMEM] * 3 + [pl.ANY],
         flops=100_000_000,
     )
-    gathered = lax.all_gather(message, "face")
-    sol, rest, rim = call(
-        middle_kernel,
-        [struct((NODES, count), F32), struct((NODES, count), F32), struct((16, count), F32)],
-        [pos, gathered, start, partial, rhs, diag_block, precond, lift, neighbour, orient],
-        scratch=[pltpu.VMEM((NODES, count), F32)],
-        flops=200_000_000,
-        scalars=1,
-    )
-    gathered = lax.all_gather(rim, "face")
-    low, rhs_send = call(
-        last_kernel,
-        [struct((NODES, count), BF16), struct((total, NODES), BF16)],
-        [pos, gathered, rest, lift, orient, target, op_got],
+    got = lax.all_to_all(
+        send.reshape(owner_count * slabs, depth, 128), ("dom", "face"), split_axis=0, concat_axis=0, tiled=True
+    ).reshape(owner_count, slabs, depth, 128)
+    coarse_op, hits = call(
+        lambda *refs: operator_kernel(staying, *refs),
+        [
+            struct((aggregates, COARSE * COARSE), F32),
+            struct((owner_count * depth, GROUP * aggregates), BF16),
+        ],
+        [op_got, local_op, facts],
+        [pltpu.VMEM] * 3,
         flops=100_000_000,
-        scalars=1,
-        anywhere=1,
-    )
-    rhs_got = lax.all_to_all(rhs_send, "dom", split_axis=0, concat_axis=0, tiled=True)
-    (coarse_op,) = call(
-        lambda *refs: gather_op_kernel(staying, *refs),
-        [struct((COARSE * COARSE, aggregates), F32)],
-        [op_got, local_op, slot],
+    )
+    (coarse_rhs,) = call(
+        lambda *refs: last_kernel(staying, *refs),
+        [struct((COARSE, aggregates), F32)],
+        [pos, got, hits, rest, facts, edge],
+        [pltpu.SMEM] + [pltpu.VMEM] * 5,
         flops=100_000_000,
     )
-    (coarse_rhs,) = call(
-        lambda *refs: gather_rhs_kernel(staying, *refs),
-        [struct((COARSE, aggregates), F32)],
-        [rhs_got, op_got, low, slot, small],
-        flops=10_000_000,
-    )
-    return (sol, coarse_op, coarse_rhs)
+    return (sol, coarse_op.T, coarse_rhs)
 
 
 def solution(mesh):

time: 44 us -> 38.7 us (0.88)
  local copies, waits for them, and re-layouts: 6.31 us -> 0.66 us
  blocking collectives: 11.2 us -> 5.69 us
  Pallas kernels: 6.41 us -> 10.7 us
  waiting for transfers between devices: 5.42 us -> 9.4 us
  starting transfers between devices: 13.4 us -> 11.1 us
    unnamed x27 -> x22, local copies, waits for them, and re-layouts: 6.31 us -> 0.66 us
    all_gather x1 -> x0, blocking collectives: 5.18 us -> none  [per_device(): gathered = lax.all_gather(rim, 'face')]
    pallas_call x6 -> x5, Pallas kernels: 6.41 us -> 10.7 us  [call(): pl.pallas_call(kernel, out_shape=tuple(outs), in_specs=[pl.BlockSpec(memo...]
    all_to_all x2, waiting for transfers between devices: 5.42 us -> 9.4 us  [the longest x1 6.34 us: per_device(): lax.all_to_all(send.reshape(owner_count * slabs, depth, 128), ('dom', 'fa...]
    all_to_all x2, starting transfers between devices: 13.4 us -> 11.1 us  [the longest x1 7.26 us: per_device(): lax.all_to_all(op_send.reshape(owner_count, capacity, entries), 'dom', sp...]
  transfers between devices with their start and end apart: 2 -> 2, of which waited for: 1 -> 2; matrix products, arithmetic and copies ran while one was open for 2% -> 0% of each run, Pallas kernels for 7% -> 8%
where the time goes in v3:
time: 38.7 us; the launch traced here: 38.4 us
  starting transfers between devices  11.1 us (29%)
  Pallas kernels  10.7 us (28%)
  waiting for transfers between devices  9.4 us (24%)
  blocking collectives  5.69 us (15%)
  between operations  0.76 us (2%)
  local copies, waits for them, and re-layouts  0.66 us (2%)
    pallas_call x5, Pallas kernels, call(): pl.pallas_call(kernel, out_shape=tuple(outs), in_specs=[pl.BlockSpec(memo...  10.7 us
    all_to_all x1, starting transfers between devices, per_device(): lax.all_to_all(op_send.reshape(owner_count, capacity, entries), 'dom', sp...  7.26 us
    all_to_all x1, waiting for transfers between devices, per_device(): lax.all_to_all(send.reshape(owner_count * slabs, depth, 128), ('dom', 'fa...  6.34 us
    all_gather x1, blocking collectives, per_device(): gathered = lax.all_gather(message, 'face')  5.69 us
    all_to_all x1, starting transfers between devices, per_device(): lax.all_to_all(send.reshape(owner_count * slabs, depth, 128), ('dom', 'fa...  3.81 us
    all_to_all x1, waiting for transfers between devices, per_device(): lax.all_to_all(op_send.reshape(owner_count, capacity, entries), 'dom', sp...  3.07 us
  transfers between devices with their start and end apart: 2, of which 2 were waited for; matrix products, arithmetic and copies ran while one was open for 0% of the time, Pallas kernels for 8%

profile of v3, /device:TPU:0, one launch (start us, length us, event | category | flops | bytes accessed | tf_op | source)
XLA Modules:
  0.0 38.4 jit_solution(7929183702958869125)
XLA Ops:
  0.6 0.0 copy-start
  0.6 0.0 copy-start.1
  0.7 4.2 %shard_map.121 = (bf16[256,768]{1,0:T(8,128)(2,1)}, bf16[768,128]{1,0:T(8,128)(2,1)}, f32[64,128]{1,0:T(8,128)}, bf16[176,128]{1,0:T(8,128)(2,1)}) custom-call(bf16[64,64,128]{2,1,0:T(8,128)(2,1)} %refs_5_.3, s32[1,128]{1,0:T(1,128)} %bitcast.11, s32[1,128]{1,0:T(1,128)} %bitcast.14, bf16[224,256]{1,0:T(8,128)(2,1)} %constant.11.clone.refs_3_, ...), custom_call_target="tpu_custom_call" | custom-call | flops 200000000 | bytes 2976768 | tf_op jit(solution)/shard_map/pallas_call | solution.py:536
  4.8 0.0 copy-start.10
  4.8 7.3 %all-to-all-start = ((bf16[8,32,768]{2,1,0:T(8,128)(2,1)}), bf16[8,32,768]{2,1,0:T(8,128)(2,1)S(1)}, u32[]{:S(2)}, u32[]{:S(2)}) async-start(bf16[8,32,768]{2,1,0:T(8,128)(2,1)} %bitcast.13), calls=%async_computation | async-start | bytes 786432 | tf_op jit(solution)/shard_map/all_to_all | solution.py:609
  12.1 0.0 copy-done.10
  12.1 0.0 copy-start.3
  12.1 0.0 copy-start.4
  12.1 0.0 copy-start.5
  12.2 0.0 copy-start.6
  12.2 5.7 %all-gather = bf16[704,128]{1,0:T(8,128)(2,1)S(1)} all-gather(bf16[176,128]{1,0:T(8,128)(2,1)S(1)} %copy-done.10), channel_id=2, replica_groups=mesh['dom'=8,'face'=4] {'face'}, dimensions={0}, use_global_device_ids=true | all-gather | bytes 225280 | tf_op jit(solution)/shard_map/all_gather | solution.py:612
  17.9 0.0 copy-start.8
  17.9 0.0 copy-start.7
  17.9 0.1 pad_add_fusion.refs_0_.pos_ref
  17.9 0.0 copy-start.9
  17.9 0.0 copy-done
  17.9 0.0 copy-done.1
  17.9 0.0 copy-done.3
  18.0 0.0 copy-done.4
  18.0 0.0 copy-done.5
  18.0 0.0 copy-done.6
  18.0 0.6 %copy-done.8 = s32[6,128]{1,0:T(8,128)S(1)} copy-done((s32[6,128]{1,0:T(8,128)S(1)}, s32[6,128]{1,0:T(8,128)}, u32[]{:S(2)}) %copy-start.8) | copy-done | bytes 3096
  18.5 0.0 copy-done.7
  18.6 0.0 copy-done.9
  18.6 2.1 %shard_map.122 = (f32[64,128]{1,0:T(8,128)}, f32[64,128]{1,0:T(8,128)S(1)}, f32[16,128]{1,0:T(8,128)S(1)}, s32[8,128]{1,0:T(8,128)S(1)}, f32[32,64]{1,0:T(8,128)S(1)}) custom-call(s32[2]{0:T(128)S(1)} %pad_add_fusion.refs_0_.pos_ref, bf16[4,176,128]{2,1,0:T(8,128)(2,1)S(1)} %bitcast.9, f32[64,128]{1,0:T(8,128)S(1)} %copy-done.4, f32[64,128]{1,0:T(8,128)S(1)} %copy-done.6, ...), custom_call_target="tpu_custom_call" | custom-call | flops 200000000 | bytes 2492936 | tf_op jit(solution)/shard_map/pallas_call | solution.py:536
  20.7 3.1 %all-to-all-done.refs_0_.after_ref = bf16[8,32,768]{2,1,0:T(8,128)(2,1)S(1)} async-done(((bf16[8,32,768]{2,1,0:T(8,128)(2,1)}), bf16[8,32,768]{2,1,0:T(8,128)(2,1)S(1)}, u32[]{:S(2)}, u32[]{:S(2)}) %all-to-all-start) | async-done | bytes 393248 | tf_op jit(solution)/shard_map/all_to_all | solution.py:609
  23.8 0.0 copy-start.2
  23.8 1.6 %shard_map.124 = bf16[8,4,8,128]{3,2,1,0:T(8,128)(2,1)} custom-call(s32[2]{0:T(128)S(1)} %pad_add_fusion.refs_0_.pos_ref, f32[64,128]{1,0:T(8,128)S(1)} %get-tuple-element.21.rest_ref.refs_3_, f32[16,128]{1,0:T(8,128)S(1)} %get-tuple-element.22.rim_ref, s32[8,128]{1,0:T(8,128)S(1)} %get-tuple-element.19.refs_2_.facts_ref.refs_4_, ...), custom_call_target="tpu_custom_call" | custom-call | flops 100000000 | bytes 503816 | tf_op jit(solution)/shard_map/pallas_call | solution.py:536
  25.4 3.8 %all-to-all-start.1 = ((bf16[32,8,128]{2,1,0:T(8,128)(2,1)}), bf16[32,8,128]{2,1,0:T(8,128)(2,1)S(1)}, u32[]{:S(2)}, u32[]{:S(2)}) async-start(bf16[32,8,128]{2,1,0:T(8,128)(2,1)} %bitcast.7), calls=%async_computation.1 | async-start | bytes 131072 | tf_op jit(solution)/shard_map/all_to_all | solution.py:639
  29.2 0.0 copy-done.2
  29.2 1.1 %shard_map.123 = (f32[64,729]{1,0:T(8,128)}, bf16[64,256]{1,0:T(8,128)(2,1)S(1)}) custom-call(bf16[8,32,768]{2,1,0:T(8,128)(2,1)S(1)} %all-to-all-done.refs_0_.after_ref, bf16[768,128]{1,0:T(8,128)(2,1)S(1)} %copy-done.2, s32[8,128]{1,0:T(8,128)S(1)} %get-tuple-element.19.refs_2_.facts_ref.refs_4_), custom_call_target="tpu_custom_call" | custom-call | flops 100000000 | bytes 813312 | tf_op jit(solution)/shard_map/pallas_call | solution.py:536
  30.3 6.3 %all-to-all-done.1 = bf16[32,8,128]{2,1,0:T(8,128)(2,1)S(1)} async-done(((bf16[32,8,128]{2,1,0:T(8,128)(2,1)}), bf16[32,8,128]{2,1,0:T(8,128)(2,1)S(1)}, u32[]{:S(2)}, u32[]{:S(2)}) %all-to-all-start.1) | async-done | bytes 65568 | tf_op jit(solution)/shard_map/all_to_all | solution.py:639
  36.6 1.7 %shard_map.125 = f32[27,64]{1,0:T(8,128)} custom-call(s32[2]{0:T(128)S(1)} %pad_add_fusion.refs_0_.pos_ref, bf16[8,4,8,128]{3,2,1,0:T(8,128)(2,1)S(1)} %bitcast.10, bf16[64,256]{1,0:T(8,128)(2,1)S(1)} %get-tuple-element.23.refs_2_, f32[64,128]{1,0:T(8,128)S(1)} %get-tuple-element.21.rest_ref.refs_3_, ...), custom_call_target="tpu_custom_call" | custom-call | flops 100000000 | bytes 150280 | tf_op jit(solution)/shard_map/pallas_call | solution.py:536
Async XLA Ops:
  0.6 17.3 %copy-start = (bf16[64,64,128]{2,1,0:T(8,128)(2,1)S(1)}, bf16[64,64,128]{2,1,0:T(8,128)(2,1)}, u32[]{:S(2)}) copy-start(bf16[64,64,128]{2,1,0:T(8,128)(2,1)} %refs_5_.3) | copy-start | bytes 3145732
  0.6 17.3 %copy-start.1 = (bf16[64,64,128]{2,1,0:T(8,128)(2,1)S(1)}, bf16[64,64,128]{2,1,0:T(8,128)(2,1)}, u32[]{:S(2)}) copy-start(bf16[64,64,128]{2,1,0:T(8,128)(2,1)} %refs_6_.3) | copy-start | bytes 3145732
  4.8 7.3 %copy-start.10 = (bf16[176,128]{1,0:T(8,128)(2,1)S(1)}, bf16[176,128]{1,0:T(8,128)(2,1)}, u32[]{:S(2)}) copy-start(bf16[176,128]{1,0:T(8,128)(2,1)} %get-tuple-element.14) | copy-start | bytes 135172
  4.8 19.0 %all-to-all-start = ((bf16[8,32,768]{2,1,0:T(8,128)(2,1)}), bf16[8,32,768]{2,1,0:T(8,128)(2,1)S(1)}, u32[]{:S(2)}, u32[]{:S(2)}) async-start(bf16[8,32,768]{2,1,0:T(8,128)(2,1)} %bitcast.13), calls=%async_computation | async-start | bytes 786432 | tf_op jit(solution)/shard_map/all_to_all | solution.py:609
  12.1 5.8 %copy-start.3 = (f32[6,16,64]{2,1,0:T(8,128)S(1)}, f32[6,16,64]{2,1,0:T(8,128)}, u32[]{:S(2)}) copy-start(f32[6,16,64]{2,1,0:T(8,128)} %refs_7_.3) | copy-start | bytes 73732
  12.1 5.8 %copy-start.4 = (f32[64,128]{1,0:T(8,128)S(1)}, f32[64,128]{1,0:T(8,128)}, u32[]{:S(2)}) copy-start(f32[64,128]{1,0:T(8,128)} %refs_2_.1) | copy-start | bytes 98308
  12.1 5.8 %copy-start.5 = (f32[64,128]{1,0:T(8,128)S(1)}, f32[64,128]{1,0:T(8,128)}, u32[]{:S(2)}) copy-start(f32[64,128]{1,0:T(8,128)} %refs_4_.3) | copy-start | bytes 98308
  12.2 5.8 %copy-start.6 = (f32[64,128]{1,0:T(8,128)S(1)}, f32[64,128]{1,0:T(8,128)}, u32[]{:S(2)}) copy-start(f32[64,128]{1,0:T(8,128)} %get-tuple-element.15.refs_3_) | copy-start | bytes 98308
  17.9 0.7 %copy-start.8 = (s32[6,128]{1,0:T(8,128)S(1)}, s32[6,128]{1,0:T(8,128)}, u32[]{:S(2)}) copy-start(s32[6,128]{1,0:T(8,128)} %refs_9_.3) | copy-start | bytes 9220
  17.9 0.7 %copy-start.7 = (s32[6,128]{1,0:T(8,128)S(1)}, s32[6,128]{1,0:T(8,128)}, u32[]{:S(2)}) copy-start(s32[6,128]{1,0:T(8,128)} %refs_8_.3) | copy-start | bytes 9220
  17.9 0.7 %copy-start.9 = (s32[128]{0:T(128)S(1)}, s32[128]{0:T(128)}, u32[]{:S(2)}) copy-start(s32[128]{0:T(128)} %param.18) | copy-start | bytes 1540
  23.8 5.4 %copy-start.2 = (bf16[768,128]{1,0:T(8,128)(2,1)S(1)}, bf16[768,128]{1,0:T(8,128)(2,1)}, u32[]{:S(2)}) copy-start(bf16[768,128]{1,0:T(8,128)(2,1)} %get-tuple-element.18.refs_1_) | copy-start | bytes 589828
  25.4 11.2 %all-to-all-start.1 = ((bf16[32,8,128]{2,1,0:T(8,128)(2,1)}), bf16[32,8,128]{2,1,0:T(8,128)(2,1)S(1)}, u32[]{:S(2)}, u32[]{:S(2)}) async-start(bf16[32,8,128]{2,1,0:T(8,128)(2,1)} %bitcast.7), calls=%async_computation.1 | async-start | bytes 131072 | tf_op jit(solution)/shard_map/all_to_all | solution.py:639

commit v4 on v3

--- a/solution.py
+++ b/solution.py
@@ -11,6 +11,7 @@
 COARSE = 27
 FACES = 6
 GROUP = 4
+SPLIT = 23
 F32 = jnp.float32
 BF16 = jnp.bfloat16
 VMEM_LIMIT = 24 * 1024 * 1024
@@ -218,17 +219,41 @@
     return dot_split(halves(lift), halves(jnp.concatenate([low, high], 0)), TN)
 
 
-def first_half(
-    start_ref, rhs_ref, diag_ref, precond_ref, lift_ref, neighbour_ref, orient_ref, owner_rank,
-    partial_ref, message_ref, wait_precond,
+START = 0
+RHS = NODES
+LIFT = 2 * NODES
+NEIGHBOUR = LIFT + FACES * 16
+ORIENT = NEIGHBOUR + 8
+OWNER = ORIENT + 8
+SLOT = OWNER + 1
+PACKED = ORIENT + 16
+
+
+class Packed:
+    def __init__(self, ref):
+        self.start = ref.at[START : START + NODES]
+        self.rhs = ref.at[RHS : RHS + NODES]
+        self.lift = ref[LIFT : LIFT + FACES * 16, 0:NODES].reshape(FACES, 16, NODES)
+        self.neighbour = ref[NEIGHBOUR : NEIGHBOUR + FACES].astype(jnp.int32)
+        self.orient = ref[ORIENT : ORIENT + FACES].astype(jnp.int32)
+        self.owner = ref[OWNER : OWNER + 1].astype(jnp.int32)
+        self.slot = ref[SLOT : SLOT + 1].astype(jnp.int32)
+
+
+def smooth_kernel(
+    staying, owner_count,
+    diag_ref, precond_ref, pack_ref,
+    message_ref, partial_ref,
 ):
+    count = diag_ref.shape[2]
+    packed = Packed(pack_ref)
+    start_ref, rhs_ref = packed.start, packed.rhs
+    lift_ref, neighbour_ref, orient_ref = packed.lift, packed.neighbour, packed.orient
     traces = face_traces(start_ref)
     shape = traces[2].shape
-    count = shape[1]
     none = jnp.zeros(shape, F32)
     coupled = coupling(traces, none, none, neighbour_ref, orient_ref, lift_ref)
     resid = rhs_ref[...] - (apply_blocks(diag_ref, start_ref[...]) - coupled)
-    wait_precond()
     partial_ref[...] = start_ref[...] + apply_blocks(precond_ref, resid)
     direct = edge_mask(shape)
     reply = response(precond_ref, lift_ref)
@@ -241,15 +266,16 @@
     message_ref[0:16] = high
     message_ref[16:32] = low
     orient = both_halves((1, count), orient_ref[2:3], orient_ref[3:4])
-    owner, rank = owner_rank
+    owner = packed.owner
+    rank = rank_row(owner, staying, owner_count)
     place = rows(shape)
     facts = jnp.where(place < 4, orient, jnp.where(place < 8, owner, rank))
     message_ref[32:48] = facts.astype(F32).astype(BF16)
 
 
-def merged(pos_ref, gathered_ref, at):
+def merged(gathered_ref, at):
     slabs = gathered_ref.shape[0]
-    pos = pos_ref[0]
+    pos = lax.axis_index("face")
     above = gathered_ref[jnp.minimum(pos + 1, slabs - 1), at].astype(F32)
     below = gathered_ref[jnp.maximum(pos - 1, 0), at].astype(F32)
     above = jnp.where(pos < slabs - 1, above, 0.0)
@@ -270,25 +296,28 @@
 
 def middle_kernel(
     staying, capacity,
-    pos_ref, gathered_ref, start_ref, partial_ref, rhs_ref, diag_ref, precond_ref, lift_ref,
-    neighbour_ref, orient_ref, slot_ref,
+    gathered_ref, diag_ref, precond_ref, pack_ref, partial_ref,
     out_ref, rest_ref, rim_ref, facts_ref, edge_ref, sol_ref, new_ref, sem,
 ):
-    own = face_traces(start_ref)
-    shape = own[2].shape
-    count = shape[1]
-    head = merged(pos_ref, gathered_ref, pl.ds(0, 16)) + merged(pos_ref, gathered_ref, pl.ds(16, 16))
-    known = merged(pos_ref, gathered_ref, pl.ds(32, 16))
+    count = diag_ref.shape[2]
+    shape = (16, count)
+    pos = lax.axis_index("face")
+    packed = Packed(pack_ref)
+    rhs_ref, slot = packed.rhs, packed.slot
+    lift_ref, neighbour_ref, orient_ref = packed.lift, packed.neighbour, packed.orient
+    head = merged(gathered_ref, pl.ds(0, 16)) + merged(gathered_ref, pl.ds(16, 16))
+    known = merged(gathered_ref, pl.ds(32, 16))
     orient = known[0:1].astype(jnp.int32)
-    sent = both_halves(shape, aside(own[3])[0], aside(own[2])[1])
-    sent = turn(sent, orient)
+    own = gathered_ref[pos, pl.ds(0, 16)].astype(F32) + gathered_ref[pos, pl.ds(16, 16)].astype(F32)
+    from_high, from_low = aside(own)
+    sent = turn(both_halves(shape, from_high, from_low), orient)
     below, above = aside(head)
     delta = halo_lift(below, above, orient_ref, lift_ref)
     sol_ref[...] = partial_ref[...] + apply_blocks(precond_ref, delta)
     later = pltpu.roll(head, count // 2, 1)
     reply = []
     for spot in range(8):
-        block = merged(pos_ref, gathered_ref, pl.ds(48 + 16 * spot, 16))
+        block = merged(gathered_ref, pl.ds(48 + 16 * spot, 16))
         reply.append((block, pltpu.roll(block, count // 2, 1)))
     reply = [pair[0] for pair in reply] + [pair[1] for pair in reply]
     change = [block * sent for block in reply]
@@ -306,7 +335,7 @@
     coupled = coupling(traces, none, none, neighbour_ref, orient_ref, lift_ref)
     rest_ref[...] = rhs_ref[...] - (apply_blocks(diag_ref, new_ref[...]) - coupled)
     rim_ref[...] = pack_rim(traces)
-    mine = gathered_ref[pos_ref[0], pl.ds(32, 16)].astype(F32)
+    mine = gathered_ref[pos, pl.ds(32, 16)].astype(F32)
     target = jnp.where(
         lanes((1, count)) >= count - count // 4, target_of(known, staying, capacity), -1
     )
@@ -314,7 +343,7 @@
     facts = jnp.where(place == 0, orient, target)
     facts = jnp.where(place == 2, target_of(mine, staying, capacity), facts)
     facts = jnp.where(place == 3, orient_ref[2:3], facts)
-    facts_ref[...] = jnp.where(place == 4, slot_ref[...], facts)
+    facts_ref[...] = jnp.where(place == 4, slot, facts)
     edge_ref[...] = lift_ref[2:4].reshape(32, NODES)
     copy.wait()
 
@@ -340,8 +369,8 @@
     return made.reshape(owners, depth, GROUP * values.shape[0])
 
 
-def send_kernel(pos_ref, rest_ref, rim_ref, facts_ref, after_ref, send_ref):
-    pos = pos_ref[0]
+def send_kernel(rest_ref, rim_ref, facts_ref, after_ref, send_ref):
+    pos = lax.axis_index("face")
     count = rest_ref.shape[1]
     edge = count // 4
     owners, slabs, depth, _ = send_ref.shape
@@ -365,7 +394,7 @@
     def _():
         group = lanes((8, count)) // edge
         rim = jnp.where(group == 0, moved_up[0:8], pltpu.roll(moved_up[8:16], edge, 1))
-        send_ref[pl.ds(pos_ref[1], 1), pl.ds(pos + 1, 1), 0:8] = rim.astype(BF16)[None, None]
+        send_ref[pl.ds(lax.axis_index("dom"), 1), pl.ds(pos + 1, 1), 0:8] = rim.astype(BF16)[None, None]
 
 
 def rank_row(owner_row, staying, owner_count):
@@ -392,12 +421,15 @@
     ]
 
 
-def first_kernel(staying, owner_count, capacity, *refs):
-    (diag_in, slot_in, owner_in, table_in, start_in, rhs_in, lift_in, neighbour_in, orient_in, precond_in) = refs[:10]
-    (send_out, local_out, partial_out, message_out) = refs[10:14]
-    (diag_ref, slot_ref, owner_ref, table_ref, start_ref, rhs_ref, lift_ref, neighbour_ref) = refs[14:22]
-    (orient_ref, precond_ref, send_ref, local_ref, partial_ref, message_ref) = refs[22:28]
-    (high_ref, low_ref, full_ref, part_sem, sem, out_sem) = refs[28:]
+def galerkin_kernel(
+    staying, owner_count, capacity,
+    diag_in, slot_in, owner_in, table_in, start_in, rhs_in, lift_in, neighbour_in, orient_in,
+    precond_in,
+    send_out, local_out, pack_out,
+    diag_ref, slot_ref, owner_ref, table_ref, lift_ref, neighbour_ref, orient_ref,
+    send_ref, local_ref, pack_ref,
+    high_ref, low_ref, full_ref, part_sem, sem, out_sem,
+):
     line = restrict_line()
     count = diag_ref.shape[2]
     chunk = 16
@@ -407,15 +439,18 @@
         return pltpu.make_async_copy(diag_in.at[:, at], diag_ref.at[:, at], part_sem.at[part])
 
     pairs = [
-        (slot_in, slot_ref), (owner_in, owner_ref), (table_in, table_ref), (start_in, start_ref),
-        (rhs_in, rhs_ref), (lift_in, lift_ref), (neighbour_in, neighbour_ref), (orient_in, orient_ref),
-        (precond_in, precond_ref),
+        (slot_in, slot_ref), (owner_in, owner_ref), (table_in, table_ref),
+        (start_in, pack_ref.at[START : START + NODES]), (rhs_in, pack_ref.at[RHS : RHS + NODES]),
+        (lift_in, lift_ref), (neighbour_in, neighbour_ref), (orient_in, orient_ref),
     ]
     copies = [pltpu.make_async_copy(src, dst, sem.at[i]) for i, (src, dst) in enumerate(pairs)]
     for part in range(NODES // chunk):
         part_copy(part).start()
     for copy in copies:
         copy.start()
+    high_ref[COARSE] = jnp.zeros((NODES, count), BF16)
+    low_ref[COARSE] = jnp.zeros((NODES, count), BF16)
+    full_ref[...] = jnp.zeros(full_ref.shape, F32)
 
     def step(part, carry):
         part_copy(part).wait()
@@ -437,41 +472,58 @@
         return carry
 
     lax.fori_loop(0, NODES // chunk, step, 0)
-    high_ref[COARSE] = jnp.zeros((NODES, count), BF16)
-    low_ref[COARSE] = jnp.zeros((NODES, count), BF16)
-    full_ref[...] = jnp.zeros(full_ref.shape, F32)
-    for copy in copies[:3]:
+    for copy in copies:
         copy.wait()
+    pack_ref[LIFT : LIFT + FACES * 16, 0:NODES] = lift_ref[...].reshape(FACES * 16, NODES)
+    pack_ref[NEIGHBOUR : NEIGHBOUR + FACES] = neighbour_ref[...].astype(F32)
+    pack_ref[ORIENT : ORIENT + FACES] = orient_ref[...].astype(F32)
+    pack_ref[OWNER : OWNER + 1] = owner_ref[...].astype(F32)
+    pack_ref[SLOT : SLOT + 1] = slot_ref[...].astype(F32)
+    pack_copy = pltpu.make_async_copy(pack_ref, pack_out, out_sem.at[2])
+    pack_copy.start()
     padded = table_ref.shape[0] // 2
     table = table_ref[...]
+    step_rows = GROUP * COARSE
+    cut = SPLIT * COARSE
     for part in range(high_ref.shape[0] // GROUP):
         high = high_ref[GROUP * part : GROUP * part + GROUP].reshape(GROUP * NODES, count)
         low = low_ref[GROUP * part : GROUP * part + GROUP].reshape(GROUP * NODES, count)
         both = dot(table, high, NN)
         made = both[:padded] + both[padded:] + dot(table[:padded], low, NN)
-        full_ref[GROUP * COARSE * part : GROUP * COARSE * part + padded] = made
-    full_ref[COARSE * COARSE : COARSE * COARSE + 1] = (slot_ref[...] + 1).astype(F32)
+        first, last = step_rows * part, min(step_rows * part + step_rows, COARSE * COARSE)
+        if first < cut:
+            end = min(cut, last)
+            full_ref[first:end] = made[: end - first]
+        if last > cut:
+            begin = max(cut, first)
+            to = 5 * 128 + begin - cut
+            full_ref[to : to + last - begin] = made[begin - first : last - first]
+    slot = (slot_ref[...] + 1).astype(F32)
+    full_ref[5 * 128 - 1 : 5 * 128] = slot
+    full_ref[6 * 128 - 1 : 6 * 128] = slot
     local = full_ref[...].astype(BF16)
     local_ref[...] = local
+    local_copy = pltpu.make_async_copy(local_ref, local_out, out_sem.at[0])
+    local_copy.start()
     owner = owner_ref[...]
     rank = rank_row(owner, staying, owner_count)
     target = jnp.where(lanes(owner.shape) >= staying, owner * capacity + rank, -1)
-    shape = (owner_count * capacity, count)
-    send_ref[...] = dot(one_hot(rows(shape) == target), local, NT).astype(BF16)
-    pairs = [(send_ref, send_out), (local_ref, local_out), (partial_ref, partial_out), (message_ref, message_out)]
-    out = [pltpu.make_async_copy(src, dst, out_sem.at[i]) for i, (src, dst) in enumerate(pairs)]
-    out[0].start()
-    out[1].start()
-    for copy in copies[3:8]:
-        copy.wait()
-    first_half(
-        start_ref, rhs_ref, diag_ref, precond_ref, lift_ref, neighbour_ref, orient_ref, (owner, rank),
-        partial_ref, message_ref, copies[8].wait,
-    )
-    out[2].start()
-    out[3].start()
-    for copy in out:
-        copy.wait()
+    twice = jnp.concatenate([target, target], 1)
+    shape = (2 * capacity, 2 * count)
+    upper = (rows(shape) >= capacity).astype(jnp.int32)
+    place = rows(shape) - capacity * upper
+    place = jnp.where(upper == (lanes(shape) >= count).astype(jnp.int32), place, -2 * owner_count * capacity)
+    hits = jnp.concatenate([one_hot(place + capacity * o == twice) for o in range(owner_count)], 0)
+    for pair in range(3):
+        wide = jnp.concatenate([local[256 * pair : 256 * pair + 128], local[256 * pair + 128 : 256 * pair + 256]], 1)
+        made = dot(hits, wide, NT)
+        made = made.reshape(owner_count, 2 * capacity, 128).astype(BF16)
+        send_ref[:, 2 * capacity * pair : 2 * capacity * pair + 2 * capacity] = made
+    send_copy = pltpu.make_async_copy(send_ref, send_out, out_sem.at[1])
+    send_copy.start()
+    pack_copy.wait()
+    local_copy.wait()
+    send_copy.wait()
 
 
 def block_sum(made, height, width):
@@ -483,20 +535,41 @@
 
 def operator_kernel(staying, got_ref, local_ref, facts_ref, op_ref, hits_ref):
     aggregates = op_ref.shape[0]
-    count = local_ref.shape[1]
-    owners, capacity, _ = got_ref.shape
-    got = got_ref[...].reshape(owners * capacity, got_ref.shape[2])
-    ids = got[:, COARSE * COARSE : COARSE * COARSE + 1].astype(F32)
-    shape = (ids.shape[0], aggregates)
-    hits = jnp.where(ids == (lanes(shape) + 1).astype(F32), 1.0, 0.0)
+    owners, size, count = got_ref.shape
+    both = size // 3
+    capacity = both // 2
+    ids = got_ref[:, 2 * both : size].astype(F32).reshape(owners * both, count)[:, count - 1 : count]
+    shape = (owners * both, 2 * aggregates)
+    column = lanes(shape)
+    column = jnp.where(column >= aggregates, column - aggregates, column)
+    hits = jnp.where(ids == (column + 1).astype(F32), 1.0, 0.0).reshape(owners, both, 2 * aggregates)
+    shape = (owners, both, 2 * aggregates)
+    upper = lax.broadcasted_iota(jnp.int32, shape, 1) >= capacity
+    right = lax.broadcasted_iota(jnp.int32, shape, 2) >= aggregates
+    paired = jnp.where(upper == right, hits, 0.0).reshape(owners * both, 2 * aggregates).astype(BF16)
     stay = stay_hits(facts_ref, staying, aggregates)
-    total = dot(hits.astype(BF16), got, TN) + dot(stay, local_ref[...], NT)
-    op_ref[...] = total[:, : COARSE * COARSE]
-    depth = capacity // GROUP
-    hits = hits.reshape(owners, GROUP, depth, aggregates)
-    hits_ref[...] = jnp.concatenate(
-        [hits[:, g].reshape(owners * depth, aggregates) for g in range(GROUP)], 1
-    ).astype(BF16)
+    out = []
+    for pair in range(3):
+        block = got_ref[:, both * pair : both * pair + both].astype(F32).reshape(owners * both, count).astype(BF16)
+        total = dot(paired, block, TN)
+        for side in range(2):
+            at = 128 * (2 * pair + side)
+            out.append(
+                total[aggregates * side : aggregates * side + aggregates] + dot(stay, local_ref[at : at + 128], NT)
+            )
+    cut = SPLIT * COARSE
+    for block in range(4):
+        op_ref[:, 128 * block : 128 * block + 128] = out[block]
+    op_ref[:, 512:cut] = out[4][:, : cut - 512]
+    op_ref[:, cut:] = out[5][:, : COARSE * COARSE - cut]
+    depth = hits_ref.shape[0] // owners
+    parts = []
+    for g in range(GROUP):
+        part = hits[:, depth * g : depth * g + depth] if depth * g + depth <= both else None
+        if part is None:
+            part = jnp.zeros((owners, depth, 2 * aggregates), F32)
+        parts.append(part.reshape(owners * depth, 2 * aggregates)[:, :aggregates])
+    hits_ref[...] = jnp.concatenate(parts, 1).astype(BF16)
 
 
 def stay_hits(facts_ref, staying, aggregates):
@@ -505,8 +578,8 @@
     return one_hot((rows(shape) == slot) & (lanes(shape) < staying))
 
 
-def last_kernel(staying, pos_ref, got_ref, hits_ref, rest_ref, facts_ref, edge_ref, out_ref):
-    pos = pos_ref[0]
+def last_kernel(staying, got_ref, hits_ref, rest_ref, facts_ref, edge_ref, out_ref):
+    pos = lax.axis_index("face")
     owners, slabs, depth, width = got_ref.shape
     aggregates = out_ref.shape[1]
     count = rest_ref.shape[1]
@@ -518,7 +591,7 @@
     main = block_sum(dot(main, hits, TN), width // GROUP, aggregates)
     side = block_sum(dot(side, hits, TN), width // GROUP, aggregates)[0:16]
 
-    rim = got_ref[pl.ds(pos_ref[1], 1), pl.ds(jnp.maximum(pos - 1, 0), 1), 0:8]
+    rim = got_ref[pl.ds(lax.axis_index("dom"), 1), pl.ds(jnp.maximum(pos - 1, 0), 1), 0:8]
     rim = jnp.where(pos > 0, rim.astype(F32).reshape(8, width), 0.0)
     rim = jnp.concatenate([rim, pltpu.roll(rim, count - edge, 1)], 0)
     rim = jnp.where(lanes(rim.shape) < edge, turn(rim, facts_ref[3:4]), 0.0)
@@ -572,46 +645,51 @@
     movers = count - staying
     capacity = 2 * ((movers + owner_count - 2) // (owner_count - 1))
     depth = ceil_to(-(-max(capacity, count // 4) // GROUP), 8)
-    capacity = GROUP * depth
-    total = owner_count * capacity
-    entries = ceil_to(COARSE * COARSE + 1, 128)
+    places = GROUP * depth
+    capacity = ceil_to(capacity, 4)
+    chunk = 6 * capacity
+    entries = 6 * 128
     groups = -(-COARSE // GROUP)
-    pos = jnp.stack([lax.axis_index("face"), lax.axis_index("dom")]).astype(jnp.int32)
     owner = owner.reshape(1, count)
     slot = slot.reshape(1, count)
     table = jnp.asarray(block_table(restrict_table(), GROUP, 16))
 
     args = [diag_block, slot, owner, table, start, rhs, lift, neighbour, orient, precond]
     outs = [
-        struct((total, entries), BF16),
+        struct((owner_count, chunk, 128), BF16),
         struct((entries, count), BF16),
-        struct((NODES, count), F32),
-        struct((176, count), BF16),
+        struct((PACKED, count), F32),
     ]
-    op_send, local_op, partial, message = call(
-        lambda *refs: first_kernel(staying, owner_count, capacity, *refs),
+    held = [each for each in args if each is not start and each is not rhs and each is not precond]
+    op_send, local_op, pack = call(
+        lambda *refs: galerkin_kernel(staying, owner_count, capacity, *refs),
         outs,
         args,
         [pl.ANY] * len(args),
         [pl.ANY] * len(outs),
-        scratch=[pltpu.VMEM(each.shape, each.dtype) for each in args + outs]
+        scratch=[pltpu.VMEM(each.shape, each.dtype) for each in held + outs]
         + [
             pltpu.VMEM((groups * GROUP, NODES, count), BF16),
             pltpu.VMEM((groups * GROUP, NODES, count), BF16),
             pltpu.VMEM((entries, count), F32),
             pltpu.SemaphoreType.DMA((NODES // 16,)),
-            pltpu.SemaphoreType.DMA((9,)),
-            pltpu.SemaphoreType.DMA((4,)),
+            pltpu.SemaphoreType.DMA((8,)),
+            pltpu.SemaphoreType.DMA((3,)),
         ],
         flops=200_000_000,
         limit=FIRST_LIMIT,
     )
-    op_got = lax.all_to_all(
-        op_send.reshape(owner_count, capacity, entries), "dom", split_axis=0, concat_axis=0, tiled=True
+    op_got = lax.all_to_all(op_send, "dom", split_axis=0, concat_axis=0, tiled=True)
+    message, partial = call(
+        lambda *refs: smooth_kernel(staying, owner_count, *refs),
+        [struct((176, count), BF16), struct((NODES, count), F32)],
+        [diag_block, precond, pack],
+        [pltpu.VMEM] * 3,
+        flops=100_000_000,
     )
     gathered = lax.all_gather(message, "face")
     sol, rest, rim, facts, edge = call(
-        lambda *refs: middle_kernel(staying, capacity, *refs),
+        lambda *refs: middle_kernel(staying, places, *refs),
         [
             struct((NODES, count), F32),
             struct((NODES, count), F32),
@@ -619,8 +697,8 @@
             struct((8, count), jnp.int32),
             struct((32, NODES), F32),
         ],
-        [pos, gathered, start, partial, rhs, diag_block, precond, lift, neighbour, orient, slot],
-        [pltpu.SMEM] + [pltpu.VMEM] * 10,
+        [gathered, diag_block, precond, pack, partial],
+        [pltpu.VMEM] * 5,
         [pl.ANY] + [pltpu.VMEM] * 4,
         scratch=[
             pltpu.VMEM((NODES, count), F32),
@@ -632,8 +710,8 @@
     (send,) = call(
         send_kernel,
         [struct((owner_count, slabs, depth, 128), BF16)],
-        [pos, rest, rim, facts, op_got],
-        [pltpu.SMEM] + [pltpu.VMEM] * 3 + [pl.ANY],
+        [rest, rim, facts, op_got],
+        [pltpu.VMEM] * 3 + [pl.ANY],
         flops=100_000_000,
     )
     got = lax.all_to_all(
@@ -652,8 +730,8 @@
     (coarse_rhs,) = call(
         lambda *refs: last_kernel(staying, *refs),
         [struct((COARSE, aggregates), F32)],
-        [pos, got, hits, rest, facts, edge],
-        [pltpu.SMEM] + [pltpu.VMEM] * 5,
+        [got, hits, rest, facts, edge],
+        [pltpu.VMEM] * 5,
         flops=100_000_000,
     )
     return (sol, coarse_op.T, coarse_rhs)

time: 38.7 us -> 36.1 us (0.933)
  Pallas kernels: 10.7 us -> 9.35 us
  local copies, waits for them, and re-layouts: 0.66 us -> 0.02 us
  waiting for transfers between devices: 9.4 us -> 8.95 us
    pallas_call x5 -> x6, Pallas kernels: 10.7 us -> 9.35 us  [call(): pl.pallas_call(kernel, out_shape=tuple(outs), in_specs=[pl.BlockSpec(memo...]
    unnamed x22 -> x8, local copies, waits for them, and re-layouts: 0.66 us -> 0.02 us
  transfers between devices with their start and end apart: 2 -> 2, of which waited for: 2 -> 2; matrix products, arithmetic and copies ran while one was open for 0% -> 0% of each run, Pallas kernels for 8% -> 10%
where the time goes in v4:
time: 36.1 us; the launch traced here: 35.8 us
  starting transfers between devices  11.2 us (31%)
  Pallas kernels  9.35 us (26%)
  waiting for transfers between devices  8.95 us (25%)
  blocking collectives  5.56 us (15%)
  between operations  0.72 us (2%)
    pallas_call x6, Pallas kernels, call(): pl.pallas_call(kernel, out_shape=tuple(outs), in_specs=[pl.BlockSpec(memo...  9.35 us
    all_to_all x1, starting transfers between devices, per_device(): lax.all_to_all(op_send, 'dom', split_axis=0, concat_axis=0, tiled=True)  7.4 us
    all_to_all x1, waiting for transfers between devices, per_device(): lax.all_to_all(send.reshape(owner_count * slabs, depth, 128), ('dom', 'fa...  6.21 us
    all_gather x1, blocking collectives, per_device(): gathered = lax.all_gather(message, 'face')  5.56 us
    all_to_all x1, starting transfers between devices, per_device(): lax.all_to_all(send.reshape(owner_count * slabs, depth, 128), ('dom', 'fa...  3.79 us
    all_to_all x1, waiting for transfers between devices, per_device(): lax.all_to_all(op_send, 'dom', split_axis=0, concat_axis=0, tiled=True)  2.74 us
  transfers between devices with their start and end apart: 2, of which 2 were waited for; matrix products, arithmetic and copies ran while one was open for 0% of the time, Pallas kernels for 10%

profile of v4, /device:TPU:0, one launch (start us, length us, event | category | flops | bytes accessed | tf_op | source)
XLA Modules:
  0.0 35.8 jit_solution(13523247026579274941)
XLA Ops:
  0.6 0.0 copy-start
  0.6 0.0 copy-start.1
  0.7 3.6 %shard_map.121 = (bf16[8,168,128]{2,1,0:T(8,128)(2,1)}, bf16[768,128]{1,0:T(8,128)(2,1)}, f32[248,128]{1,0:T(8,128)}) custom-call(bf16[64,64,128]{2,1,0:T(8,128)(2,1)} %refs_1_.3, s32[1,128]{1,0:T(1,128)} %bitcast.8, s32[1,128]{1,0:T(1,128)} %bitcast.9, bf16[224,256]{1,0:T(8,128)(2,1)} %constant.2.clone.refs_3_, f32[64,128]{1,0:T(8,128)} %refs_4_.1, ...), custom_call_target="tpu_custom_call" | custom-call | flops 200000000 | bytes 2976768 | tf_op jit(solution)/shard_map/pallas_call | solution.py:609
  4.3 0.0 copy-start.2
  4.3 7.4 %all-to-all-start = ((bf16[8,168,128]{2,1,0:T(8,128)(2,1)}), bf16[8,168,128]{2,1,0:T(8,128)(2,1)S(1)}, u32[]{:S(2)}, u32[]{:S(2)}) async-start(bf16[8,168,128]{2,1,0:T(8,128)(2,1)} %get-tuple-element.19), calls=%async_computation | async-start | bytes 688128 | tf_op jit(solution)/shard_map/all_to_all | solution.py:682
  11.7 0.0 copy-done
  11.7 0.0 copy-done.1
  11.7 0.0 copy-done.2
  11.7 0.7 %shard_map.122 = (bf16[176,128]{1,0:T(8,128)(2,1)S(1)}, f32[64,128]{1,0:T(8,128)S(1)}) custom-call(bf16[64,64,128]{2,1,0:T(8,128)(2,1)S(1)} %copy-done, bf16[64,64,128]{2,1,0:T(8,128)(2,1)S(1)} %copy-done.1, f32[248,128]{1,0:T(8,128)S(1)} %copy-done.2), custom_call_target="tpu_custom_call" | custom-call | flops 100000000 | bytes 2301952 | tf_op jit(solution)/shard_map/pallas_call | solution.py:609
  12.4 5.6 %all-gather = bf16[704,128]{1,0:T(8,128)(2,1)S(1)} all-gather(bf16[176,128]{1,0:T(8,128)(2,1)S(1)} %get-tuple-element.16), channel_id=2, replica_groups=mesh['dom'=8,'face'=4] {'face'}, dimensions={0}, use_global_device_ids=true | all-gather | bytes 225280 | tf_op jit(solution)/shard_map/all_gather | solution.py:690
  18.0 1.6 %shard_map.123 = (f32[64,128]{1,0:T(8,128)}, f32[64,128]{1,0:T(8,128)S(1)}, f32[16,128]{1,0:T(8,128)S(1)}, s32[8,128]{1,0:T(8,128)S(1)}, f32[32,64]{1,0:T(8,128)S(1)}) custom-call(bf16[4,176,128]{2,1,0:T(8,128)(2,1)S(1)} %bitcast.6, bf16[64,64,128]{2,1,0:T(8,128)(2,1)S(1)} %copy-done, bf16[64,64,128]{2,1,0:T(8,128)(2,1)S(1)} %copy-done.1, ...), custom_call_target="tpu_custom_call" | custom-call | flops 200000000 | bytes 2523136 | tf_op jit(solution)/shard_map/pallas_call | solution.py:609
  19.6 2.7 %all-to-all-done.refs_0_.after_ref = bf16[8,168,128]{2,1,0:T(8,128)(2,1)S(1)} async-done(((bf16[8,168,128]{2,1,0:T(8,128)(2,1)}), bf16[8,168,128]{2,1,0:T(8,128)(2,1)S(1)}, u32[]{:S(2)}, u32[]{:S(2)}) %all-to-all-start) | async-done | bytes 344096 | tf_op jit(solution)/shard_map/all_to_all | solution.py:682
  22.4 0.0 copy-start.3
  22.4 1.0 %shard_map.125 = bf16[8,4,8,128]{3,2,1,0:T(8,128)(2,1)} custom-call(f32[64,128]{1,0:T(8,128)S(1)} %get-tuple-element.23.rest_ref.refs_2_, f32[16,128]{1,0:T(8,128)S(1)} %get-tuple-element.24.rim_ref, s32[8,128]{1,0:T(8,128)S(1)} %get-tuple-element.21.refs_2_.facts_ref.refs_3_, bf16[8,168,128]{2,1,0:T(8,128)(2,1)S(1)} %all-to-all-done.refs_0_.after_ref), custom_call_target="tpu_custom_call" | custom-call | flops 100000000 | bytes 454656 | tf_op jit(solution)/shard_map/pallas_call | solution.py:609
  23.4 3.8 %all-to-all-start.1 = ((bf16[32,8,128]{2,1,0:T(8,128)(2,1)}), bf16[32,8,128]{2,1,0:T(8,128)(2,1)S(1)}, u32[]{:S(2)}, u32[]{:S(2)}) async-start(bf16[32,8,128]{2,1,0:T(8,128)(2,1)} %bitcast.4), calls=%async_computation.1 | async-start | bytes 131072 | tf_op jit(solution)/shard_map/all_to_all | solution.py:717
  27.2 0.0 copy-done.3
  27.2 1.2 %shard_map.124 = (f32[64,729]{1,0:T(8,128)}, bf16[64,256]{1,0:T(8,128)(2,1)S(1)}) custom-call(bf16[8,168,128]{2,1,0:T(8,128)(2,1)S(1)} %all-to-all-done.refs_0_.after_ref, bf16[768,128]{1,0:T(8,128)(2,1)S(1)} %copy-done.3, s32[8,128]{1,0:T(8,128)S(1)} %get-tuple-element.21.refs_2_.facts_ref.refs_3_), custom_call_target="tpu_custom_call" | custom-call | flops 100000000 | bytes 764160 | tf_op jit(solution)/shard_map/pallas_call | solution.py:609
  28.4 6.2 %all-to-all-done.1 = bf16[32,8,128]{2,1,0:T(8,128)(2,1)S(1)} async-done(((bf16[32,8,128]{2,1,0:T(8,128)(2,1)}), bf16[32,8,128]{2,1,0:T(8,128)(2,1)S(1)}, u32[]{:S(2)}, u32[]{:S(2)}) %all-to-all-start.1) | async-done | bytes 65568 | tf_op jit(solution)/shard_map/all_to_all | solution.py:717
  34.6 1.2 %shard_map.126 = f32[27,64]{1,0:T(8,128)} custom-call(bf16[8,4,8,128]{3,2,1,0:T(8,128)(2,1)S(1)} %bitcast.7, bf16[64,256]{1,0:T(8,128)(2,1)S(1)} %get-tuple-element.25.refs_1_, f32[64,128]{1,0:T(8,128)S(1)} %get-tuple-element.23.rest_ref.refs_2_, s32[8,128]{1,0:T(8,128)S(1)} %get-tuple-element.21.refs_2_.facts_ref.refs_3_, ...), custom_call_target="tpu_custom_call" | custom-call | flops 100000000 | bytes 150272 | tf_op jit(solution)/shard_map/pallas_call | solution.py:609
Async XLA Ops:
  0.6 11.1 %copy-start = (bf16[64,64,128]{2,1,0:T(8,128)(2,1)S(1)}, bf16[64,64,128]{2,1,0:T(8,128)(2,1)}, u32[]{:S(2)}) copy-start(bf16[64,64,128]{2,1,0:T(8,128)(2,1)} %refs_1_.3) | copy-start | bytes 3145732
  0.6 11.0 %copy-start.1 = (bf16[64,64,128]{2,1,0:T(8,128)(2,1)S(1)}, bf16[64,64,128]{2,1,0:T(8,128)(2,1)}, u32[]{:S(2)}) copy-start(bf16[64,64,128]{2,1,0:T(8,128)(2,1)} %refs_2_.1) | copy-start | bytes 3145732
  4.3 7.4 %copy-start.2 = (f32[248,128]{1,0:T(8,128)S(1)}, f32[248,128]{1,0:T(8,128)}, u32[]{:S(2)}) copy-start(f32[248,128]{1,0:T(8,128)} %get-tuple-element.15.refs_2_.refs_3_) | copy-start | bytes 380932
  4.3 18.1 %all-to-all-start = ((bf16[8,168,128]{2,1,0:T(8,128)(2,1)}), bf16[8,168,128]{2,1,0:T(8,128)(2,1)S(1)}, u32[]{:S(2)}, u32[]{:S(2)}) async-start(bf16[8,168,128]{2,1,0:T(8,128)(2,1)} %get-tuple-element.19), calls=%async_computation | async-start | bytes 688128 | tf_op jit(solution)/shard_map/all_to_all | solution.py:682
  22.4 4.8 %copy-start.3 = (bf16[768,128]{1,0:T(8,128)(2,1)S(1)}, bf16[768,128]{1,0:T(8,128)(2,1)}, u32[]{:S(2)}) copy-start(bf16[768,128]{1,0:T(8,128)(2,1)} %get-tuple-element.20.refs_1_) | copy-start | bytes 589828
  23.4 11.2 %all-to-all-start.1 = ((bf16[32,8,128]{2,1,0:T(8,128)(2,1)}), bf16[32,8,128]{2,1,0:T(8,128)(2,1)S(1)}, u32[]{:S(2)}, u32[]{:S(2)}) async-start(bf16[32,8,128]{2,1,0:T(8,128)(2,1)} %bitcast.4), calls=%async_computation.1 | async-start | bytes 131072 | tf_op jit(solution)/shard_map/all_to_all | solution.py:717

commit v5 on v4

--- a/solution.py
+++ b/solution.py
@@ -59,14 +59,12 @@
     return lax.dot_general(left, right, dims, preferred_element_type=F32)
 
 
-def dot_split(left, right, dims):
-    left_high, left_low = left
+def dot_split(left, right):
+    left_high, left_low = halves(left)
     right_high, right_low = right
-    return (
-        dot(left_high, right_high, dims)
-        + dot(left_low, right_high, dims)
-        + dot(left_high, right_low, dims)
-    )
+    size = left.shape[0]
+    both = dot(jnp.concatenate([left_high, left_low], 0), right_high, NN)
+    return both[:size] + both[size:] + dot(left_high, right_low, NN)
 
 
 def small_table():
@@ -164,7 +162,7 @@
     return jnp.where(lanes(shape) < shape[1] // 2, traces[2], traces[3])
 
 
-def coupling(traces, below, above, neighbour_ref, orient_ref, lift_ref):
+def coupling(traces, below, above, neighbour_ref, orient_ref, lift):
     count = below.shape[1]
     edge = count // 4
     turned = []
@@ -175,9 +173,8 @@
         if face == 3:
             values = jnp.where(lanes(values.shape) >= count - edge, above, values)
         turned.append(turn(values, orient_ref[face : face + 1]))
-    turned = jnp.concatenate(turned, 0)
-    lift = lift_ref[...].reshape(FACES * 16, NODES)
-    return dot_split(halves(lift), halves(turned), TN)
+    turned = jnp.concatenate(turned + [jnp.zeros((count - FACES * 16, count), F32)], 0)
+    return dot_split(lift, halves(turned))
 
 
 def edge_mask(shape):
@@ -192,11 +189,11 @@
     return jnp.where(lanes(shape) < shape[1] // 2, low, high)
 
 
-def response(precond_ref, lift_ref):
+def response(precond_ref, edge):
     count = precond_ref.shape[2]
     parts = []
-    for face in (2, 3):
-        parts.extend(halves(lift_ref[face]))
+    for lift in (edge[0:16], edge[16:32]):
+        parts.extend(halves(lift))
     stack = jnp.concatenate(parts, 0)
     shape = (NODES, count)
     out = []
@@ -210,19 +207,21 @@
     return out
 
 
-def halo_lift(below, above, orient_ref, lift_ref):
+def halo_lift(below, above, orient_ref, lift):
     shape = below.shape
     edge = shape[1] // 4
     low = jnp.where(lanes(shape) < edge, turn(below, orient_ref[2:3]), 0.0)
     high = jnp.where(lanes(shape) >= shape[1] - edge, turn(above, orient_ref[3:4]), 0.0)
-    lift = lift_ref[2:4].reshape(32, NODES)
-    return dot_split(halves(lift), halves(jnp.concatenate([low, high], 0)), TN)
+    none = jnp.zeros((32, shape[1]), F32)
+    rest = jnp.zeros((shape[1] - 64, shape[1]), F32)
+    return dot_split(lift, halves(jnp.concatenate([none, low, high, rest], 0)))
 
 
 START = 0
 RHS = NODES
 LIFT = 2 * NODES
-NEIGHBOUR = LIFT + FACES * 16
+EDGE = LIFT + NODES
+NEIGHBOUR = EDGE + 32
 ORIENT = NEIGHBOUR + 8
 OWNER = ORIENT + 8
 SLOT = OWNER + 1
@@ -233,7 +232,8 @@
     def __init__(self, ref):
         self.start = ref.at[START : START + NODES]
         self.rhs = ref.at[RHS : RHS + NODES]
-        self.lift = ref[LIFT : LIFT + FACES * 16, 0:NODES].reshape(FACES, 16, NODES)
+        self.lift = ref[LIFT : LIFT + NODES]
+        self.edge = ref[EDGE : EDGE + 32, 0:NODES]
         self.neighbour = ref[NEIGHBOUR : NEIGHBOUR + FACES].astype(jnp.int32)
         self.orient = ref[ORIENT : ORIENT + FACES].astype(jnp.int32)
         self.owner = ref[OWNER : OWNER + 1].astype(jnp.int32)
@@ -248,15 +248,15 @@
     count = diag_ref.shape[2]
     packed = Packed(pack_ref)
     start_ref, rhs_ref = packed.start, packed.rhs
-    lift_ref, neighbour_ref, orient_ref = packed.lift, packed.neighbour, packed.orient
+    lift, neighbour_ref, orient_ref = packed.lift, packed.neighbour, packed.orient
     traces = face_traces(start_ref)
     shape = traces[2].shape
     none = jnp.zeros(shape, F32)
-    coupled = coupling(traces, none, none, neighbour_ref, orient_ref, lift_ref)
+    coupled = coupling(traces, none, none, neighbour_ref, orient_ref, lift)
     resid = rhs_ref[...] - (apply_blocks(diag_ref, start_ref[...]) - coupled)
     partial_ref[...] = start_ref[...] + apply_blocks(precond_ref, resid)
     direct = edge_mask(shape)
-    reply = response(precond_ref, lift_ref)
+    reply = response(precond_ref, packed.edge)
     for spot in range(8):
         message_ref[48 + 16 * spot : 64 + 16 * spot] = jnp.where(
             direct, reply[spot], pltpu.roll(reply[spot + 8], count // 2, 1)
@@ -297,14 +297,14 @@
 def middle_kernel(
     staying, capacity,
     gathered_ref, diag_ref, precond_ref, pack_ref, partial_ref,
-    out_ref, rest_ref, rim_ref, facts_ref, edge_ref, sol_ref, new_ref, sem,
+    new_ref, rest_ref, rim_ref, facts_ref, edge_ref, sol_ref,
 ):
     count = diag_ref.shape[2]
     shape = (16, count)
     pos = lax.axis_index("face")
     packed = Packed(pack_ref)
     rhs_ref, slot = packed.rhs, packed.slot
-    lift_ref, neighbour_ref, orient_ref = packed.lift, packed.neighbour, packed.orient
+    lift, neighbour_ref, orient_ref = packed.lift, packed.neighbour, packed.orient
     head = merged(gathered_ref, pl.ds(0, 16)) + merged(gathered_ref, pl.ds(16, 16))
     known = merged(gathered_ref, pl.ds(32, 16))
     orient = known[0:1].astype(jnp.int32)
@@ -312,7 +312,7 @@
     from_high, from_low = aside(own)
     sent = turn(both_halves(shape, from_high, from_low), orient)
     below, above = aside(head)
-    delta = halo_lift(below, above, orient_ref, lift_ref)
+    delta = halo_lift(below, above, orient_ref, lift)
     sol_ref[...] = partial_ref[...] + apply_blocks(precond_ref, delta)
     later = pltpu.roll(head, count // 2, 1)
     reply = []
@@ -325,14 +325,12 @@
     change = jnp.concatenate([fold(change[:8]), fold(change[8:])], 0)
     below, above = aside(later + change)
     traces = face_traces(sol_ref)
-    coupled = coupling(traces, below, above, neighbour_ref, orient_ref, lift_ref)
+    coupled = coupling(traces, below, above, neighbour_ref, orient_ref, lift)
     resid = rhs_ref[...] - (apply_blocks(diag_ref, sol_ref[...]) - coupled)
     new_ref[...] = sol_ref[...] + apply_blocks(precond_ref, resid)
-    copy = pltpu.make_async_copy(new_ref, out_ref, sem)
-    copy.start()
     traces = face_traces(new_ref)
     none = jnp.zeros(shape, F32)
-    coupled = coupling(traces, none, none, neighbour_ref, orient_ref, lift_ref)
+    coupled = coupling(traces, none, none, neighbour_ref, orient_ref, lift)
     rest_ref[...] = rhs_ref[...] - (apply_blocks(diag_ref, new_ref[...]) - coupled)
     rim_ref[...] = pack_rim(traces)
     mine = gathered_ref[pos, pl.ds(32, 16)].astype(F32)
@@ -344,8 +342,7 @@
     facts = jnp.where(place == 2, target_of(mine, staying, capacity), facts)
     facts = jnp.where(place == 3, orient_ref[2:3], facts)
     facts_ref[...] = jnp.where(place == 4, slot, facts)
-    edge_ref[...] = lift_ref[2:4].reshape(32, NODES)
-    copy.wait()
+    edge_ref[...] = lift
 
 
 def spread(values, copies):
@@ -377,7 +374,7 @@
     high, low = halves(rest_ref[...])
     keep = lanes(low.shape) >= count - edge
     low = jnp.where(keep, low.astype(F32), 0.0).astype(BF16)
-    made = dot_split(halves(small_table()), (high, low), NN)
+    made = dot_split(small_table(), (high, low))
     send_ref[...] = jnp.zeros(send_ref.shape, BF16)
     ours = packed_by_target(made.astype(BF16), facts_ref[2:3], owners, depth)
     send_ref[:, pl.ds(pos, 1)] = ours.astype(BF16)[:, None]
@@ -428,15 +425,16 @@
     send_out, local_out, pack_out,
     diag_ref, slot_ref, owner_ref, table_ref, lift_ref, neighbour_ref, orient_ref,
     send_ref, local_ref, pack_ref,
-    high_ref, low_ref, full_ref, part_sem, sem, out_sem,
+    full_ref, part_sem, sem, out_sem, send_sem,
 ):
     line = restrict_line()
     count = diag_ref.shape[2]
-    chunk = 16
+    chunk = 2 * GROUP
+    wide_step = 4
 
     def part_copy(part):
-        at = pl.ds(pl.multiple_of(part * chunk, chunk), chunk)
-        return pltpu.make_async_copy(diag_in.at[:, at], diag_ref.at[:, at], part_sem.at[part])
+        at = pl.ds(part * wide_step * chunk, wide_step * chunk)
+        return pltpu.make_async_copy(diag_in.at[at], diag_ref.at[at], part_sem.at[part])
 
     pairs = [
         (slot_in, slot_ref), (owner_in, owner_ref), (table_in, table_ref),
@@ -444,60 +442,48 @@
         (lift_in, lift_ref), (neighbour_in, neighbour_ref), (orient_in, orient_ref),
     ]
     copies = [pltpu.make_async_copy(src, dst, sem.at[i]) for i, (src, dst) in enumerate(pairs)]
-    for part in range(NODES // chunk):
+    for part in range(NODES // (wide_step * chunk)):
         part_copy(part).start()
     for copy in copies:
         copy.start()
-    high_ref[COARSE] = jnp.zeros((NODES, count), BF16)
-    low_ref[COARSE] = jnp.zeros((NODES, count), BF16)
-    full_ref[...] = jnp.zeros(full_ref.shape, F32)
-
-    def step(part, carry):
-        part_copy(part).wait()
-        at = pl.ds(pl.multiple_of(part * chunk, chunk), chunk)
-        planes = []
-        for i in range(4):
-            bars = []
-            for j in range(4):
-                four = [diag_ref[16 * i + 4 * j + k, at].astype(F32) for k in range(4)]
-                bars.append(contract(four, line))
-            sheet = [contract([bars[j][k] for j in range(4)], line) for k in range(3)]
-            planes.append([sheet[k][j] for j in range(3) for k in range(3)])
-        for rest in range(9):
-            made = contract([planes[i][rest] for i in range(4)], line)
-            for i in range(3):
-                high, low = halves(made[i])
-                high_ref[9 * i + rest, at] = high
-                low_ref[9 * i + rest, at] = low
-        return carry
-
-    lax.fori_loop(0, NODES // chunk, step, 0)
     for copy in copies:
         copy.wait()
-    pack_ref[LIFT : LIFT + FACES * 16, 0:NODES] = lift_ref[...].reshape(FACES * 16, NODES)
+    stacked = lift_ref[...].reshape(FACES * 16, NODES)
+    stacked = jnp.concatenate([stacked, jnp.zeros((count - FACES * 16, NODES), F32)], 0)
+    pack_ref[LIFT : LIFT + NODES] = stacked.T
+    pack_ref[EDGE : EDGE + 32, 0:NODES] = stacked[32:64]
     pack_ref[NEIGHBOUR : NEIGHBOUR + FACES] = neighbour_ref[...].astype(F32)
     pack_ref[ORIENT : ORIENT + FACES] = orient_ref[...].astype(F32)
     pack_ref[OWNER : OWNER + 1] = owner_ref[...].astype(F32)
     pack_ref[SLOT : SLOT + 1] = slot_ref[...].astype(F32)
-    pack_copy = pltpu.make_async_copy(pack_ref, pack_out, out_sem.at[2])
+    pack_copy = pltpu.make_async_copy(pack_ref, pack_out, out_sem.at[1])
     pack_copy.start()
-    padded = table_ref.shape[0] // 2
     table = table_ref[...]
-    step_rows = GROUP * COARSE
-    cut = SPLIT * COARSE
-    for part in range(high_ref.shape[0] // GROUP):
-        high = high_ref[GROUP * part : GROUP * part + GROUP].reshape(GROUP * NODES, count)
-        low = low_ref[GROUP * part : GROUP * part + GROUP].reshape(GROUP * NODES, count)
-        both = dot(table, high, NN)
-        made = both[:padded] + both[padded:] + dot(table[:padded], low, NN)
-        first, last = step_rows * part, min(step_rows * part + step_rows, COARSE * COARSE)
-        if first < cut:
-            end = min(cut, last)
-            full_ref[first:end] = made[: end - first]
-        if last > cut:
-            begin = max(cut, first)
-            to = 5 * 128 + begin - cut
-            full_ref[to : to + last - begin] = made[begin - first : last - first]
+    padded = table.shape[0] // 2
+    tall = padded // GROUP
+    planes = []
+    for i in range(4):
+        bars = []
+        for half in range(2):
+            part = 2 * i + half
+            if part % wide_step == 0:
+                part_copy(part // wide_step).wait()
+            wide = [
+                diag_ref[chunk * part + GROUP * j : chunk * part + GROUP * j + GROUP].reshape(GROUP * NODES, count)
+                for j in range(2)
+            ]
+            both = dot(table, jnp.concatenate(wide, 1), NN)
+            made = both[:padded] + both[padded:]
+            for j in range(2):
+                four = [made[tall * k : tall * k + tall, count * j : count * j + count] for k in range(4)]
+                bars.append(contract(four, line))
+        sheet = [contract([bars[j][k] for j in range(4)], line) for k in range(3)]
+        planes.append([sheet[k][j] for j in range(3) for k in range(3)])
+    made = [contract([planes[i][rest] for i in range(4)], line) for rest in range(9)]
+    for c in range(COARSE):
+        at = COARSE * c if c < SPLIT else 5 * 128 + COARSE * (c - SPLIT)
+        full_ref[at : at + tall] = made[c % 9][c // 9]
+    full_ref[5 * 128 + COARSE * (COARSE - SPLIT) :] = jnp.zeros((128 - COARSE * (COARSE - SPLIT), count), F32)
     slot = (slot_ref[...] + 1).astype(F32)
     full_ref[5 * 128 - 1 : 5 * 128] = slot
     full_ref[6 * 128 - 1 : 6 * 128] = slot
@@ -513,17 +499,26 @@
     upper = (rows(shape) >= capacity).astype(jnp.int32)
     place = rows(shape) - capacity * upper
     place = jnp.where(upper == (lanes(shape) >= count).astype(jnp.int32), place, -2 * owner_count * capacity)
-    hits = jnp.concatenate([one_hot(place + capacity * o == twice) for o in range(owner_count)], 0)
-    for pair in range(3):
-        wide = jnp.concatenate([local[256 * pair : 256 * pair + 128], local[256 * pair + 128 : 256 * pair + 256]], 1)
-        made = dot(hits, wide, NT)
-        made = made.reshape(owner_count, 2 * capacity, 128).astype(BF16)
-        send_ref[:, 2 * capacity * pair : 2 * capacity * pair + 2 * capacity] = made
-    send_copy = pltpu.make_async_copy(send_ref, send_out, out_sem.at[1])
-    send_copy.start()
+    wide = [
+        jnp.concatenate([local[256 * pair : 256 * pair + 128], local[256 * pair + 128 : 256 * pair + 256]], 1)
+        for pair in range(3)
+    ]
+    send_copies = []
+    share = max(owner_count // 2, 1)
+    for first in range(0, owner_count, share):
+        some = pl.ds(first, share)
+        hits = [one_hot(place + capacity * o == twice) for o in range(first, first + share)]
+        hits = jnp.concatenate(hits, 0)
+        for pair in range(3):
+            made = dot(hits, wide[pair], NT).reshape(share, 2 * capacity, 128).astype(BF16)
+            send_ref[some, 2 * capacity * pair : 2 * capacity * pair + 2 * capacity] = made
+        copy = pltpu.make_async_copy(send_ref.at[some], send_out.at[some], send_sem.at[first // share])
+        copy.start()
+        send_copies.append(copy)
+    for copy in send_copies:
+        copy.wait()
     pack_copy.wait()
     local_copy.wait()
-    send_copy.wait()
 
 
 def block_sum(made, height, width):
@@ -533,7 +528,7 @@
     return total
 
 
-def operator_kernel(staying, got_ref, local_ref, facts_ref, op_ref, hits_ref):
+def sum_operators(staying, got_ref, local_ref, facts_ref, op_ref, depth):
     aggregates = op_ref.shape[0]
     owners, size, count = got_ref.shape
     both = size // 3
@@ -562,14 +557,13 @@
         op_ref[:, 128 * block : 128 * block + 128] = out[block]
     op_ref[:, 512:cut] = out[4][:, : cut - 512]
     op_ref[:, cut:] = out[5][:, : COARSE * COARSE - cut]
-    depth = hits_ref.shape[0] // owners
     parts = []
     for g in range(GROUP):
         part = hits[:, depth * g : depth * g + depth] if depth * g + depth <= both else None
         if part is None:
             part = jnp.zeros((owners, depth, 2 * aggregates), F32)
         parts.append(part.reshape(owners * depth, 2 * aggregates)[:, :aggregates])
-    hits_ref[...] = jnp.concatenate(parts, 1).astype(BF16)
+    return jnp.concatenate(parts, 1).astype(BF16)
 
 
 def stay_hits(facts_ref, staying, aggregates):
@@ -578,13 +572,22 @@
     return one_hot((rows(shape) == slot) & (lanes(shape) < staying))
 
 
-def last_kernel(staying, got_ref, hits_ref, rest_ref, facts_ref, edge_ref, out_ref):
+def last_kernel(
+    staying,
+    got_ref, op_got_ref, local_ref, rest_ref, facts_ref, edge_ref, sol_ref,
+    sol_out, op_out, rhs_out,
+    op_ref, out_ref, sem,
+):
+    sol_copy = pltpu.make_async_copy(sol_ref, sol_out, sem.at[0])
+    sol_copy.start()
+    hits = sum_operators(staying, op_got_ref, local_ref, facts_ref, op_ref, got_ref.shape[2])
+    op_copy = pltpu.make_async_copy(op_ref, op_out, sem.at[1])
+    op_copy.start()
     pos = lax.axis_index("face")
     owners, slabs, depth, width = got_ref.shape
     aggregates = out_ref.shape[1]
     count = rest_ref.shape[1]
     edge = count // 4
-    hits = hits_ref[...]
     main = got_ref[:, pl.ds(pos, 1)].astype(F32).reshape(owners * depth, width).astype(BF16)
     side = got_ref[:, pl.ds(jnp.minimum(pos + 1, slabs - 1), 1)]
     side = jnp.where(pos < slabs - 1, side.astype(F32).reshape(owners * depth, width), 0.0).astype(BF16)
@@ -595,11 +598,21 @@
     rim = jnp.where(pos > 0, rim.astype(F32).reshape(8, width), 0.0)
     rim = jnp.concatenate([rim, pltpu.roll(rim, count - edge, 1)], 0)
     rim = jnp.where(lanes(rim.shape) < edge, turn(rim, facts_ref[3:4]), 0.0)
-    rest = rest_ref[...] + dot_split(halves(edge_ref[0:16]), halves(rim), TN)
+    none = jnp.zeros((32, count), F32)
+    rim = jnp.concatenate([none, rim, jnp.zeros((count - 48, count), F32)], 0)
+    rest = rest_ref[...] + dot_split(edge_ref[...], halves(rim))
     nodes = dot(rest.astype(BF16), stay_hits(facts_ref, staying, aggregates), NT)
-    nodes = nodes + dot_split(halves(edge_ref[16:32]), halves(side), TN)
-    made = dot_split(halves(small_table()), halves(nodes), NN)
+    side = jnp.concatenate(
+        [jnp.zeros((48, aggregates), F32), side, jnp.zeros((count - 64, aggregates), F32)], 0
+    )
+    nodes = nodes + dot_split(edge_ref[...], halves(side))
+    made = dot_split(small_table(), halves(nodes))
     out_ref[...] = (made + main)[:COARSE]
+    rhs_copy = pltpu.make_async_copy(out_ref, rhs_out, sem.at[2])
+    rhs_copy.start()
+    sol_copy.wait()
+    op_copy.wait()
+    rhs_copy.wait()
 
 
 def call(kernel, outs, args, spaces, out_spaces=None, scratch=(), flops=0, limit=VMEM_LIMIT):
@@ -623,13 +636,13 @@
     return jax.ShapeDtypeStruct(shape, dtype)
 
 
-def block_table(table, copies, row_step):
+def block_table(table, copies, tall):
     out = []
     for part in split_table(table):
-        full = np.zeros((ceil_to(copies * table.shape[0], row_step), copies * table.shape[1]), BF16)
+        full = np.zeros((copies * tall, copies * table.shape[1]), BF16)
         for copy in range(copies):
             full[
-                copy * table.shape[0] : (copy + 1) * table.shape[0],
+                copy * tall : copy * tall + table.shape[0],
                 copy * table.shape[1] : (copy + 1) * table.shape[1],
             ] = part
         out.append(full)
@@ -649,10 +662,9 @@
     capacity = ceil_to(capacity, 4)
     chunk = 6 * capacity
     entries = 6 * 128
-    groups = -(-COARSE // GROUP)
     owner = owner.reshape(1, count)
     slot = slot.reshape(1, count)
-    table = jnp.asarray(block_table(restrict_table(), GROUP, 16))
+    table = jnp.asarray(block_table(restrict_table(), GROUP, 32))
 
     args = [diag_block, slot, owner, table, start, rhs, lift, neighbour, orient, precond]
     outs = [
@@ -669,12 +681,11 @@
         [pl.ANY] * len(outs),
         scratch=[pltpu.VMEM(each.shape, each.dtype) for each in held + outs]
         + [
-            pltpu.VMEM((groups * GROUP, NODES, count), BF16),
-            pltpu.VMEM((groups * GROUP, NODES, count), BF16),
             pltpu.VMEM((entries, count), F32),
-            pltpu.SemaphoreType.DMA((NODES // 16,)),
+            pltpu.SemaphoreType.DMA((2,)),
             pltpu.SemaphoreType.DMA((8,)),
-            pltpu.SemaphoreType.DMA((3,)),
+            pltpu.SemaphoreType.DMA((2,)),
+            pltpu.SemaphoreType.DMA((2,)),
         ],
         flops=200_000_000,
         limit=FIRST_LIMIT,
@@ -695,16 +706,11 @@
             struct((NODES, count), F32),
             struct((16, count), F32),
             struct((8, count), jnp.int32),
-            struct((32, NODES), F32),
+            struct((NODES, count), F32),
         ],
         [gathered, diag_block, precond, pack, partial],
         [pltpu.VMEM] * 5,
-        [pl.ANY] + [pltpu.VMEM] * 4,
-        scratch=[
-            pltpu.VMEM((NODES, count), F32),
-            pltpu.VMEM((NODES, count), F32),
-            pltpu.SemaphoreType.DMA(()),
-        ],
+        scratch=[pltpu.VMEM((NODES, count), F32)],
         flops=200_000_000,
     )
     (send,) = call(
@@ -717,21 +723,18 @@
     got = lax.all_to_all(
         send.reshape(owner_count * slabs, depth, 128), ("dom", "face"), split_axis=0, concat_axis=0, tiled=True
     ).reshape(owner_count, slabs, depth, 128)
-    coarse_op, hits = call(
-        lambda *refs: operator_kernel(staying, *refs),
-        [
-            struct((aggregates, COARSE * COARSE), F32),
-            struct((owner_count * depth, GROUP * aggregates), BF16),
-        ],
-        [op_got, local_op, facts],
-        [pltpu.VMEM] * 3,
-        flops=100_000_000,
-    )
-    (coarse_rhs,) = call(
+    outs = [
+        struct((NODES, count), F32),
+        struct((aggregates, COARSE * COARSE), F32),
+        struct((COARSE, aggregates), F32),
+    ]
+    sol, coarse_op, coarse_rhs = call(
         lambda *refs: last_kernel(staying, *refs),
-        [struct((COARSE, aggregates), F32)],
-        [got, hits, rest, facts, edge],
-        [pltpu.VMEM] * 5,
+        outs,
+        [got, op_got, local_op, rest, facts, edge, sol],
+        [pltpu.VMEM] * 7,
+        [pl.ANY] * 3,
+        scratch=[pltpu.VMEM(each.shape, each.dtype) for each in outs[1:]] + [pltpu.SemaphoreType.DMA((3,))],
         flops=100_000_000,
     )
     return (sol, coarse_op.T, coarse_rhs)

time: 36.1 us -> 35 us (0.970)
  blocking collectives: 5.56 us -> 16.6 us
  waiting for transfers between devices: 8.95 us -> 3.12 us
  starting transfers between devices: 11.2 us -> 7.39 us
  Pallas kernels: 9.35 us -> 7 us
    all_to_all x0 -> x1, blocking collectives: none -> 11 us  [per_device(): lax.all_to_all(send.reshape(owner_count * slabs, depth, 128), ('dom', 'fa...]
    all_to_all x1 -> x0, waiting for transfers between devices: 6.21 us -> none  [per_device(): lax.all_to_all(send.reshape(owner_count * slabs, depth, 128), ('dom', 'fa...]
    all_to_all x1 -> x0, starting transfers between devices: 3.79 us -> none  [per_device(): lax.all_to_all(send.reshape(owner_count * slabs, depth, 128), ('dom', 'fa...]
    pallas_call x6 -> x5, Pallas kernels: 9.35 us -> 7 us  [call(): pl.pallas_call(kernel, out_shape=tuple(outs), in_specs=[pl.BlockSpec(memo...]
    all_to_all x1, waiting for transfers between devices: 2.74 us -> 3.12 us  [per_device(): lax.all_to_all(op_send, 'dom', split_axis=0, concat_axis=0, tiled=True)]
  transfers between devices with their start and end apart: 2 -> 1, of which waited for: 2 -> 1; matrix products, arithmetic and copies ran while one was open for 0% -> 0% of each run, Pallas kernels for 10% -> 6%
where the time goes in v5:
time: 35 us; the launch traced here: 34.8 us
  blocking collectives  16.6 us (47%)
  starting transfers between devices  7.39 us (21%)
  Pallas kernels  7 us (20%)
  waiting for transfers between devices  3.12 us (9%)
  between operations  0.7 us (2%)
    all_to_all x1, blocking collectives, per_device(): lax.all_to_all(send.reshape(owner_count * slabs, depth, 128), ('dom', 'fa...  11 us
    all_to_all x1, starting transfers between devices, per_device(): lax.all_to_all(op_send, 'dom', split_axis=0, concat_axis=0, tiled=True)  7.39 us
    pallas_call x5, Pallas kernels, call(): pl.pallas_call(kernel, out_shape=tuple(outs), in_specs=[pl.BlockSpec(memo...  7 us
    all_gather x1, blocking collectives, per_device(): gathered = lax.all_gather(message, 'face')  5.56 us
    all_to_all x1, waiting for transfers between devices, per_device(): lax.all_to_all(op_send, 'dom', split_axis=0, concat_axis=0, tiled=True)  3.12 us
  transfers between devices with their start and end apart: 1, of which 1 were waited for; matrix products, arithmetic and copies ran while one was open for 0% of the time, Pallas kernels for 6%

profile of v5, /device:TPU:0, one launch (start us, length us, event | category | flops | bytes accessed | tf_op | source)
XLA Modules:
  0.0 34.8 jit_solution(9988512490470477731)
XLA Ops:
  0.6 0.0 copy-start
  0.6 0.0 copy-start.1
  0.7 3.2 %shard_map.121 = (bf16[8,168,128]{2,1,0:T(8,128)(2,1)}, bf16[768,128]{1,0:T(8,128)(2,1)}, f32[248,128]{1,0:T(8,128)}) custom-call(bf16[64,64,128]{2,1,0:T(8,128)(2,1)} %refs_1_.3, s32[1,128]{1,0:T(1,128)} %bitcast.9, s32[1,128]{1,0:T(1,128)} %bitcast.10, bf16[256,256]{1,0:T(8,128)(2,1)} %constant.2.clone.refs_3_, f32[64,128]{1,0:T(8,128)} %refs_4_.1, ...), custom_call_target="tpu_custom_call" | custom-call | flops 200000000 | bytes 2993152 | tf_op jit(solution)/shard_map/pallas_call | solution.py:622
  3.9 0.0 copy-start.2
  3.9 7.4 %all-to-all-start = ((bf16[8,168,128]{2,1,0:T(8,128)(2,1)}), bf16[8,168,128]{2,1,0:T(8,128)(2,1)S(1)}, u32[]{:S(2)}, u32[]{:S(2)}) async-start(bf16[8,168,128]{2,1,0:T(8,128)(2,1)} %get-tuple-element.22), calls=%async_computation | async-start | bytes 688128 | tf_op jit(solution)/shard_map/all_to_all | solution.py:693
  11.3 0.0 copy-done
  11.3 0.0 copy-done.1
  11.3 0.0 copy-done.2
  11.3 0.7 %shard_map.122 = (bf16[176,128]{1,0:T(8,128)(2,1)S(1)}, f32[64,128]{1,0:T(8,128)S(1)}) custom-call(bf16[64,64,128]{2,1,0:T(8,128)(2,1)S(1)} %copy-done, bf16[64,64,128]{2,1,0:T(8,128)(2,1)S(1)} %copy-done.1, f32[248,128]{1,0:T(8,128)S(1)} %copy-done.2), custom_call_target="tpu_custom_call" | custom-call | flops 100000000 | bytes 2301952 | tf_op jit(solution)/shard_map/pallas_call | solution.py:622
  12.0 5.6 %all-gather = bf16[704,128]{1,0:T(8,128)(2,1)S(1)} all-gather(bf16[176,128]{1,0:T(8,128)(2,1)S(1)} %get-tuple-element.17), channel_id=2, replica_groups=mesh['dom'=8,'face'=4] {'face'}, dimensions={0}, use_global_device_ids=true | all-gather | bytes 225280 | tf_op jit(solution)/shard_map/all_gather | solution.py:701
  17.6 1.2 %shard_map.123 = (f32[64,128]{1,0:T(8,128)S(1)}, f32[64,128]{1,0:T(8,128)S(1)}, f32[16,128]{1,0:T(8,128)S(1)}, s32[8,128]{1,0:T(8,128)S(1)}, f32[64,128]{1,0:T(8,128)S(1)}) custom-call(bf16[4,176,128]{2,1,0:T(8,128)(2,1)S(1)} %bitcast.6, bf16[64,64,128]{2,1,0:T(8,128)(2,1)S(1)} %copy-done, bf16[64,64,128]{2,1,0:T(8,128)(2,1)S(1)} %copy-done.1, ...), custom_call_target="tpu_custom_call" | custom-call | flops 200000000 | bytes 2547712 | tf_op jit(solution)/shard_map/pallas_call | solution.py:622
  18.8 3.1 %all-to-all-done.after_ref.refs_1_ = bf16[8,168,128]{2,1,0:T(8,128)(2,1)S(1)} async-done(((bf16[8,168,128]{2,1,0:T(8,128)(2,1)}), bf16[8,168,128]{2,1,0:T(8,128)(2,1)S(1)}, u32[]{:S(2)}, u32[]{:S(2)}) %all-to-all-start) | async-done | bytes 344096 | tf_op jit(solution)/shard_map/all_to_all | solution.py:693
  22.0 0.0 copy-start.3
  22.0 0.4 %shard_map.124 = bf16[8,4,8,128]{3,2,1,0:T(8,128)(2,1)S(1)} custom-call(f32[64,128]{1,0:T(8,128)S(1)} %get-tuple-element.19.rest_ref.refs_3_, f32[16,128]{1,0:T(8,128)S(1)} %get-tuple-element.20.rim_ref, s32[8,128]{1,0:T(8,128)S(1)} %get-tuple-element.21.facts_ref.refs_4_, bf16[8,168,128]{2,1,0:T(8,128)(2,1)S(1)} %all-to-all-done.after_ref.refs_1_), custom_call_target="tpu_custom_call" | custom-call | flops 100000000 | bytes 454656 | tf_op jit(solution)/shard_map/pallas_call | solution.py:622
  22.4 11.0 %all_to_all.10 = bf16[32,8,128]{2,1,0:T(8,128)(2,1)S(1)} all-to-all(bf16[32,8,128]{2,1,0:T(8,128)(2,1)S(1)} %bitcast.7), channel_id=1, replica_groups=mesh['dom'=8,'face'=4] {'dom','face'}, dimensions={0} | all-to-all | bytes 131072 | tf_op jit(solution)/shard_map/all_to_all | solution.py:723
  33.4 0.0 copy-done.3
  33.4 1.4 %shard_map.125 = (f32[64,128]{1,0:T(8,128)}, f32[64,729]{1,0:T(8,128)}, f32[27,64]{1,0:T(8,128)}) custom-call(bf16[8,4,8,128]{3,2,1,0:T(8,128)(2,1)S(1)} %bitcast.8, bf16[8,168,128]{2,1,0:T(8,128)(2,1)S(1)} %all-to-all-done.after_ref.refs_1_, bf16[768,128]{1,0:T(8,128)(2,1)S(1)} %copy-done.3, f32[64,128]{1,0:T(8,128)S(1)} %get-tuple-element.19.rest_ref.refs_3_, ...), custom_call_target="tpu_custom_call" | custom-call | flops 100000000 | bytes 934912 | tf_op jit(solution)/shard_map/pallas_call | solution.py:622
Async XLA Ops:
  0.6 10.7 %copy-start = (bf16[64,64,128]{2,1,0:T(8,128)(2,1)S(1)}, bf16[64,64,128]{2,1,0:T(8,128)(2,1)}, u32[]{:S(2)}) copy-start(bf16[64,64,128]{2,1,0:T(8,128)(2,1)} %refs_1_.3) | copy-start | bytes 3145732
  0.6 10.7 %copy-start.1 = (bf16[64,64,128]{2,1,0:T(8,128)(2,1)S(1)}, bf16[64,64,128]{2,1,0:T(8,128)(2,1)}, u32[]{:S(2)}) copy-start(bf16[64,64,128]{2,1,0:T(8,128)(2,1)} %refs_2_.1) | copy-start | bytes 3145732
  3.9 7.4 %copy-start.2 = (f32[248,128]{1,0:T(8,128)S(1)}, f32[248,128]{1,0:T(8,128)}, u32[]{:S(2)}) copy-start(f32[248,128]{1,0:T(8,128)} %get-tuple-element.16.refs_2_.refs_3_) | copy-start | bytes 380932
  3.9 18.1 %all-to-all-start = ((bf16[8,168,128]{2,1,0:T(8,128)(2,1)}), bf16[8,168,128]{2,1,0:T(8,128)(2,1)S(1)}, u32[]{:S(2)}, u32[]{:S(2)}) async-start(bf16[8,168,128]{2,1,0:T(8,128)(2,1)} %get-tuple-element.22), calls=%async_computation | async-start | bytes 688128 | tf_op jit(solution)/shard_map/all_to_all | solution.py:693
  22.0 11.4 %copy-start.3 = (bf16[768,128]{1,0:T(8,128)(2,1)S(1)}, bf16[768,128]{1,0:T(8,128)(2,1)}, u32[]{:S(2)}) copy-start(bf16[768,128]{1,0:T(8,128)(2,1)} %get-tuple-element.23.refs_2_) | copy-start | bytes 589828

commit v6 on v5

--- a/solution.py
+++ b/solution.py
@@ -221,7 +221,10 @@
 RHS = NODES
 LIFT = 2 * NODES
 EDGE = LIFT + NODES
-NEIGHBOUR = EDGE + 32
+TABLE = EDGE + 32
+SIDE = TABLE + 32
+COUPLED = SIDE + 32
+NEIGHBOUR = COUPLED + NODES
 ORIENT = NEIGHBOUR + 8
 OWNER = ORIENT + 8
 SLOT = OWNER + 1
@@ -234,6 +237,9 @@
         self.rhs = ref.at[RHS : RHS + NODES]
         self.lift = ref[LIFT : LIFT + NODES]
         self.edge = ref[EDGE : EDGE + 32, 0:NODES]
+        self.table = ref[TABLE : TABLE + 32, 0:NODES]
+        self.side = ref[SIDE : SIDE + 32]
+        self.coupled = ref[COUPLED : COUPLED + NODES]
         self.neighbour = ref[NEIGHBOUR : NEIGHBOUR + FACES].astype(jnp.int32)
         self.orient = ref[ORIENT : ORIENT + FACES].astype(jnp.int32)
         self.owner = ref[OWNER : OWNER + 1].astype(jnp.int32)
@@ -248,12 +254,10 @@
     count = diag_ref.shape[2]
     packed = Packed(pack_ref)
     start_ref, rhs_ref = packed.start, packed.rhs
-    lift, neighbour_ref, orient_ref = packed.lift, packed.neighbour, packed.orient
+    orient_ref = packed.orient
     traces = face_traces(start_ref)
     shape = traces[2].shape
-    none = jnp.zeros(shape, F32)
-    coupled = coupling(traces, none, none, neighbour_ref, orient_ref, lift)
-    resid = rhs_ref[...] - (apply_blocks(diag_ref, start_ref[...]) - coupled)
+    resid = rhs_ref[...] - (apply_blocks(diag_ref, start_ref[...]) - packed.coupled)
     partial_ref[...] = start_ref[...] + apply_blocks(precond_ref, resid)
     direct = edge_mask(shape)
     reply = response(precond_ref, packed.edge)
@@ -297,7 +301,7 @@
 def middle_kernel(
     staying, capacity,
     gathered_ref, diag_ref, precond_ref, pack_ref, partial_ref,
-    new_ref, rest_ref, rim_ref, facts_ref, edge_ref, sol_ref,
+    new_ref, rest_ref, facts_ref, edge_ref, send_ref, sol_ref,
 ):
     count = diag_ref.shape[2]
     shape = (16, count)
@@ -331,18 +335,17 @@
     traces = face_traces(new_ref)
     none = jnp.zeros(shape, F32)
     coupled = coupling(traces, none, none, neighbour_ref, orient_ref, lift)
-    rest_ref[...] = rhs_ref[...] - (apply_blocks(diag_ref, new_ref[...]) - coupled)
-    rim_ref[...] = pack_rim(traces)
+    rest = rhs_ref[...] - (apply_blocks(diag_ref, new_ref[...]) - coupled)
+    rest_ref[...] = rest
     mine = gathered_ref[pos, pl.ds(32, 16)].astype(F32)
     target = jnp.where(
         lanes((1, count)) >= count - count // 4, target_of(known, staying, capacity), -1
     )
+    fill_messages(rest, traces, target_of(mine, staying, capacity), target, orient, packed.table, packed.side, send_ref)
     place = rows((8, count))
-    facts = jnp.where(place == 0, orient, target)
-    facts = jnp.where(place == 2, target_of(mine, staying, capacity), facts)
-    facts = jnp.where(place == 3, orient_ref[2:3], facts)
-    facts_ref[...] = jnp.where(place == 4, slot, facts)
-    edge_ref[...] = lift
+    facts_ref[...] = jnp.where(place < 4, orient_ref[2:3], slot)
+    edge_ref[0:NODES] = lift
+    edge_ref[NODES : NODES + 32, 0:NODES] = packed.table
 
 
 def spread(values, copies):
@@ -366,32 +369,38 @@
     return made.reshape(owners, depth, GROUP * values.shape[0])
 
 
-def send_kernel(rest_ref, rim_ref, facts_ref, after_ref, send_ref):
+def fill_messages(rest, traces, own_target, their_target, their_orient, table, side, send_ref):
     pos = lax.axis_index("face")
-    count = rest_ref.shape[1]
+    count = rest.shape[1]
     edge = count // 4
     owners, slabs, depth, _ = send_ref.shape
-    high, low = halves(rest_ref[...])
+    high, low = halves(rest)
     keep = lanes(low.shape) >= count - edge
     low = jnp.where(keep, low.astype(F32), 0.0).astype(BF16)
-    made = dot_split(small_table(), (high, low))
+    made = dot_split(table, (high, low))
+    ours = packed_by_target(made.astype(BF16), own_target, owners, depth)
+    turned = turn(aside(traces[2])[1], their_orient)
+    turned = jnp.concatenate([turned, jnp.zeros((count - 16, count), F32)], 0)
+    lifted = dot_split(side, halves(turned))
+    theirs = packed_by_target(lifted.astype(BF16), their_target, owners, depth)
+    moved = aside(traces[3])[0]
+    group = lanes((8, count)) // edge
+    rim = jnp.where(group == 0, moved[0:8], pltpu.roll(moved[8:16], edge, 1))
     send_ref[...] = jnp.zeros(send_ref.shape, BF16)
-    ours = packed_by_target(made.astype(BF16), facts_ref[2:3], owners, depth)
-    send_ref[:, pl.ds(pos, 1)] = ours.astype(BF16)[:, None]
-    moved_up, moved_down = aside(rim_ref[...])
 
     @pl.when(pos > 0)
     def _():
-        turned = turn(moved_down, facts_ref[0:1])
-        turned = jnp.concatenate([turned, jnp.zeros(turned.shape, F32)], 0).astype(BF16)
-        theirs = packed_by_target(turned, facts_ref[1:2], owners, depth)
         send_ref[:, pl.ds(pos - 1, 1)] = theirs.astype(BF16)[:, None]
 
     @pl.when(pos < slabs - 1)
     def _():
-        group = lanes((8, count)) // edge
-        rim = jnp.where(group == 0, moved_up[0:8], pltpu.roll(moved_up[8:16], edge, 1))
         send_ref[pl.ds(lax.axis_index("dom"), 1), pl.ds(pos + 1, 1), 0:8] = rim.astype(BF16)[None, None]
+
+    send_ref[:, pl.ds(pos, 1)] = ours.astype(BF16)[:, None]
+
+
+def pass_kernel(made_ref, after_ref, send_ref):
+    send_ref[...] = made_ref[...]
 
 
 def rank_row(owner_row, staying, owner_count):
@@ -425,7 +434,7 @@
     send_out, local_out, pack_out,
     diag_ref, slot_ref, owner_ref, table_ref, lift_ref, neighbour_ref, orient_ref,
     send_ref, local_ref, pack_ref,
-    full_ref, part_sem, sem, out_sem, send_sem,
+    full_ref, hits_ref, part_sem, sem, out_sem, send_sem,
 ):
     line = restrict_line()
     count = diag_ref.shape[2]
@@ -442,15 +451,23 @@
         (lift_in, lift_ref), (neighbour_in, neighbour_ref), (orient_in, orient_ref),
     ]
     copies = [pltpu.make_async_copy(src, dst, sem.at[i]) for i, (src, dst) in enumerate(pairs)]
+    for copy in copies:
+        copy.start()
     for part in range(NODES // (wide_step * chunk)):
         part_copy(part).start()
-    for copy in copies:
-        copy.start()
     for copy in copies:
         copy.wait()
     stacked = lift_ref[...].reshape(FACES * 16, NODES)
     stacked = jnp.concatenate([stacked, jnp.zeros((count - FACES * 16, NODES), F32)], 0)
-    pack_ref[LIFT : LIFT + NODES] = stacked.T
+    lift = stacked.T
+    pack_ref[LIFT : LIFT + NODES] = lift
+    table = small_table()
+    pack_ref[TABLE : TABLE + 32, 0:NODES] = table
+    above = jnp.concatenate([stacked[48:64], jnp.zeros((count - 16, NODES), F32)], 0)
+    pack_ref[SIDE : SIDE + 32] = dot_split(table, halves(above.T))
+    traces = face_traces(pack_ref.at[START : START + NODES])
+    none = jnp.zeros(traces[2].shape, F32)
+    pack_ref[COUPLED : COUPLED + NODES] = coupling(traces, none, none, neighbour_ref[...], orient_ref[...], lift)
     pack_ref[EDGE : EDGE + 32, 0:NODES] = stacked[32:64]
     pack_ref[NEIGHBOUR : NEIGHBOUR + FACES] = neighbour_ref[...].astype(F32)
     pack_ref[ORIENT : ORIENT + FACES] = orient_ref[...].astype(F32)
@@ -458,6 +475,16 @@
     pack_ref[SLOT : SLOT + 1] = slot_ref[...].astype(F32)
     pack_copy = pltpu.make_async_copy(pack_ref, pack_out, out_sem.at[1])
     pack_copy.start()
+    owner = owner_ref[...]
+    rank = rank_row(owner, staying, owner_count)
+    target = jnp.where(lanes(owner.shape) >= staying, owner * capacity + rank, -1)
+    twice = jnp.concatenate([target, target], 1)
+    shape = (2 * capacity, 2 * count)
+    upper = (rows(shape) >= capacity).astype(jnp.int32)
+    place = rows(shape) - capacity * upper
+    place = jnp.where(upper == (lanes(shape) >= count).astype(jnp.int32), place, -2 * owner_count * capacity)
+    for o in range(owner_count):
+        hits_ref[2 * capacity * o : 2 * capacity * o + 2 * capacity] = one_hot(place + capacity * o == twice)
     table = table_ref[...]
     padded = table.shape[0] // 2
     tall = padded // GROUP
@@ -480,6 +507,7 @@
         sheet = [contract([bars[j][k] for j in range(4)], line) for k in range(3)]
         planes.append([sheet[k][j] for j in range(3) for k in range(3)])
     made = [contract([planes[i][rest] for i in range(4)], line) for rest in range(9)]
+    full_ref[5 * 128 - 16 : 5 * 128] = jnp.zeros((16, count), F32)
     for c in range(COARSE):
         at = COARSE * c if c < SPLIT else 5 * 128 + COARSE * (c - SPLIT)
         full_ref[at : at + tall] = made[c % 9][c // 9]
@@ -491,14 +519,6 @@
     local_ref[...] = local
     local_copy = pltpu.make_async_copy(local_ref, local_out, out_sem.at[0])
     local_copy.start()
-    owner = owner_ref[...]
-    rank = rank_row(owner, staying, owner_count)
-    target = jnp.where(lanes(owner.shape) >= staying, owner * capacity + rank, -1)
-    twice = jnp.concatenate([target, target], 1)
-    shape = (2 * capacity, 2 * count)
-    upper = (rows(shape) >= capacity).astype(jnp.int32)
-    place = rows(shape) - capacity * upper
-    place = jnp.where(upper == (lanes(shape) >= count).astype(jnp.int32), place, -2 * owner_count * capacity)
     wide = [
         jnp.concatenate([local[256 * pair : 256 * pair + 128], local[256 * pair + 128 : 256 * pair + 256]], 1)
         for pair in range(3)
@@ -507,8 +527,7 @@
     share = max(owner_count // 2, 1)
     for first in range(0, owner_count, share):
         some = pl.ds(first, share)
-        hits = [one_hot(place + capacity * o == twice) for o in range(first, first + share)]
-        hits = jnp.concatenate(hits, 0)
+        hits = hits_ref[2 * capacity * first : 2 * capacity * (first + share)]
         for pair in range(3):
             made = dot(hits, wide[pair], NT).reshape(share, 2 * capacity, 128).astype(BF16)
             send_ref[some, 2 * capacity * pair : 2 * capacity * pair + 2 * capacity] = made
@@ -528,7 +547,7 @@
     return total
 
 
-def sum_operators(staying, got_ref, local_ref, facts_ref, op_ref, depth):
+def sum_operators(staying, got_ref, local_ref, facts_ref, op_ref, op_out, sem, depth):
     aggregates = op_ref.shape[0]
     owners, size, count = got_ref.shape
     both = size // 3
@@ -543,27 +562,31 @@
     right = lax.broadcasted_iota(jnp.int32, shape, 2) >= aggregates
     paired = jnp.where(upper == right, hits, 0.0).reshape(owners * both, 2 * aggregates).astype(BF16)
     stay = stay_hits(facts_ref, staying, aggregates)
-    out = []
+    cut = SPLIT * COARSE
+    copies = []
     for pair in range(3):
         block = got_ref[:, both * pair : both * pair + both].astype(F32).reshape(owners * both, count).astype(BF16)
         total = dot(paired, block, TN)
+        out = []
         for side in range(2):
             at = 128 * (2 * pair + side)
             out.append(
                 total[aggregates * side : aggregates * side + aggregates] + dot(stay, local_ref[at : at + 128], NT)
             )
-    cut = SPLIT * COARSE
-    for block in range(4):
-        op_ref[:, 128 * block : 128 * block + 128] = out[block]
-    op_ref[:, 512:cut] = out[4][:, : cut - 512]
-    op_ref[:, cut:] = out[5][:, : COARSE * COARSE - cut]
+        first, last = 256 * pair, min(256 * pair + 256, COARSE * COARSE)
+        middle = cut if pair == 2 else first + 128
+        op_ref[:, first:middle] = out[0][:, : middle - first]
+        op_ref[:, middle:last] = out[1][:, : last - middle]
+        some = pl.ds(first, last - first)
+        copies.append(pltpu.make_async_copy(op_ref.at[:, some], op_out.at[:, some], sem.at[pair]))
+        copies[-1].start()
     parts = []
     for g in range(GROUP):
         part = hits[:, depth * g : depth * g + depth] if depth * g + depth <= both else None
         if part is None:
             part = jnp.zeros((owners, depth, 2 * aggregates), F32)
         parts.append(part.reshape(owners * depth, 2 * aggregates)[:, :aggregates])
-    return jnp.concatenate(parts, 1).astype(BF16)
+    return jnp.concatenate(parts, 1).astype(BF16), copies
 
 
 def stay_hits(facts_ref, staying, aggregates):
@@ -576,13 +599,13 @@
     staying,
     got_ref, op_got_ref, local_ref, rest_ref, facts_ref, edge_ref, sol_ref,
     sol_out, op_out, rhs_out,
-    op_ref, out_ref, sem,
+    op_ref, out_ref, sem, op_sem,
 ):
     sol_copy = pltpu.make_async_copy(sol_ref, sol_out, sem.at[0])
     sol_copy.start()
-    hits = sum_operators(staying, op_got_ref, local_ref, facts_ref, op_ref, got_ref.shape[2])
-    op_copy = pltpu.make_async_copy(op_ref, op_out, sem.at[1])
-    op_copy.start()
+    hits, copies = sum_operators(
+        staying, op_got_ref, local_ref, facts_ref, op_ref, op_out, op_sem, got_ref.shape[2]
+    )
     pos = lax.axis_index("face")
     owners, slabs, depth, width = got_ref.shape
     aggregates = out_ref.shape[1]
@@ -591,28 +614,23 @@
     main = got_ref[:, pl.ds(pos, 1)].astype(F32).reshape(owners * depth, width).astype(BF16)
     side = got_ref[:, pl.ds(jnp.minimum(pos + 1, slabs - 1), 1)]
     side = jnp.where(pos < slabs - 1, side.astype(F32).reshape(owners * depth, width), 0.0).astype(BF16)
-    main = block_sum(dot(main, hits, TN), width // GROUP, aggregates)
-    side = block_sum(dot(side, hits, TN), width // GROUP, aggregates)[0:16]
+    main = dot(jnp.concatenate([main, side], 0), jnp.concatenate([hits, hits], 0), TN)
+    main = block_sum(main, width // GROUP, aggregates)
 
     rim = got_ref[pl.ds(lax.axis_index("dom"), 1), pl.ds(jnp.maximum(pos - 1, 0), 1), 0:8]
     rim = jnp.where(pos > 0, rim.astype(F32).reshape(8, width), 0.0)
     rim = jnp.concatenate([rim, pltpu.roll(rim, count - edge, 1)], 0)
-    rim = jnp.where(lanes(rim.shape) < edge, turn(rim, facts_ref[3:4]), 0.0)
+    rim = jnp.where(lanes(rim.shape) < edge, turn(rim, facts_ref[0:1]), 0.0)
     none = jnp.zeros((32, count), F32)
     rim = jnp.concatenate([none, rim, jnp.zeros((count - 48, count), F32)], 0)
-    rest = rest_ref[...] + dot_split(edge_ref[...], halves(rim))
+    rest = rest_ref[...] + dot_split(edge_ref[0:NODES], halves(rim))
     nodes = dot(rest.astype(BF16), stay_hits(facts_ref, staying, aggregates), NT)
-    side = jnp.concatenate(
-        [jnp.zeros((48, aggregates), F32), side, jnp.zeros((count - 64, aggregates), F32)], 0
-    )
-    nodes = nodes + dot_split(edge_ref[...], halves(side))
-    made = dot_split(small_table(), halves(nodes))
+    made = dot_split(edge_ref[NODES : NODES + 32, 0:NODES], halves(nodes))
     out_ref[...] = (made + main)[:COARSE]
-    rhs_copy = pltpu.make_async_copy(out_ref, rhs_out, sem.at[2])
+    rhs_copy = pltpu.make_async_copy(out_ref, rhs_out, sem.at[1])
     rhs_copy.start()
-    sol_copy.wait()
-    op_copy.wait()
-    rhs_copy.wait()
+    for copy in [sol_copy, rhs_copy] + copies:
+        copy.wait()
 
 
 def call(kernel, outs, args, spaces, out_spaces=None, scratch=(), flops=0, limit=VMEM_LIMIT):
@@ -682,6 +700,7 @@
         scratch=[pltpu.VMEM(each.shape, each.dtype) for each in held + outs]
         + [
             pltpu.VMEM((entries, count), F32),
+            pltpu.VMEM((2 * capacity * owner_count, 2 * count), BF16),
             pltpu.SemaphoreType.DMA((2,)),
             pltpu.SemaphoreType.DMA((8,)),
             pltpu.SemaphoreType.DMA((2,)),
@@ -699,14 +718,14 @@
         flops=100_000_000,
     )
     gathered = lax.all_gather(message, "face")
-    sol, rest, rim, facts, edge = call(
+    sol, rest, facts, edge, made = call(
         lambda *refs: middle_kernel(staying, places, *refs),
         [
             struct((NODES, count), F32),
             struct((NODES, count), F32),
-            struct((16, count), F32),
             struct((8, count), jnp.int32),
-            struct((NODES, count), F32),
+            struct((NODES + 32, count), F32),
+            struct((owner_count, slabs, depth, 128), BF16),
         ],
         [gathered, diag_block, precond, pack, partial],
         [pltpu.VMEM] * 5,
@@ -714,11 +733,11 @@
         flops=200_000_000,
     )
     (send,) = call(
-        send_kernel,
-        [struct((owner_count, slabs, depth, 128), BF16)],
-        [rest, rim, facts, op_got],
-        [pltpu.VMEM] * 3 + [pl.ANY],
-        flops=100_000_000,
+        pass_kernel,
+        [struct(made.shape, made.dtype)],
+        [made, op_got],
+        [pltpu.VMEM, pl.ANY],
+        flops=1_000_000,
     )
     got = lax.all_to_all(
         send.reshape(owner_count * slabs, depth, 128), ("dom", "face"), split_axis=0, concat_axis=0, tiled=True
@@ -734,7 +753,7 @@
         [got, op_got, local_op, rest, facts, edge, sol],
         [pltpu.VMEM] * 7,
         [pl.ANY] * 3,
-        scratch=[pltpu.VMEM(each.shape, each.dtype) for each in outs[1:]] + [pltpu.SemaphoreType.DMA((3,))],
+        scratch=[pltpu.VMEM(each.shape, each.dtype) for each in outs[1:]] + [pltpu.SemaphoreType.DMA((2,)), pltpu.SemaphoreType.DMA((3,))],
         flops=100_000_000,
     )
     return (sol, coarse_op.T, coarse_rhs)

time: 35 us -> 34.4 us (0.983)
  waiting for transfers between devices: 3.12 us -> 2.69 us
    all_to_all x1, waiting for transfers between devices: 3.12 us -> 2.69 us  [per_device(): lax.all_to_all(op_send, 'dom', split_axis=0, concat_axis=0, tiled=True)]
  transfers between devices with their start and end apart: 1 -> 1, of which waited for: 1 -> 1; matrix products, arithmetic and copies ran while one was open for 0% -> 0% of each run, Pallas kernels for 6% -> 7%
where the time goes in v6:
time: 34.4 us; the launch traced here: 34.2 us
  blocking collectives  16.4 us (48%)
  starting transfers between devices  7.4 us (22%)
  Pallas kernels  6.95 us (20%)
  waiting for transfers between devices  2.69 us (8%)
  between operations  0.7 us (2%)
    all_to_all x1, blocking collectives, per_device(): lax.all_to_all(send.reshape(owner_count * slabs, depth, 128), ('dom', 'fa...  10.9 us
    all_to_all x1, starting transfers between devices, per_device(): lax.all_to_all(op_send, 'dom', split_axis=0, concat_axis=0, tiled=True)  7.4 us
    pallas_call x5, Pallas kernels, call(): pl.pallas_call(kernel, out_shape=tuple(outs), in_specs=[pl.BlockSpec(memo...  6.95 us
    all_gather x1, blocking collectives, per_device(): gathered = lax.all_gather(message, 'face')  5.56 us
    all_to_all x1, waiting for transfers between devices, per_device(): lax.all_to_all(op_send, 'dom', split_axis=0, concat_axis=0, tiled=True)  2.69 us
  transfers between devices with their start and end apart: 1, of which 1 were waited for; matrix products, arithmetic and copies ran while one was open for 0% of the time, Pallas kernels for 7%

profile of v6, /device:TPU:0, one launch (start us, length us, event | category | flops | bytes accessed | tf_op | source)
XLA Modules:
  0.0 34.2 jit_solution(8802080808077119367)
XLA Ops:
  0.6 0.0 copy-start
  0.6 0.0 copy-start.1
  0.7 3.2 %shard_map.121 = (bf16[8,168,128]{2,1,0:T(8,128)(2,1)}, bf16[768,128]{1,0:T(8,128)(2,1)}, f32[376,128]{1,0:T(8,128)}) custom-call(bf16[64,64,128]{2,1,0:T(8,128)(2,1)} %refs_1_.3, s32[1,128]{1,0:T(1,128)} %bitcast.9, s32[1,128]{1,0:T(1,128)} %bitcast.10, bf16[256,256]{1,0:T(8,128)(2,1)} %constant.2.clone.refs_3_, f32[64,128]{1,0:T(8,128)} %refs_4_.1, ...), custom_call_target="tpu_custom_call" | custom-call | flops 200000000 | bytes 3058688 | tf_op jit(solution)/shard_map/pallas_call | solution.py:640
  3.9 0.0 copy-start.2
  3.9 7.4 %all-to-all-start = ((bf16[8,168,128]{2,1,0:T(8,128)(2,1)}), bf16[8,168,128]{2,1,0:T(8,128)(2,1)S(1)}, u32[]{:S(2)}, u32[]{:S(2)}) async-start(bf16[8,168,128]{2,1,0:T(8,128)(2,1)} %get-tuple-element.20), calls=%async_computation | async-start | bytes 688128 | tf_op jit(solution)/shard_map/all_to_all | solution.py:712
  11.3 0.0 copy-done
  11.3 0.0 copy-done.1
  11.3 0.0 copy-done.2
  11.3 0.6 %shard_map.122 = (bf16[176,128]{1,0:T(8,128)(2,1)S(1)}, f32[64,128]{1,0:T(8,128)S(1)}) custom-call(bf16[64,64,128]{2,1,0:T(8,128)(2,1)S(1)} %copy-done, bf16[64,64,128]{2,1,0:T(8,128)(2,1)S(1)} %copy-done.1, f32[376,128]{1,0:T(8,128)S(1)} %copy-done.2), custom_call_target="tpu_custom_call" | custom-call | flops 100000000 | bytes 2367488 | tf_op jit(solution)/shard_map/pallas_call | solution.py:640
  12.0 5.6 %all-gather = bf16[704,128]{1,0:T(8,128)(2,1)S(1)} all-gather(bf16[176,128]{1,0:T(8,128)(2,1)S(1)} %get-tuple-element.17), channel_id=2, replica_groups=mesh['dom'=8,'face'=4] {'face'}, dimensions={0}, use_global_device_ids=true | all-gather | bytes 225280 | tf_op jit(solution)/shard_map/all_gather | solution.py:720
  17.5 1.7 %shard_map.123 = (f32[64,128]{1,0:T(8,128)S(1)}, f32[64,128]{1,0:T(8,128)S(1)}, s32[8,128]{1,0:T(8,128)S(1)}, f32[96,128]{1,0:T(8,128)S(1)}, bf16[8,4,8,128]{3,2,1,0:T(8,128)(2,1)S(1)}) custom-call(bf16[4,176,128]{2,1,0:T(8,128)(2,1)S(1)} %bitcast.6, bf16[64,64,128]{2,1,0:T(8,128)(2,1)S(1)} %copy-done, bf16[64,64,128]{2,1,0:T(8,128)(2,1)S(1)} %copy-done.1, ...), custom_call_target="tpu_custom_call" | custom-call | flops 200000000 | bytes 2686976 | tf_op jit(solution)/shard_map/pallas_call | solution.py:640
  19.3 2.7 %all-to-all-done.after_ref.refs_1_ = bf16[8,168,128]{2,1,0:T(8,128)(2,1)S(1)} async-done(((bf16[8,168,128]{2,1,0:T(8,128)(2,1)}), bf16[8,168,128]{2,1,0:T(8,128)(2,1)S(1)}, u32[]{:S(2)}, u32[]{:S(2)}) %all-to-all-start) | async-done | bytes 344096 | tf_op jit(solution)/shard_map/all_to_all | solution.py:712
  22.0 0.0 copy-start.3
  22.0 10.9 %all_to_all.10 = bf16[32,8,128]{2,1,0:T(8,128)(2,1)S(1)} all-to-all(bf16[32,8,128]{2,1,0:T(8,128)(2,1)S(1)} %bitcast.8), channel_id=1, replica_groups=mesh['dom'=8,'face'=4] {'dom','face'}, dimensions={0} | all-to-all | bytes 131072 | tf_op jit(solution)/shard_map/all_to_all | solution.py:742
  32.8 0.0 copy-done.3
  32.8 1.3 %shard_map.125 = (f32[64,128]{1,0:T(8,128)}, f32[64,729]{1,0:T(8,128)}, f32[27,64]{1,0:T(8,128)}) custom-call(bf16[8,4,8,128]{3,2,1,0:T(8,128)(2,1)S(1)} %bitcast.7, bf16[8,168,128]{2,1,0:T(8,128)(2,1)S(1)} %all-to-all-done.after_ref.refs_1_, bf16[768,128]{1,0:T(8,128)(2,1)S(1)} %copy-done.3, f32[64,128]{1,0:T(8,128)S(1)} %get-tuple-element.22.refs_3_, ...), custom_call_target="tpu_custom_call" | custom-call | flops 100000000 | bytes 951296 | tf_op jit(solution)/shard_map/pallas_call | solution.py:640
  (1 shorter events, 0.0 us)
Async XLA Ops:
  0.6 10.7 %copy-start = (bf16[64,64,128]{2,1,0:T(8,128)(2,1)S(1)}, bf16[64,64,128]{2,1,0:T(8,128)(2,1)}, u32[]{:S(2)}) copy-start(bf16[64,64,128]{2,1,0:T(8,128)(2,1)} %refs_1_.3) | copy-start | bytes 3145732
  0.6 10.7 %copy-start.1 = (bf16[64,64,128]{2,1,0:T(8,128)(2,1)S(1)}, bf16[64,64,128]{2,1,0:T(8,128)(2,1)}, u32[]{:S(2)}) copy-start(bf16[64,64,128]{2,1,0:T(8,128)(2,1)} %refs_2_.1) | copy-start | bytes 3145732
  3.9 7.4 %copy-start.2 = (f32[376,128]{1,0:T(8,128)S(1)}, f32[376,128]{1,0:T(8,128)}, u32[]{:S(2)}) copy-start(f32[376,128]{1,0:T(8,128)} %get-tuple-element.16.refs_2_.refs_3_) | copy-start | bytes 577540
  3.9 18.1 %all-to-all-start = ((bf16[8,168,128]{2,1,0:T(8,128)(2,1)}), bf16[8,168,128]{2,1,0:T(8,128)(2,1)S(1)}, u32[]{:S(2)}, u32[]{:S(2)}) async-start(bf16[8,168,128]{2,1,0:T(8,128)(2,1)} %get-tuple-element.20), calls=%async_computation | async-start | bytes 688128 | tf_op jit(solution)/shard_map/all_to_all | solution.py:712
  22.0 10.9 %copy-start.3 = (bf16[768,128]{1,0:T(8,128)(2,1)S(1)}, bf16[768,128]{1,0:T(8,128)(2,1)}, u32[]{:S(2)}) copy-start(bf16[768,128]{1,0:T(8,128)(2,1)} %get-tuple-element.21.refs_2_) | copy-start | bytes 589828

commit v7 on v6

v7 whole, which is shorter than its diff:
```python
import jax
import jax.numpy as jnp
import numpy as np
from jax import lax
from jax.experimental import pallas as pl
from jax.experimental.pallas import tpu as pltpu
from jax.sharding import PartitionSpec as P

SWEEPS = 2
NODES = 64
COARSE = 27
FACES = 6
GROUP = 4
SPLIT = 23
F32 = jnp.float32
BF16 = jnp.bfloat16
VMEM_LIMIT = 24 * 1024 * 1024
FIRST_LIMIT = None

NN = (((1,), (0,)), ((), ()))
NT = (((1,), (1,)), ((), ()))
TN = (((0,), (0,)), ((), ()))


def restrict_line():
    fine = np.array([-1.0, -1.0 / np.sqrt(5.0), 1.0 / np.sqrt(5.0), 1.0])
    coarse = np.array([-1.0, 0.0, 1.0])
    basis = np.ones((4, 3))
    for column in range(3):
        for other in range(3):
            if other != column:
                basis[:, column] *= (fine - coarse[other]) / (coarse[column] - coarse[other])
    return basis.T


def restrict_table():
    line = restrict_line()
    return np.kron(np.kron(line, line), line)


def split_table(table):
    table = table.astype(np.float32)
    high = table.astype(BF16)
    low = (table - high.astype(np.float32)).astype(BF16)
    return high, low


def ceil_to(value, step):
    return -(-value // step) * step


def halves(values):
    high = values.astype(BF16)
    low = (values - high.astype(F32)).astype(BF16)
    return high, low


def dot(left, right, dims):
    return lax.dot_general(left, right, dims, preferred_element_type=F32)


def dot_split(left, right):
    left_high, left_low = halves(left)
    right_high, right_low = right
    size = left.shape[0]
    both = dot(jnp.concatenate([left_high, left_low], 0), right_high, NN)
    return both[:size] + both[size:] + dot(left_high, right_low, NN)


def small_table():
    shape = (32, NODES)
    line = restrict_line()
    row, col = rows(shape), lanes(shape)
    step = 9
    table = jnp.ones(shape, F32)
    left = row
    for digit in range(3):
        mine = (left >= step).astype(jnp.int32) + (left >= 2 * step).astype(jnp.int32)
        left = left - step * mine
        fine = (col >> (4 - 2 * digit)) & 3
        value = jnp.zeros(shape, F32)
        for i in range(3):
            for j in range(4):
                value = jnp.where((mine == i) & (fine == j), float(line[i, j]), value)
        table = table * value
        step //= 3
    return jnp.where(row < COARSE, table, 0.0)


def lanes(shape):
    return lax.broadcasted_iota(jnp.int32, shape, 1)


def rows(shape):
    return lax.broadcasted_iota(jnp.int32, shape, 0)


def face_traces(ref):
    return [
        ref[0:16],
        ref[48:64],
        jnp.concatenate([ref[16 * i : 16 * i + 4] for i in range(4)], 0),
        jnp.concatenate([ref[16 * i + 12 : 16 * i + 16] for i in range(4)], 0),
        ref[pl.ds(0, 16, stride=4)],
        ref[pl.ds(3, 16, stride=4)],
    ]


def take(values, index, axis):
    return jnp.take_along_axis(values, index, axis=axis, mode="promise_in_bounds")


def turn(values, orient_row):
    shape = values.shape
    orient = jnp.broadcast_to(orient_row, shape)
    place = rows(shape)
    first = (place >> 2) ^ ((orient & 1) * 3)
    second = (place & 3) ^ (((orient >> 1) & 1) * 3)
    flip = (orient & 4) > 0
    source = jnp.where(flip, 4 * second + first, 4 * first + second)
    out = []
    for half in (source[:8], source[8:]):
        within = half & 7
        out.append(jnp.where(half >= 8, take(values[8:], within, 0), take(values[:8], within, 0)))
    return jnp.concatenate(out, 0)


def pick(traces, neighbour_ref, face):
    values = traces[face ^ 1]
    count = values.shape[1]
    index = jnp.clip(neighbour_ref[face : face + 1] - (face ^ 1) * count, 0, count - 1)
    return take(values, jnp.broadcast_to(index, values.shape), 1)


def fold(parts):
    place = rows(parts[0].shape)
    step = 1
    while len(parts) > 1:
        even = (place & step) == 0
        parts = [
            jnp.where(even, x, y) + pltpu.roll(jnp.where(even, y, x), step, 0)
            for x, y in zip(parts[::2], parts[1::2])
        ]
        step *= 2
    return parts[0]


def apply_blocks(ref, values):
    count = values.shape[1]
    tiles = values.reshape(NODES // 8, 8, count)
    out = []
    for group in range(NODES // 8):
        parts = []
        for node in range(8 * group, 8 * group + 8):
            parts.append(jnp.sum(ref[node].astype(F32).reshape(NODES // 8, 8, count) * tiles, axis=0))
        out.append(fold(parts))
    return jnp.concatenate(out, 0)


def pack_rim(traces):
    shape = traces[2].shape
    return jnp.where(lanes(shape) < shape[1] // 2, traces[2], traces[3])


def coupling(traces, below, above, neighbour_ref, orient_ref, lift):
    count = below.shape[1]
    edge = count // 4
    turned = []
    for face in range(FACES):
        values = pick(traces, neighbour_ref, face)
        if face == 2:
            values = jnp.where(lanes(values.shape) < edge, below, values)
        if face == 3:
            values = jnp.where(lanes(values.shape) >= count - edge, above, values)
        turned.append(turn(values, orient_ref[face : face + 1]))
    turned = jnp.concatenate(turned + [jnp.zeros((count - FACES * 16, count), F32)], 0)
    return dot_split(lift, halves(turned))


def edge_mask(shape):
    return (lanes(shape) < shape[1] // 4) | (lanes(shape) >= shape[1] - shape[1] // 4)


def low_mask(shape):
    return ((lanes(shape) // (shape[1] // 4)) & 1) == 0


def both_halves(shape, low, high):
    return jnp.where(lanes(shape) < shape[1] // 2, low, high)


def response(precond_ref, edge):
    count = precond_ref.shape[2]
    parts = []
    for lift in (edge[0:16], edge[16:32]):
        parts.extend(halves(lift))
    stack = jnp.concatenate(parts, 0)
    shape = (NODES, count)
    out = []
    for spot in range(16):
        node = 16 * (spot // 4) + spot % 4
        block = both_halves(shape, precond_ref[node].astype(F32), precond_ref[node + 12].astype(F32))
        made = dot(stack, block.astype(BF16), NN)
        out.append(
            both_halves((16, count), made[0:16] + made[16:32], made[32:48] + made[48:64])
        )
    return out


def halo_lift(below, above, orient_ref, lift):
    shape = below.shape
    edge = shape[1] // 4
    low = jnp.where(lanes(shape) < edge, turn(below, orient_ref[2:3]), 0.0)
    high = jnp.where(lanes(shape) >= shape[1] - edge, turn(above, orient_ref[3:4]), 0.0)
    none = jnp.zeros((32, shape[1]), F32)
    rest = jnp.zeros((shape[1] - 64, shape[1]), F32)
    return dot_split(lift, halves(jnp.concatenate([none, low, high, rest], 0)))


RHS = 0
PARTIAL = NODES
LIFT = 2 * NODES
EDGE = LIFT + NODES
TABLE = EDGE + 32
NEIGHBOUR = TABLE + 32
ORIENT = NEIGHBOUR + 8
OWNER = ORIENT + 8
RANK = OWNER + 1
SLOT = OWNER + 2
PACKED = ORIENT + 16


class Packed:
    def __init__(self, ref):
        self.rhs = ref.at[RHS : RHS + NODES]
        self.partial = ref.at[PARTIAL : PARTIAL + NODES]
        self.lift = ref[LIFT : LIFT + NODES]
        self.table = ref[TABLE : TABLE + 32, 0:NODES]
        self.neighbour = ref[NEIGHBOUR : NEIGHBOUR + FACES].astype(jnp.int32)
        self.orient = ref[ORIENT : ORIENT + FACES].astype(jnp.int32)
        self.owner = ref[OWNER : OWNER + 1].astype(jnp.int32)
        self.rank = ref[RANK : RANK + 1].astype(jnp.int32)
        self.slot = ref[SLOT : SLOT + 1].astype(jnp.int32)

    def target(self, staying, capacity):
        return jnp.where(lanes(self.owner.shape) >= staying, self.owner * capacity + self.rank, -1)


def smooth_kernel(
    staying, owner_count,
    diag_in, precond_in, start_in, rhs_in, lift_in, neighbour_in, orient_in, owner_in, slot_in,
    message_out, pack_out,
    diag_ref, precond_ref, start_ref, lift_ref, neighbour_ref, orient_ref, owner_ref, slot_ref,
    message_ref, pack_ref, sem, diag_sem, precond_sem, out_sem,
):
    count = diag_ref.shape[2]
    pairs = [
        (start_in, start_ref), (neighbour_in, neighbour_ref), (orient_in, orient_ref), (lift_in, lift_ref),
        (rhs_in, pack_ref.at[RHS : RHS + NODES]), (owner_in, owner_ref), (slot_in, slot_ref),
    ]
    copies = [pltpu.make_async_copy(src, dst, sem.at[i]) for i, (src, dst) in enumerate(pairs)]
    diag_copy = pltpu.make_async_copy(diag_in, diag_ref, diag_sem)
    precond_copy = pltpu.make_async_copy(precond_in, precond_ref, precond_sem)
    for copy in copies + [diag_copy, precond_copy]:
        copy.start()
    for copy in copies:
        copy.wait()
    stacked = lift_ref[...].reshape(FACES * 16, NODES)
    lift = jnp.concatenate([stacked, jnp.zeros((count - FACES * 16, NODES), F32)], 0).T
    pack_ref[LIFT : LIFT + NODES] = lift
    pack_ref[EDGE : EDGE + 32, 0:NODES] = stacked[32:64]
    pack_ref[TABLE : TABLE + 32, 0:NODES] = small_table()
    pack_ref[NEIGHBOUR : NEIGHBOUR + FACES] = neighbour_ref[...].astype(F32)
    pack_ref[ORIENT : ORIENT + FACES] = orient_ref[...].astype(F32)
    owner = owner_ref[...]
    rank = rank_row(owner, staying, owner_count)
    pack_ref[OWNER : OWNER + 1] = owner.astype(F32)
    pack_ref[RANK : RANK + 1] = rank.astype(F32)
    pack_ref[SLOT : SLOT + 1] = slot_ref[...].astype(F32)
    traces = face_traces(start_ref)
    shape = traces[2].shape
    direct = edge_mask(shape)
    none = jnp.zeros(shape, F32)
    coupled = coupling(traces, none, none, neighbour_ref[...], orient_ref[...], lift)
    orient = both_halves((1, count), orient_ref[2:3], orient_ref[3:4])
    message_ref[32:48] = jnp.broadcast_to(orient.astype(F32), shape).astype(BF16)
    diag_copy.wait()
    resid = pack_ref[RHS : RHS + NODES] - (apply_blocks(diag_ref, start_ref[...]) - coupled)
    precond_copy.wait()
    reply = response(precond_ref, stacked[32:64])
    for spot in range(8):
        message_ref[48 + 16 * spot : 64 + 16 * spot] = jnp.where(
            direct, reply[spot], pltpu.roll(reply[spot + 8], count // 2, 1)
        ).astype(BF16)
    partial_ref = pack_ref.at[PARTIAL : PARTIAL + NODES]
    partial_ref[...] = start_ref[...] + apply_blocks(precond_ref, resid)
    pack_copy = pltpu.make_async_copy(pack_ref, pack_out, out_sem.at[0])
    pack_copy.start()
    later = pack_rim(face_traces(partial_ref))
    high, low = halves(jnp.where(direct, pack_rim(traces), pltpu.roll(later, count // 2, 1)))
    message_ref[0:16] = high
    message_ref[16:32] = low
    message_copy = pltpu.make_async_copy(message_ref, message_out, out_sem.at[1])
    message_copy.start()
    pack_copy.wait()
    message_copy.wait()


def sides(first, second):
    pos, slabs = lax.axis_index("face"), lax.axis_size("face")
    even = lax.rem(pos, 2) == 0
    above = jnp.where(even, first, second)
    below = jnp.where(even, second, first)
    return jnp.where(pos < slabs - 1, above, 0.0), jnp.where(pos > 0, below, 0.0)


def merged(first_ref, second_ref, at):
    above, below = sides(first_ref[at].astype(F32), second_ref[at].astype(F32))
    return jnp.where(low_mask(above.shape), above, below)


def aside(values):
    count = values.shape[1]
    return pltpu.roll(values, count // 4, 1), pltpu.roll(values, count - count // 4, 1)


def middle_kernel(
    first_ref, second_ref, message_ref, diag_ref, precond_ref, pack_ref, after_ref,
    new_ref, rest_ref, rim_ref, sol_ref,
):
    count = diag_ref.shape[2]
    shape = (16, count)
    packed = Packed(pack_ref)
    rhs_ref, partial_ref = packed.rhs, packed.partial
    lift, neighbour_ref, orient_ref = packed.lift, packed.neighbour, packed.orient
    head = merged(first_ref, second_ref, pl.ds(0, 16)) + merged(first_ref, second_ref, pl.ds(16, 16))
    orient = merged(first_ref, second_ref, pl.ds(32, 16))[0:1].astype(jnp.int32)
    own = message_ref[0:16].astype(F32) + message_ref[16:32].astype(F32)
    from_high, from_low = aside(own)
    sent = turn(both_halves(shape, from_high, from_low), orient)
    below, above = aside(head)
    delta = halo_lift(below, above, orient_ref, lift)
    sol_ref[...] = partial_ref[...] + apply_blocks(precond_ref, delta)
    later = pltpu.roll(head, count // 2, 1)
    reply = []
    for spot in range(8):
        block = merged(first_ref, second_ref, pl.ds(48 + 16 * spot, 16))
        reply.append((block, pltpu.roll(block, count // 2, 1)))
    reply = [pair[0] for pair in reply] + [pair[1] for pair in reply]
    change = [block * sent for block in reply]
    change = [block[:8] + block[8:] for block in change]
    change = jnp.concatenate([fold(change[:8]), fold(change[8:])], 0)
    below, above = aside(later + change)
    traces = face_traces(sol_ref)
    coupled = coupling(traces, below, above, neighbour_ref, orient_ref, lift)
    resid = rhs_ref[...] - (apply_blocks(diag_ref, sol_ref[...]) - coupled)
    new_ref[...] = sol_ref[...] + apply_blocks(precond_ref, resid)
    traces = face_traces(new_ref)
    rim_ref[...] = pack_rim(traces)
    none = jnp.zeros(shape, F32)
    coupled = coupling(traces, none, none, neighbour_ref, orient_ref, lift)
    rest_ref[...] = rhs_ref[...] - (apply_blocks(diag_ref, new_ref[...]) - coupled)


def spread(values, copies):
    none = jnp.zeros(values.shape, values.dtype)
    return jnp.concatenate(
        [
            jnp.concatenate([values if i == j else none for j in range(copies)], 1)
            for i in range(copies)
        ],
        0,
    )


def packed_by_target(values, target, owners, depth):
    count = values.shape[1]
    shape = (owners * depth, count)
    place = rows(shape)
    base = (place // depth) * (GROUP * depth) + place % depth
    hits = jnp.concatenate([one_hot(base + depth * g == target) for g in range(GROUP)], 1)
    made = dot(hits, spread(values, GROUP), NT)
    return made.reshape(owners, depth, GROUP * values.shape[0])


def send_kernel(staying, first_ref, second_ref, rest_ref, pack_ref, made_ref, low_ref, send_ref):
    packed = Packed(pack_ref)
    owners, size, _ = made_ref.shape
    depth = send_ref.shape[1] - size
    above, below = sides(first_ref[...], second_ref[...])
    below, above = aside(below)[0], aside(above)[1]
    low = (rest_ref[...] + halo_lift(below, above, packed.orient, packed.lift)).astype(BF16)
    low_ref[...] = low
    table_high, table_low = halves(packed.table)
    both = dot(jnp.concatenate([table_high, table_low], 0), low, NN)
    made = both[:32] + both[32:]
    ours = packed_by_target(made.astype(BF16), packed.target(staying, GROUP * depth), owners, depth)
    send_ref[:, 0:size] = made_ref[...]
    send_ref[:, size:] = ours.astype(BF16)


def rank_row(owner_row, staying, owner_count):
    count = owner_row.shape[1]
    shape = (owner_count, count)
    hits = (rows(shape) == owner_row) & (lanes(shape) >= staying)
    hits = jnp.where(hits, 1.0, 0.0)
    before = jnp.where(rows((count, count)) < lanes((count, count)), 1.0, 0.0)
    earlier = dot(hits.astype(BF16), before.astype(BF16), NN)
    return jnp.sum(hits * earlier, axis=0, keepdims=True).astype(jnp.int32)


def one_hot(condition):
    return jnp.where(condition, 1.0, 0.0).astype(BF16)


def contract(four, line):
    first, second = float(line[0, 1]), float(line[0, 2])
    middle = float(line[1, 1])
    return [
        four[0] + first * four[1] + second * four[2],
        middle * (four[1] + four[2]),
        four[3] + second * four[1] + first * four[2],
    ]


def galerkin_kernel(staying, capacity, diag_ref, pack_ref, table_ref, send_ref, local_ref, full_ref):
    line = restrict_line()
    count = diag_ref.shape[2]
    owner_count = send_ref.shape[0]
    packed = Packed(pack_ref)
    target = packed.target(staying, capacity)
    twice = jnp.concatenate([target, target], 1)
    shape = (2 * capacity, 2 * count)
    upper = (rows(shape) >= capacity).astype(jnp.int32)
    place = rows(shape) - capacity * upper
    place = jnp.where(upper == (lanes(shape) >= count).astype(jnp.int32), place, -2 * owner_count * capacity)
    hits = jnp.concatenate([one_hot(place + capacity * o == twice) for o in range(owner_count)], 0)
    table = table_ref[...]
    padded = table.shape[0] // 2
    tall = padded // GROUP
    planes = []
    for i in range(4):
        bars = []
        for half in range(2):
            first = 2 * GROUP * (2 * i + half)
            wide = [
                diag_ref[first + GROUP * j : first + GROUP * j + GROUP].reshape(GROUP * NODES, count)
                for j in range(2)
            ]
            both = dot(table, jnp.concatenate(wide, 1), NN)
            made = both[:padded] + both[padded:]
            for j in range(2):
                four = [made[tall * k : tall * k + tall, count * j : count * j + count] for k in range(4)]
                bars.append(contract(four, line))
        sheet = [contract([bars[j][k] for j in range(4)], line) for k in range(3)]
        planes.append([sheet[k][j] for j in range(3) for k in range(3)])
    made = [contract([planes[i][rest] for i in range(4)], line) for rest in range(9)]
    full_ref[5 * 128 - 16 : 5 * 128] = jnp.zeros((16, count), F32)
    for c in range(COARSE):
        at = COARSE * c if c < SPLIT else 5 * 128 + COARSE * (c - SPLIT)
        full_ref[at : at + tall] = made[c % 9][c // 9]
    full_ref[5 * 128 + COARSE * (COARSE - SPLIT) :] = jnp.zeros((128 - COARSE * (COARSE - SPLIT), count), F32)
    slot = (packed.slot + 1).astype(F32)
    full_ref[5 * 128 - 1 : 5 * 128] = slot
    full_ref[6 * 128 - 1 : 6 * 128] = slot
    local = full_ref[...].astype(BF16)
    local_ref[...] = local
    for pair in range(3):
        wide = jnp.concatenate([local[256 * pair : 256 * pair + 128], local[256 * pair + 128 : 256 * pair + 256]], 1)
        made = dot(hits, wide, NT).reshape(owner_count, 2 * capacity, 128).astype(BF16)
        send_ref[:, 2 * capacity * pair : 2 * capacity * pair + 2 * capacity] = made


def block_sum(made, height, width):
    total = made[0:height, 0:width]
    for g in range(1, GROUP):
        total = total + made[height * g : height * g + height, width * g : width * g + width]
    return total


def sum_operators(got_ref, size, local_ref, stay, op_ref, op_out, sem, depth):
    aggregates = op_ref.shape[0]
    owners, _, count = got_ref.shape
    both = size // 3
    capacity = both // 2
    ids = got_ref[:, 2 * both : size].astype(F32).reshape(owners * both, count)[:, count - 1 : count]
    shape = (owners * both, 2 * aggregates)
    column = lanes(shape)
    column = jnp.where(column >= aggregates, column - aggregates, column)
    hits = jnp.where(ids == (column + 1).astype(F32), 1.0, 0.0).reshape(owners, both, 2 * aggregates)
    shape = (owners, both, 2 * aggregates)
    upper = lax.broadcasted_iota(jnp.int32, shape, 1) >= capacity
    right = lax.broadcasted_iota(jnp.int32, shape, 2) >= aggregates
    paired = jnp.where(upper == right, hits, 0.0).reshape(owners * both, 2 * aggregates).astype(BF16)
    cut = SPLIT * COARSE
    copies = []
    for pair in range(3):
        block = got_ref[:, both * pair : both * pair + both].astype(F32).reshape(owners * both, count).astype(BF16)
        total = dot(paired, block, TN)
        out = []
        for side in range(2):
            at = 128 * (2 * pair + side)
            out.append(
                total[aggregates * side : aggregates * side + aggregates] + dot(stay, local_ref[at : at + 128], NT)
            )
        first, last = 256 * pair, min(256 * pair + 256, COARSE * COARSE)
        middle = cut if pair == 2 else first + 128
        op_ref[:, first:middle] = out[0][:, : middle - first]
        op_ref[:, middle:last] = out[1][:, : last - middle]
        some = pl.ds(first, last - first)
        copies.append(pltpu.make_async_copy(op_ref.at[:, some], op_out.at[:, some], sem.at[pair]))
        copies[-1].start()
    parts = []
    for g in range(GROUP):
        part = hits[:, depth * g : depth * g + depth] if depth * g + depth <= both else None
        if part is None:
            part = jnp.zeros((owners, depth, 2 * aggregates), F32)
        parts.append(part.reshape(owners * depth, 2 * aggregates)[:, :aggregates])
    return jnp.concatenate(parts, 1).astype(BF16), copies


def last_kernel(
    staying, depth, got_ref, local_ref, low_ref, pack_ref, sol_ref,
    sol_out, op_out, rhs_out,
    op_ref, out_ref, sem, op_sem,
):
    sol_copy = pltpu.make_async_copy(sol_ref, sol_out, sem.at[0])
    sol_copy.start()
    packed = Packed(pack_ref)
    owners, size, width = got_ref.shape
    aggregates = out_ref.shape[1]
    shape = (aggregates, low_ref.shape[1])
    stay = one_hot((rows(shape) == packed.slot) & (lanes(shape) < staying))
    hits, copies = sum_operators(got_ref, size - depth, local_ref, stay, op_ref, op_out, op_sem, depth)
    main = got_ref[:, size - depth :].astype(F32).reshape(owners * depth, width).astype(BF16)
    main = block_sum(dot(main, hits, TN), width // GROUP, aggregates)
    nodes = dot(low_ref[...], stay, NT)
    made = dot_split(packed.table, halves(nodes))
    out_ref[...] = (made + main)[:COARSE]
    rhs_copy = pltpu.make_async_copy(out_ref, rhs_out, sem.at[1])
    rhs_copy.start()
    for copy in [sol_copy, rhs_copy] + copies:
        copy.wait()


def call(kernel, outs, args, spaces, out_spaces=None, scratch=(), flops=0, limit=VMEM_LIMIT):
    bytes_in = sum(a.size * a.dtype.itemsize for a in args)
    bytes_out = sum(o.size * o.dtype.itemsize for o in outs)
    out_spaces = out_spaces or [pltpu.VMEM] * len(outs)
    return pl.pallas_call(
        kernel,
        out_shape=tuple(outs),
        in_specs=[pl.BlockSpec(memory_space=space) for space in spaces],
        out_specs=tuple(pl.BlockSpec(memory_space=space) for space in out_spaces),
        scratch_shapes=list(scratch),
        compiler_params=pltpu.CompilerParams(vmem_limit_bytes=limit),
        cost_estimate=pl.CostEstimate(
            flops=flops, bytes_accessed=bytes_in + bytes_out, transcendentals=0
        ),
    )(*args)


def struct(shape, dtype):
    return jax.ShapeDtypeStruct(shape, dtype)


def block_table(table, copies, tall):
    out = []
    for part in split_table(table):
        full = np.zeros((copies * tall, copies * table.shape[1]), BF16)
        for copy in range(copies):
            full[
                copy * tall : copy * tall + table.shape[0],
                copy * table.shape[1] : (copy + 1) * table.shape[1],
            ] = part
        out.append(full)
    return np.concatenate(out, 0)


def per_device(start, rhs, diag_block, precond, lift, neighbour, orient, owner, slot):
    count = start.shape[1]
    staying = count // 4
    aggregates = count // 2
    owner_count = lax.axis_size("dom")
    slabs = lax.axis_size("face")
    movers = count - staying
    capacity = 2 * ((movers + owner_count - 2) // (owner_count - 1))
    depth = ceil_to(-(-capacity // GROUP), 8)
    capacity = ceil_to(capacity, 4)
    chunk = 6 * capacity
    entries = 6 * 128
    owner = owner.reshape(1, count)
    slot = slot.reshape(1, count)
    table = jnp.asarray(block_table(restrict_table(), GROUP, 32))
    pairs = [(i, i ^ 1) for i in range(slabs)]
    others = [(i, (i + 1 if i % 2 else i - 1) % slabs) for i in range(slabs)]

    def exchange(values):
        return lax.ppermute(values, "face", pairs), lax.ppermute(values, "face", others)

    args = [diag_block, precond, start, rhs, lift, neighbour, orient, owner, slot]
    outs = [struct((176, count), BF16), struct((PACKED, count), F32)]
    held = [each for each in args if each is not rhs]
    message, pack = call(
        lambda *refs: smooth_kernel(staying, owner_count, *refs),
        outs,
        args,
        [pl.ANY] * len(args),
        [pl.ANY] * len(outs),
        scratch=[pltpu.VMEM(each.shape, each.dtype) for each in held + outs]
        + [
            pltpu.SemaphoreType.DMA((7,)),
            pltpu.SemaphoreType.DMA(()),
            pltpu.SemaphoreType.DMA(()),
            pltpu.SemaphoreType.DMA((2,)),
        ],
        flops=100_000_000,
        limit=FIRST_LIMIT,
    )
    first, second = exchange(message)
    made, local_op = call(
        lambda *refs: galerkin_kernel(staying, capacity, *refs),
        [struct((owner_count, chunk, 128), BF16), struct((entries, count), BF16)],
        [diag_block, pack, table],
        [pltpu.VMEM] * 3,
        scratch=[pltpu.VMEM((entries, count), F32)],
        flops=1_000_000_000,
    )
    sol, rest, rim = call(
        middle_kernel,
        [struct((NODES, count), F32), struct((NODES, count), F32), struct((16, count), F32)],
        [first, second, message, diag_block, precond, pack, made],
        [pltpu.VMEM] * 6 + [pl.ANY],
        scratch=[pltpu.VMEM((NODES, count), F32)],
        flops=200_000_000,
    )
    first, second = exchange(rim)
    low, send = call(
        lambda *refs: send_kernel(staying, *refs),
        [struct((NODES, count), BF16), struct((owner_count, chunk + depth, 128), BF16)],
        [first, second, rest, pack, made],
        [pltpu.VMEM] * 5,
        flops=50_000_000,
    )
    got = lax.all_to_all(send, "dom", split_axis=0, concat_axis=0, tiled=True)
    outs = [
        struct((NODES, count), F32),
        struct((aggregates, COARSE * COARSE), F32),
        struct((COARSE, aggregates), F32),
    ]
    sol, coarse_op, coarse_rhs = call(
        lambda *refs: last_kernel(staying, depth, *refs),
        outs,
        [got, local_op, low, pack, sol],
        [pltpu.VMEM] * 5,
        [pl.ANY] * 3,
        scratch=[pltpu.VMEM(each.shape, each.dtype) for each in outs[1:]]
        + [pltpu.SemaphoreType.DMA((2,)), pltpu.SemaphoreType.DMA((3,))],
        flops=100_000_000,
    )
    return (sol, coarse_op.T, coarse_rhs)


def solution(mesh):
    return jax.shard_map(
        per_device,
        mesh=mesh,
        in_specs=(
            P(None, ("dom", "face")),
            P(None, ("dom", "face")),
            P(None, None, ("dom", "face")),
            P(None, None, ("dom", "face")),
            P(),
            P(None, ("dom", "face")),
            P(None, ("dom", "face")),
            P(("dom", "face")),
            P(("dom", "face")),
        ),
        out_specs=(P(None, ("dom", "face")), P(None, ("dom", "face")), P(None, ("dom", "face"))),
        check_vma=False,
    )
```

time: 34.4 us -> 32.9 us (0.956)
  starting transfers between devices: 7.4 us -> 5.23 us
  waiting for transfers between devices: 2.69 us -> 1.07 us
  blocking collectives: 16.4 us -> 17.7 us
  local copies, waits for them, and re-layouts: 0.02 us -> 1.31 us
    all_to_all x1 -> x0, starting transfers between devices: 7.4 us -> none  [per_device(): lax.all_to_all(op_send, 'dom', split_axis=0, concat_axis=0, tiled=True)]
    all_to_all x1, blocking collectives: 10.9 us -> 17.7 us  [per_device(): got = lax.all_to_all(send, 'dom', split_axis=0, concat_axis=0, tiled=True)]
    all_gather x1 -> x0, blocking collectives: 5.56 us -> none  [per_device(): gathered = lax.all_gather(message, 'face')]
    ppermute x0 -> x4, starting transfers between devices: none -> 5.23 us  [the longest x2 4.16 us: exchange(): lax.ppermute(values, 'face', others)]
    all_to_all x1 -> x0, waiting for transfers between devices: 2.69 us -> none  [per_device(): lax.all_to_all(op_send, 'dom', split_axis=0, concat_axis=0, tiled=True)]
    unnamed x8 -> x10, local copies, waits for them, and re-layouts: 0.02 us -> 1.31 us
    ppermute x0 -> x4, waiting for transfers between devices: none -> 1.07 us  [the longest x2 1.06 us: exchange(): lax.ppermute(values, 'face', others)]
  transfers between devices with their start and end apart: 1 -> 4, of which waited for: 1 -> 1; matrix products, arithmetic and copies ran while one was open for 0% -> 0% of each run, Pallas kernels for 7% -> 2%
where the time goes in v7:
time: 32.9 us; the launch traced here: 32.7 us
  blocking collectives  17.7 us (54%)
  Pallas kernels  6.7 us (20%)
  starting transfers between devices  5.23 us (16%)
  local copies, waits for them, and re-layouts  1.31 us (4%)
  waiting for transfers between devices  1.07 us (3%)
  between operations  0.7 us (2%)
    all_to_all x1, blocking collectives, per_device(): got = lax.all_to_all(send, 'dom', split_axis=0, concat_axis=0, tiled=True)  17.7 us
    pallas_call x5, Pallas kernels, call(): pl.pallas_call(kernel, out_shape=tuple(outs), in_specs=[pl.BlockSpec(memo...  6.7 us
    ppermute x2, starting transfers between devices, exchange(): lax.ppermute(values, 'face', others)  4.16 us
    unnamed x10, local copies, waits for them, and re-layouts  1.31 us
    ppermute x2, starting transfers between devices, exchange(): lax.ppermute(values, 'face', pairs)  1.07 us
    ppermute x2, waiting for transfers between devices, exchange(): lax.ppermute(values, 'face', others)  1.06 us
  transfers between devices with their start and end apart: 4, of which 1 were waited for; matrix products, arithmetic and copies ran while one was open for 0% of the time, Pallas kernels for 2%

profile of v7, /device:TPU:0, one launch (start us, length us, event | category | flops | bytes accessed | tf_op | source)
XLA Modules:
  0.0 32.7 jit_solution(16083437666973976271)
XLA Ops:
  0.6 0.0 copy-start
  0.6 0.0 copy-start.4
  0.7 2.9 %shard_map.121 = (bf16[176,128]{1,0:T(8,128)(2,1)}, f32[280,128]{1,0:T(8,128)}) custom-call(bf16[64,64,128]{2,1,0:T(8,128)(2,1)} %diag_ref.1, bf16[64,64,128]{2,1,0:T(8,128)(2,1)} %precond_ref.1, f32[64,128]{1,0:T(8,128)} %refs_2_.2, f32[64,128]{1,0:T(8,128)} %refs_3_.1, f32[6,16,64]{2,1,0:T(8,128)} %refs_4_.1, s32[6,128]{1,0:T(8,128)} %refs_5_.1, ...), custom_call_target="tpu_custom_call" | custom-call | flops 100000000 | bytes 2382848 | tf_op jit(solution)/shard_map/pallas_call | solution.py:550
  3.6 2.5 %collective-permute-start.1 = (bf16[176,128]{1,0:T(8,128)(2,1)}, bf16[176,128]{1,0:T(8,128)(2,1)S(1)}, u32[]{:S(2)}, u32[]{:S(2)}) collective-permute-start(bf16[176,128]{1,0:T(8,128)(2,1)} %get-tuple-element.15.message_ref), channel_id=1, source_target_pairs={{0,3},{1,2},{2,1},{3,0},{4,7},{5,6},{6,5},{7,4},{8,11},{9,10},{10,... | collective-permute-start | bytes 135176 | tf_op jit(solution)/shard_map/ppermute | solution.py:599
  6.0 0.7 %collective-permute-start = (bf16[176,128]{1,0:T(8,128)(2,1)}, bf16[176,128]{1,0:T(8,128)(2,1)S(1)}, u32[]{:S(2)}, u32[]{:S(2)}) collective-permute-start(bf16[176,128]{1,0:T(8,128)(2,1)} %get-tuple-element.15.message_ref), channel_id=1, source_target_pairs={{0,1},{1,0},{2,3},{3,2},{4,5},{5,4},{6,7},{7,6},{8,9},{9,8},{10,11... | collective-permute-start | bytes 135176 | tf_op jit(solution)/shard_map/ppermute | solution.py:599
  6.7 0.0 copy-done
  6.7 0.0 copy-done.4
  6.7 0.0 copy-start.2
  6.7 0.9 %copy-done.2 = f32[280,128]{1,0:T(8,128)S(1)} copy-done((f32[280,128]{1,0:T(8,128)S(1)}, f32[280,128]{1,0:T(8,128)}, u32[]{:S(2)}) %copy-start.2) | copy-done | bytes 143384
  7.6 0.0 copy-start.1
  7.6 0.0 copy-start.3
  7.6 0.8 %shard_map.122 = (bf16[8,168,128]{2,1,0:T(8,128)(2,1)S(1)}, bf16[768,128]{1,0:T(8,128)(2,1)S(1)}) custom-call(bf16[64,64,128]{2,1,0:T(8,128)(2,1)S(1)} %copy-done, f32[280,128]{1,0:T(8,128)S(1)} %copy-done.2, bf16[256,256]{1,0:T(8,128)(2,1)S(1)} %copy-done.4), custom_call_target="tpu_custom_call" | custom-call | flops 1000000000 | bytes 1863680 | tf_op jit(solution)/shard_map/pallas_call | solution.py:550
  8.5 0.0 collective-permute-done.1.second_ref
  8.5 0.0 collective-permute-done.first_ref
  8.5 0.4 %copy-done.1 = bf16[64,64,128]{2,1,0:T(8,128)(2,1)S(1)} copy-done((bf16[64,64,128]{2,1,0:T(8,128)(2,1)S(1)}, bf16[64,64,128]{2,1,0:T(8,128)(2,1)}, u32[]{:S(2)}) %copy-start.1) | copy-done | bytes 1048600
  8.9 0.0 copy-done.3
  8.9 1.2 %shard_map.123 = (f32[64,128]{1,0:T(8,128)S(1)}, f32[64,128]{1,0:T(8,128)S(1)}, f32[16,128]{1,0:T(8,128)S(1)}) custom-call(bf16[176,128]{1,0:T(8,128)(2,1)S(1)} %collective-permute-done.first_ref, bf16[176,128]{1,0:T(8,128)(2,1)S(1)} %collective-permute-done.1.second_ref, bf16[176,128]{1,0:T(8,128)(2,1)S(1)} %copy-done.3, bf16[64,64,128]{2,1,0:T(8,128)(2,1)S(1)} %copy-done, ...), custom_call_target="tpu_custom_call" | custom-call | flops 200000000 | bytes 2793472 | tf_op jit(solution)/shard_map/pallas_call | solution.py:550
  10.1 1.7 %collective-permute-start.3 = (f32[16,128]{1,0:T(8,128)S(1)}, f32[16,128]{1,0:T(8,128)S(1)}, u32[]{:S(2)}, u32[]{:S(2)}) collective-permute-start(f32[16,128]{1,0:T(8,128)S(1)} %get-tuple-element.18), channel_id=1, source_target_pairs={{0,3},{1,2},{2,1},{3,0},{4,7},{5,6},{6,5},{7,4},{8,11},{9,10},{10,... | collective-permute-start | bytes 24584 | tf_op jit(solution)/shard_map/ppermute | solution.py:599
  11.7 0.4 %collective-permute-start.2 = (f32[16,128]{1,0:T(8,128)S(1)}, f32[16,128]{1,0:T(8,128)S(1)}, u32[]{:S(2)}, u32[]{:S(2)}) collective-permute-start(f32[16,128]{1,0:T(8,128)S(1)} %get-tuple-element.18), channel_id=1, source_target_pairs={{0,1},{1,0},{2,3},{3,2},{4,5},{5,4},{6,7},{7,6},{8,9},{9,8},{10,11... | collective-permute-start | bytes 24584 | tf_op jit(solution)/shard_map/ppermute | solution.py:599
  12.1 1.1 %collective-permute-done.3.refs_1_ = f32[16,128]{1,0:T(8,128)S(1)} collective-permute-done((f32[16,128]{1,0:T(8,128)S(1)}, f32[16,128]{1,0:T(8,128)S(1)}, u32[]{:S(2)}, u32[]{:S(2)}) %collective-permute-start.3) | collective-permute-done | bytes 8224 | tf_op jit(solution)/shard_map/ppermute | solution.py:599
  13.2 0.0 collective-permute-done.2.refs_0_
  13.2 0.5 %shard_map.124 = (bf16[64,128]{1,0:T(8,128)(2,1)S(1)}, bf16[8,176,128]{2,1,0:T(8,128)(2,1)S(1)}) custom-call(f32[16,128]{1,0:T(8,128)S(1)} %collective-permute-done.2.refs_0_, f32[16,128]{1,0:T(8,128)S(1)} %collective-permute-done.3.refs_1_, f32[64,128]{1,0:T(8,128)S(1)} %get-tuple-element.19.refs_2_, f32[280,128]{1,0:T(8,128)S(1)} %copy-done.2, ...), custom_call_target="tpu_custom_call" | custom-call | flops 50000000 | bytes 913408 | tf_op jit(solution)/shard_map/pallas_call | solution.py:550
  13.7 17.7 %all_to_all.5.refs_0_ = bf16[8,176,128]{2,1,0:T(8,128)(2,1)S(1)} all-to-all(bf16[8,176,128]{2,1,0:T(8,128)(2,1)S(1)} %get-tuple-element.20), channel_id=1, replica_groups=mesh['dom'=8,'face'=4] {'dom'}, dimensions={0} | all-to-all | bytes 720896 | tf_op jit(solution)/shard_map/all_to_all | solution.py:645
  31.4 1.3 %shard_map.125 = (f32[64,128]{1,0:T(8,128)}, f32[64,729]{1,0:T(8,128)}, f32[27,64]{1,0:T(8,128)}) custom-call(bf16[8,176,128]{2,1,0:T(8,128)(2,1)S(1)} %all_to_all.5.refs_0_, bf16[768,128]{1,0:T(8,128)(2,1)S(1)} %get-tuple-element.21.refs_1_, bf16[64,128]{1,0:T(8,128)(2,1)S(1)} %get-tuple-element.22.refs_2_, f32[280,128]{1,0:T(8,128)S(1)} %copy-done.2, ...), custom_call_target="tpu_custom_call" | custom-call | flops 100000000 | bytes 975872 | tf_op jit(solution)/shard_map/pallas_call | solution.py:550
Async XLA Ops:
  0.6 6.1 %copy-start = (bf16[64,64,128]{2,1,0:T(8,128)(2,1)S(1)}, bf16[64,64,128]{2,1,0:T(8,128)(2,1)}, u32[]{:S(2)}) copy-start(bf16[64,64,128]{2,1,0:T(8,128)(2,1)} %diag_ref.1) | copy-start | bytes 3145732
  0.6 6.1 %copy-start.4 = (bf16[256,256]{1,0:T(8,128)(2,1)S(1)}, bf16[256,256]{1,0:T(8,128)(2,1)}, u32[]{:S(2)}) copy-start(bf16[256,256]{1,0:T(8,128)(2,1)} %constant.2.clone.refs_2_) | copy-start | bytes 393220
  3.6 4.9 %collective-permute-start.1 = (bf16[176,128]{1,0:T(8,128)(2,1)}, bf16[176,128]{1,0:T(8,128)(2,1)S(1)}, u32[]{:S(2)}, u32[]{:S(2)}) collective-permute-start(bf16[176,128]{1,0:T(8,128)(2,1)} %get-tuple-element.15.message_ref), channel_id=1, source_target_pairs={{0,3},{1,2},{2,1},{3,0},{4,7},{5,6},{6,5},{7,4},{8,11},{9,10},{10,... | collective-permute-start | bytes 135176 | tf_op jit(solution)/shard_map/ppermute | solution.py:599
  6.0 2.4 %collective-permute-start = (bf16[176,128]{1,0:T(8,128)(2,1)}, bf16[176,128]{1,0:T(8,128)(2,1)S(1)}, u32[]{:S(2)}, u32[]{:S(2)}) collective-permute-start(bf16[176,128]{1,0:T(8,128)(2,1)} %get-tuple-element.15.message_ref), channel_id=1, source_target_pairs={{0,1},{1,0},{2,3},{3,2},{4,5},{5,4},{6,7},{7,6},{8,9},{9,8},{10,11... | collective-permute-start | bytes 135176 | tf_op jit(solution)/shard_map/ppermute | solution.py:599
  6.7 0.9 %copy-start.2 = (f32[280,128]{1,0:T(8,128)S(1)}, f32[280,128]{1,0:T(8,128)}, u32[]{:S(2)}) copy-start(f32[280,128]{1,0:T(8,128)} %get-tuple-element.16.refs_1_.pack_ref.refs_3_) | copy-start | bytes 430084
  7.6 1.2 %copy-start.1 = (bf16[64,64,128]{2,1,0:T(8,128)(2,1)S(1)}, bf16[64,64,128]{2,1,0:T(8,128)(2,1)}, u32[]{:S(2)}) copy-start(bf16[64,64,128]{2,1,0:T(8,128)(2,1)} %precond_ref.1) | copy-start | bytes 3145732
  7.6 1.2 %copy-start.3 = (bf16[176,128]{1,0:T(8,128)(2,1)S(1)}, bf16[176,128]{1,0:T(8,128)(2,1)}, u32[]{:S(2)}) copy-start(bf16[176,128]{1,0:T(8,128)(2,1)} %get-tuple-element.15.message_ref) | copy-start | bytes 135172
  10.1 3.1 %collective-permute-start.3 = (f32[16,128]{1,0:T(8,128)S(1)}, f32[16,128]{1,0:T(8,128)S(1)}, u32[]{:S(2)}, u32[]{:S(2)}) collective-permute-start(f32[16,128]{1,0:T(8,128)S(1)} %get-tuple-element.18), channel_id=1, source_target_pairs={{0,3},{1,2},{2,1},{3,0},{4,7},{5,6},{6,5},{7,4},{8,11},{9,10},{10,... | collective-permute-start | bytes 24584 | tf_op jit(solution)/shard_map/ppermute | solution.py:599
  11.7 1.5 %collective-permute-start.2 = (f32[16,128]{1,0:T(8,128)S(1)}, f32[16,128]{1,0:T(8,128)S(1)}, u32[]{:S(2)}, u32[]{:S(2)}) collective-permute-start(f32[16,128]{1,0:T(8,128)S(1)} %get-tuple-element.18), channel_id=1, source_target_pairs={{0,1},{1,0},{2,3},{3,2},{4,5},{5,4},{6,7},{7,6},{8,9},{9,8},{10,11... | collective-permute-start | bytes 24584 | tf_op jit(solution)/shard_map/ppermute | solution.py:599

commit v8 on v7

--- a/solution.py
+++ b/solution.py
@@ -12,6 +12,8 @@
 FACES = 6
 GROUP = 4
 SPLIT = 23
+CUT = 15
+RIM_ROWS = ((0, 64),)
 F32 = jnp.float32
 BF16 = jnp.bfloat16
 VMEM_LIMIT = 24 * 1024 * 1024
@@ -73,7 +75,8 @@
     row, col = rows(shape), lanes(shape)
     step = 9
     table = jnp.ones(shape, F32)
-    left = row
+    place = jnp.where(row > CUT, row - 1, row)
+    left = place
     for digit in range(3):
         mine = (left >= step).astype(jnp.int32) + (left >= 2 * step).astype(jnp.int32)
         left = left - step * mine
@@ -84,7 +87,7 @@
                 value = jnp.where((mine == i) & (fine == j), float(line[i, j]), value)
         table = table * value
         step //= 3
-    return jnp.where(row < COARSE, table, 0.0)
+    return jnp.where((row != CUT) & (place < COARSE), table, 0.0)
 
 
 def lanes(shape):
@@ -145,15 +148,15 @@
     return parts[0]
 
 
+def block_row(ref, node, tiles):
+    return jnp.sum(ref[node].astype(F32).reshape(tiles.shape) * tiles, axis=0)
+
+
 def apply_blocks(ref, values):
-    count = values.shape[1]
-    tiles = values.reshape(NODES // 8, 8, count)
+    tiles = values.reshape(NODES // 8, 8, values.shape[1])
     out = []
     for group in range(NODES // 8):
-        parts = []
-        for node in range(8 * group, 8 * group + 8):
-            parts.append(jnp.sum(ref[node].astype(F32).reshape(NODES // 8, 8, count) * tiles, axis=0))
-        out.append(fold(parts))
+        out.append(fold([block_row(ref, node, tiles) for node in range(8 * group, 8 * group + 8)]))
     return jnp.concatenate(out, 0)
 
 
@@ -175,14 +178,6 @@
         turned.append(turn(values, orient_ref[face : face + 1]))
     turned = jnp.concatenate(turned + [jnp.zeros((count - FACES * 16, count), F32)], 0)
     return dot_split(lift, halves(turned))
-
-
-def edge_mask(shape):
-    return (lanes(shape) < shape[1] // 4) | (lanes(shape) >= shape[1] - shape[1] // 4)
-
-
-def low_mask(shape):
-    return ((lanes(shape) // (shape[1] // 4)) & 1) == 0
 
 
 def both_halves(shape, low, high):
@@ -218,8 +213,9 @@
 
 
 RHS = 0
-PARTIAL = NODES
-LIFT = 2 * NODES
+START = NODES
+RESID = 2 * NODES
+LIFT = 3 * NODES
 EDGE = LIFT + NODES
 TABLE = EDGE + 32
 NEIGHBOUR = TABLE + 32
@@ -233,7 +229,8 @@
 class Packed:
     def __init__(self, ref):
         self.rhs = ref.at[RHS : RHS + NODES]
-        self.partial = ref.at[PARTIAL : PARTIAL + NODES]
+        self.start = ref.at[START : START + NODES]
+        self.resid = ref.at[RESID : RESID + NODES]
         self.lift = ref[LIFT : LIFT + NODES]
         self.table = ref[TABLE : TABLE + 32, 0:NODES]
         self.neighbour = ref[NEIGHBOUR : NEIGHBOUR + FACES].astype(jnp.int32)
@@ -248,20 +245,26 @@
 
 def smooth_kernel(
     staying, owner_count,
-    diag_in, precond_in, start_in, rhs_in, lift_in, neighbour_in, orient_in, owner_in, slot_in,
-    message_out, pack_out,
-    diag_ref, precond_ref, start_ref, lift_ref, neighbour_ref, orient_ref, owner_ref, slot_ref,
-    message_ref, pack_ref, sem, diag_sem, precond_sem, out_sem,
+    diag_in, precond_in, start_in, rhs_in, lift_in, neighbour_in, orient_in, owner_in, slot_in, table_in,
+    first_out, second_out, pack_out,
+    diag_ref, precond_ref, lift_ref, neighbour_ref, orient_ref, owner_ref, slot_ref,
+    first_ref, second_ref, pack_ref, sem, diag_sem, precond_sem, out_sem,
 ):
     count = diag_ref.shape[2]
+    start_ref = pack_ref.at[START : START + NODES]
     pairs = [
         (start_in, start_ref), (neighbour_in, neighbour_ref), (orient_in, orient_ref), (lift_in, lift_ref),
         (rhs_in, pack_ref.at[RHS : RHS + NODES]), (owner_in, owner_ref), (slot_in, slot_ref),
     ]
     copies = [pltpu.make_async_copy(src, dst, sem.at[i]) for i, (src, dst) in enumerate(pairs)]
     diag_copy = pltpu.make_async_copy(diag_in, diag_ref, diag_sem)
-    precond_copy = pltpu.make_async_copy(precond_in, precond_ref, precond_sem)
-    for copy in copies + [diag_copy, precond_copy]:
+    precond_copies = []
+    for part, (begin, end) in enumerate(RIM_ROWS):
+        at = pl.ds(begin, end - begin)
+        precond_copies.append(
+            pltpu.make_async_copy(precond_in.at[at], precond_ref.at[at], precond_sem.at[part])
+        )
+    for copy in copies + [diag_copy] + precond_copies:
         copy.start()
     for copy in copies:
         copy.wait()
@@ -279,31 +282,50 @@
     pack_ref[SLOT : SLOT + 1] = slot_ref[...].astype(F32)
     traces = face_traces(start_ref)
     shape = traces[2].shape
-    direct = edge_mask(shape)
     none = jnp.zeros(shape, F32)
     coupled = coupling(traces, none, none, neighbour_ref[...], orient_ref[...], lift)
     orient = both_halves((1, count), orient_ref[2:3], orient_ref[3:4])
-    message_ref[32:48] = jnp.broadcast_to(orient.astype(F32), shape).astype(BF16)
+    even = lax.rem(lax.axis_index("face"), 2) == 0
+
+    def write(at, values):
+        low, high = fold_lanes(values)
+        first_ref[at : at + 16] = jnp.where(even, high, low).astype(BF16)
+        second_ref[at : at + 16] = jnp.where(even, low, high).astype(BF16)
+
+    write(16, [jnp.broadcast_to(orient.astype(F32), shape)] * GROUP)
     diag_copy.wait()
     resid = pack_ref[RHS : RHS + NODES] - (apply_blocks(diag_ref, start_ref[...]) - coupled)
-    precond_copy.wait()
-    reply = response(precond_ref, stacked[32:64])
-    for spot in range(8):
-        message_ref[48 + 16 * spot : 64 + 16 * spot] = jnp.where(
-            direct, reply[spot], pltpu.roll(reply[spot + 8], count // 2, 1)
-        ).astype(BF16)
-    partial_ref = pack_ref.at[PARTIAL : PARTIAL + NODES]
-    partial_ref[...] = start_ref[...] + apply_blocks(precond_ref, resid)
+    pack_ref[RESID : RESID + NODES] = resid
     pack_copy = pltpu.make_async_copy(pack_ref, pack_out, out_sem.at[0])
     pack_copy.start()
-    later = pack_rim(face_traces(partial_ref))
-    high, low = halves(jnp.where(direct, pack_rim(traces), pltpu.roll(later, count // 2, 1)))
-    message_ref[0:16] = high
-    message_ref[16:32] = low
-    message_copy = pltpu.make_async_copy(message_ref, message_out, out_sem.at[1])
-    message_copy.start()
-    pack_copy.wait()
-    message_copy.wait()
+    for copy in precond_copies:
+        copy.wait()
+    reply = response(precond_ref, stacked[32:64])
+    for q in range(4):
+        write(32 + 16 * q, reply[GROUP * q : GROUP * q + GROUP])
+    tiles = resid.reshape(NODES // 8, 8, count)
+    steps = []
+    for i in range(4):
+        nodes = [16 * i + k for k in range(4)] + [16 * i + 12 + k for k in range(4)]
+        steps.append(fold([block_row(precond_ref, node, tiles) for node in nodes]))
+    change = both_halves(
+        shape,
+        jnp.concatenate([step[0:4] for step in steps], 0),
+        jnp.concatenate([step[4:8] for step in steps], 0),
+    )
+    parts = []
+    for values in (pack_rim(traces), pack_rim(traces) + change):
+        high, low = halves(values)
+        parts.extend([high.astype(F32), low.astype(F32)])
+    write(0, parts)
+    message_copies = [
+        pltpu.make_async_copy(first_ref, first_out, out_sem.at[1]),
+        pltpu.make_async_copy(second_ref, second_out, out_sem.at[2]),
+    ]
+    for copy in message_copies:
+        copy.start()
+    for copy in [pack_copy] + message_copies:
+        copy.wait()
 
 
 def sides(first, second):
@@ -314,9 +336,30 @@
     return jnp.where(pos < slabs - 1, above, 0.0), jnp.where(pos > 0, below, 0.0)
 
 
-def merged(first_ref, second_ref, at):
-    above, below = sides(first_ref[at].astype(F32), second_ref[at].astype(F32))
-    return jnp.where(low_mask(above.shape), above, below)
+def fold_lanes(values):
+    shape = values[0].shape
+    edge = shape[1] // GROUP
+    rolled = [values[0]] + [pltpu.roll(values[g], g * edge, 1) for g in range(1, GROUP)]
+    group = lanes(shape) // edge
+    low, high = rolled[0], rolled[1]
+    for g in range(1, GROUP):
+        low = jnp.where(group == g, rolled[g], low)
+        high = jnp.where(group == g, rolled[(g + 1) % GROUP], high)
+    return low, high
+
+
+def unfold_lanes(above, below):
+    shape = above.shape
+    edge = shape[1] // GROUP
+    out = []
+    for g in range(GROUP):
+        if g:
+            up = pltpu.roll(above, shape[1] - g * edge, 1)
+            down = pltpu.roll(below, shape[1] - g * edge, 1)
+        else:
+            up, down = above, below
+        out.append(both_halves(shape, up, down))
+    return out
 
 
 def aside(values):
@@ -325,28 +368,27 @@
 
 
 def middle_kernel(
-    first_ref, second_ref, message_ref, diag_ref, precond_ref, pack_ref, after_ref,
-    new_ref, rest_ref, rim_ref, sol_ref,
+    first_ref, second_ref, diag_ref, precond_ref, pack_ref, partial_ref,
+    new_ref, rim_ref, sol_ref,
 ):
     count = diag_ref.shape[2]
     shape = (16, count)
     packed = Packed(pack_ref)
-    rhs_ref, partial_ref = packed.rhs, packed.partial
+    rhs_ref = packed.rhs
     lift, neighbour_ref, orient_ref = packed.lift, packed.neighbour, packed.orient
-    head = merged(first_ref, second_ref, pl.ds(0, 16)) + merged(first_ref, second_ref, pl.ds(16, 16))
-    orient = merged(first_ref, second_ref, pl.ds(32, 16))[0:1].astype(jnp.int32)
-    own = message_ref[0:16].astype(F32) + message_ref[16:32].astype(F32)
-    from_high, from_low = aside(own)
+    above, below = sides(first_ref[...].astype(F32), second_ref[...].astype(F32))
+    head_high, head_low, later_high, later_low = unfold_lanes(above[0:16], below[0:16])
+    head, later = head_high + head_low, later_high + later_low
+    orient = both_halves((16, count), above[16:32], below[16:32])[0:1].astype(jnp.int32)
+    from_high, from_low = aside(pack_rim(face_traces(packed.start)))
     sent = turn(both_halves(shape, from_high, from_low), orient)
+    reply = []
+    for q in range(4):
+        at = slice(32 + 16 * q, 48 + 16 * q)
+        reply.extend(unfold_lanes(above[at], below[at]))
     below, above = aside(head)
     delta = halo_lift(below, above, orient_ref, lift)
     sol_ref[...] = partial_ref[...] + apply_blocks(precond_ref, delta)
-    later = pltpu.roll(head, count // 2, 1)
-    reply = []
-    for spot in range(8):
-        block = merged(first_ref, second_ref, pl.ds(48 + 16 * spot, 16))
-        reply.append((block, pltpu.roll(block, count // 2, 1)))
-    reply = [pair[0] for pair in reply] + [pair[1] for pair in reply]
     change = [block * sent for block in reply]
     change = [block[:8] + block[8:] for block in change]
     change = jnp.concatenate([fold(change[:8]), fold(change[8:])], 0)
@@ -355,48 +397,35 @@
     coupled = coupling(traces, below, above, neighbour_ref, orient_ref, lift)
     resid = rhs_ref[...] - (apply_blocks(diag_ref, sol_ref[...]) - coupled)
     new_ref[...] = sol_ref[...] + apply_blocks(precond_ref, resid)
-    traces = face_traces(new_ref)
-    rim_ref[...] = pack_rim(traces)
-    none = jnp.zeros(shape, F32)
-    coupled = coupling(traces, none, none, neighbour_ref, orient_ref, lift)
-    rest_ref[...] = rhs_ref[...] - (apply_blocks(diag_ref, new_ref[...]) - coupled)
-
-
-def spread(values, copies):
-    none = jnp.zeros(values.shape, values.dtype)
-    return jnp.concatenate(
-        [
-            jnp.concatenate([values if i == j else none for j in range(copies)], 1)
-            for i in range(copies)
-        ],
-        0,
-    )
-
-
-def packed_by_target(values, target, owners, depth):
-    count = values.shape[1]
-    shape = (owners * depth, count)
-    place = rows(shape)
-    base = (place // depth) * (GROUP * depth) + place % depth
-    hits = jnp.concatenate([one_hot(base + depth * g == target) for g in range(GROUP)], 1)
-    made = dot(hits, spread(values, GROUP), NT)
-    return made.reshape(owners, depth, GROUP * values.shape[0])
-
-
-def send_kernel(staying, first_ref, second_ref, rest_ref, pack_ref, made_ref, low_ref, send_ref):
+    rim_ref[...] = pack_rim(face_traces(new_ref))
+
+
+def rest_kernel(diag_ref, pack_ref, sol_ref, rest_ref):
     packed = Packed(pack_ref)
-    owners, size, _ = made_ref.shape
-    depth = send_ref.shape[1] - size
+    traces = face_traces(sol_ref)
+    none = jnp.zeros(traces[2].shape, F32)
+    coupled = coupling(traces, none, none, packed.neighbour, packed.orient, packed.lift)
+    rest_ref[...] = packed.rhs[...] - (apply_blocks(diag_ref, sol_ref[...]) - coupled)
+
+
+def send_kernel(first_ref, second_ref, rest_ref, pack_ref, made_ref, hits_ref, low_ref, send_ref):
+    packed = Packed(pack_ref)
+    owners, size, count = made_ref.shape
+    both = size // 3
     above, below = sides(first_ref[...], second_ref[...])
     below, above = aside(below)[0], aside(above)[1]
     low = (rest_ref[...] + halo_lift(below, above, packed.orient, packed.lift)).astype(BF16)
     low_ref[...] = low
     table_high, table_low = halves(packed.table)
-    both = dot(jnp.concatenate([table_high, table_low], 0), low, NN)
-    made = both[:32] + both[32:]
-    ours = packed_by_target(made.astype(BF16), packed.target(staying, GROUP * depth), owners, depth)
-    send_ref[:, 0:size] = made_ref[...]
-    send_ref[:, size:] = ours.astype(BF16)
+    made = dot(jnp.concatenate([table_high, table_low], 0), low, NN)
+    made = (made[:32] + made[32:]).astype(BF16)
+    none = jnp.zeros((count - 16, count), BF16)
+    wide = jnp.concatenate(
+        [jnp.concatenate([none, made[:16]], 0), jnp.concatenate([none, made[16:]], 0)], 1
+    )
+    extra = dot(hits_ref[...], wide, NT).reshape(owners, both, count)
+    send_ref[:, 0 : 2 * both] = made_ref[:, 0 : 2 * both]
+    send_ref[:, 2 * both :] = (made_ref[:, 2 * both :].astype(F32) + extra).astype(BF16)
 
 
 def rank_row(owner_row, staying, owner_count):
@@ -423,11 +452,15 @@
     ]
 
 
-def galerkin_kernel(staying, capacity, diag_ref, pack_ref, table_ref, send_ref, local_ref, full_ref):
+def galerkin_kernel(
+    staying, capacity, diag_ref, precond_ref, pack_ref, table_ref,
+    send_ref, local_ref, hits_ref, partial_ref, full_ref,
+):
     line = restrict_line()
     count = diag_ref.shape[2]
     owner_count = send_ref.shape[0]
     packed = Packed(pack_ref)
+    partial_ref[...] = packed.start[...] + apply_blocks(precond_ref, packed.resid[...])
     target = packed.target(staying, capacity)
     twice = jnp.concatenate([target, target], 1)
     shape = (2 * capacity, 2 * count)
@@ -435,6 +468,7 @@
     place = rows(shape) - capacity * upper
     place = jnp.where(upper == (lanes(shape) >= count).astype(jnp.int32), place, -2 * owner_count * capacity)
     hits = jnp.concatenate([one_hot(place + capacity * o == twice) for o in range(owner_count)], 0)
+    hits_ref[...] = hits
     table = table_ref[...]
     padded = table.shape[0] // 2
     tall = padded // GROUP
@@ -471,18 +505,20 @@
         send_ref[:, 2 * capacity * pair : 2 * capacity * pair + 2 * capacity] = made
 
 
-def block_sum(made, height, width):
-    total = made[0:height, 0:width]
-    for g in range(1, GROUP):
-        total = total + made[height * g : height * g + height, width * g : width * g + width]
-    return total
-
-
-def sum_operators(got_ref, size, local_ref, stay, op_ref, op_out, sem, depth):
+def last_kernel(
+    staying, got_ref, local_ref, low_ref, pack_ref, sol_ref,
+    sol_out, op_out, rhs_out,
+    op_ref, out_ref, sem, op_sem,
+):
+    sol_copy = pltpu.make_async_copy(sol_ref, sol_out, sem.at[0])
+    sol_copy.start()
+    packed = Packed(pack_ref)
     aggregates = op_ref.shape[0]
-    owners, _, count = got_ref.shape
+    owners, size, count = got_ref.shape
     both = size // 3
     capacity = both // 2
+    shape = (aggregates, low_ref.shape[1])
+    stay = one_hot((rows(shape) == packed.slot) & (lanes(shape) < staying))
     ids = got_ref[:, 2 * both : size].astype(F32).reshape(owners * both, count)[:, count - 1 : count]
     shape = (owners * both, 2 * aggregates)
     column = lanes(shape)
@@ -494,7 +530,7 @@
     paired = jnp.where(upper == right, hits, 0.0).reshape(owners * both, 2 * aggregates).astype(BF16)
     cut = SPLIT * COARSE
     copies = []
-    for pair in range(3):
+    for pair in (2, 0, 1):
         block = got_ref[:, both * pair : both * pair + both].astype(F32).reshape(owners * both, count).astype(BF16)
         total = dot(paired, block, TN)
         out = []
@@ -508,38 +544,17 @@
         op_ref[:, first:middle] = out[0][:, : middle - first]
         op_ref[:, middle:last] = out[1][:, : last - middle]
         some = pl.ds(first, last - first)
-        copies.append(pltpu.make_async_copy(op_ref.at[:, some], op_out.at[:, some], sem.at[pair]))
+        copies.append(pltpu.make_async_copy(op_ref.at[:, some], op_out.at[:, some], op_sem.at[pair]))
         copies[-1].start()
-    parts = []
-    for g in range(GROUP):
-        part = hits[:, depth * g : depth * g + depth] if depth * g + depth <= both else None
-        if part is None:
-            part = jnp.zeros((owners, depth, 2 * aggregates), F32)
-        parts.append(part.reshape(owners * depth, 2 * aggregates)[:, :aggregates])
-    return jnp.concatenate(parts, 1).astype(BF16), copies
-
-
-def last_kernel(
-    staying, depth, got_ref, local_ref, low_ref, pack_ref, sol_ref,
-    sol_out, op_out, rhs_out,
-    op_ref, out_ref, sem, op_sem,
-):
-    sol_copy = pltpu.make_async_copy(sol_ref, sol_out, sem.at[0])
-    sol_copy.start()
-    packed = Packed(pack_ref)
-    owners, size, width = got_ref.shape
-    aggregates = out_ref.shape[1]
-    shape = (aggregates, low_ref.shape[1])
-    stay = one_hot((rows(shape) == packed.slot) & (lanes(shape) < staying))
-    hits, copies = sum_operators(got_ref, size - depth, local_ref, stay, op_ref, op_out, op_sem, depth)
-    main = got_ref[:, size - depth :].astype(F32).reshape(owners * depth, width).astype(BF16)
-    main = block_sum(dot(main, hits, TN), width // GROUP, aggregates)
-    nodes = dot(low_ref[...], stay, NT)
-    made = dot_split(packed.table, halves(nodes))
-    out_ref[...] = (made + main)[:COARSE]
-    rhs_copy = pltpu.make_async_copy(out_ref, rhs_out, sem.at[1])
-    rhs_copy.start()
-    for copy in [sol_copy, rhs_copy] + copies:
+        if pair == 2:
+            nodes = dot(low_ref[...], stay, NT)
+            made = dot_split(packed.table, halves(nodes))
+            sums = [made[16 * side : 16 * side + 16] + out[side].T[count - 16 :] for side in range(2)]
+            out_ref[0:CUT] = sums[0][0:CUT]
+            out_ref[CUT:COARSE] = sums[1][0 : COARSE - CUT]
+            copies.append(pltpu.make_async_copy(out_ref, rhs_out, sem.at[1]))
+            copies[-1].start()
+    for copy in [sol_copy] + copies:
         copy.wait()
 
 
@@ -585,7 +600,6 @@
     slabs = lax.axis_size("face")
     movers = count - staying
     capacity = 2 * ((movers + owner_count - 2) // (owner_count - 1))
-    depth = ceil_to(-(-capacity // GROUP), 8)
     capacity = ceil_to(capacity, 4)
     chunk = 6 * capacity
     entries = 6 * 128
@@ -595,13 +609,13 @@
     pairs = [(i, i ^ 1) for i in range(slabs)]
     others = [(i, (i + 1 if i % 2 else i - 1) % slabs) for i in range(slabs)]
 
-    def exchange(values):
-        return lax.ppermute(values, "face", pairs), lax.ppermute(values, "face", others)
-
-    args = [diag_block, precond, start, rhs, lift, neighbour, orient, owner, slot]
-    outs = [struct((176, count), BF16), struct((PACKED, count), F32)]
-    held = [each for each in args if each is not rhs]
-    message, pack = call(
+    def exchange(one, other):
+        return lax.ppermute(one, "face", pairs), lax.ppermute(other, "face", others)
+
+    args = [diag_block, precond, start, rhs, lift, neighbour, orient, owner, slot, table]
+    outs = [struct((96, count), BF16), struct((96, count), BF16), struct((PACKED, count), F32)]
+    held = [each for each in args if each is not rhs and each is not start and each is not table]
+    to_first, to_second, pack = call(
         lambda *refs: smooth_kernel(staying, owner_count, *refs),
         outs,
         args,
@@ -611,35 +625,47 @@
         + [
             pltpu.SemaphoreType.DMA((7,)),
             pltpu.SemaphoreType.DMA(()),
-            pltpu.SemaphoreType.DMA(()),
-            pltpu.SemaphoreType.DMA((2,)),
+            pltpu.SemaphoreType.DMA((len(RIM_ROWS),)),
+            pltpu.SemaphoreType.DMA((3,)),
         ],
         flops=100_000_000,
         limit=FIRST_LIMIT,
     )
-    first, second = exchange(message)
-    made, local_op = call(
+    first, second = exchange(to_first, to_second)
+    made, local_op, hits, partial = call(
         lambda *refs: galerkin_kernel(staying, capacity, *refs),
-        [struct((owner_count, chunk, 128), BF16), struct((entries, count), BF16)],
-        [diag_block, pack, table],
-        [pltpu.VMEM] * 3,
+        [
+            struct((owner_count, chunk, 128), BF16),
+            struct((entries, count), BF16),
+            struct((2 * capacity * owner_count, 2 * count), BF16),
+            struct((NODES, count), F32),
+        ],
+        [diag_block, precond, pack, table],
+        [pltpu.VMEM] * 4,
         scratch=[pltpu.VMEM((entries, count), F32)],
         flops=1_000_000_000,
     )
-    sol, rest, rim = call(
+    sol, rim = call(
         middle_kernel,
-        [struct((NODES, count), F32), struct((NODES, count), F32), struct((16, count), F32)],
-        [first, second, message, diag_block, precond, pack, made],
-        [pltpu.VMEM] * 6 + [pl.ANY],
+        [struct((NODES, count), F32), struct((16, count), F32)],
+        [first, second, diag_block, precond, pack, partial],
+        [pltpu.VMEM] * 6,
         scratch=[pltpu.VMEM((NODES, count), F32)],
         flops=200_000_000,
     )
-    first, second = exchange(rim)
+    first, second = exchange(rim, rim)
+    (rest,) = call(
+        rest_kernel,
+        [struct((NODES, count), F32)],
+        [diag_block, pack, sol],
+        [pltpu.VMEM] * 3,
+        flops=1_000_000_000,
+    )
     low, send = call(
-        lambda *refs: send_kernel(staying, *refs),
-        [struct((NODES, count), BF16), struct((owner_count, chunk + depth, 128), BF16)],
-        [first, second, rest, pack, made],
-        [pltpu.VMEM] * 5,
+        send_kernel,
+        [struct((NODES, count), BF16), struct((owner_count, chunk, 128), BF16)],
+        [first, second, rest, pack, made, hits],
+        [pltpu.VMEM] * 6,
         flops=50_000_000,
     )
     got = lax.all_to_all(send, "dom", split_axis=0, concat_axis=0, tiled=True)
@@ -649,7 +675,7 @@
         struct((COARSE, aggregates), F32),
     ]
     sol, coarse_op, coarse_rhs = call(
-        lambda *refs: last_kernel(staying, depth, *refs),
+        lambda *refs: last_kernel(staying, *refs),
         outs,
         [got, local_op, low, pack, sol],
         [pltpu.VMEM] * 5,

time: 32.9 us -> 32.3 us (0.982)
  Pallas kernels: 6.7 us -> 7.24 us
  starting transfers between devices: 5.23 us -> 4.75 us
  blocking collectives: 17.7 us -> 17.3 us
  local copies, waits for them, and re-layouts: 1.31 us -> 0.93 us
    pallas_call x5 -> x6, Pallas kernels: 6.7 us -> 7.24 us  [call(): pl.pallas_call(kernel, out_shape=tuple(outs), in_specs=[pl.BlockSpec(memo...]
    ppermute x4, starting transfers between devices: 5.23 us -> 4.75 us  [the longest x2 4.16 us: exchange(): lax.ppermute(other, 'face', others)]
    all_to_all x1, blocking collectives: 17.7 us -> 17.3 us  [per_device(): got = lax.all_to_all(send, 'dom', split_axis=0, concat_axis=0, tiled=True)]
    unnamed x10, local copies, waits for them, and re-layouts: 1.31 us -> 0.93 us
  transfers between devices with their start and end apart: 4 -> 4, of which waited for: 1 -> 1; matrix products, arithmetic and copies ran while one was open for 0% -> 0% of each run, Pallas kernels for 2% -> 4%
where the time goes in v8:
time: 32.3 us; the launch traced here: 32.1 us
  blocking collectives  17.3 us (54%)
  Pallas kernels  7.24 us (22%)
  starting transfers between devices  4.75 us (15%)
  waiting for transfers between devices  1.18 us (4%)
  local copies, waits for them, and re-layouts  0.93 us (3%)
  between operations  0.72 us (2%)
    all_to_all x1, blocking collectives, per_device(): got = lax.all_to_all(send, 'dom', split_axis=0, concat_axis=0, tiled=True)  17.3 us
    pallas_call x6, Pallas kernels, call(): pl.pallas_call(kernel, out_shape=tuple(outs), in_specs=[pl.BlockSpec(memo...  7.24 us
    ppermute x2, starting transfers between devices, exchange(): lax.ppermute(other, 'face', others)  4.16 us
    ppermute x2, waiting for transfers between devices, exchange(): lax.ppermute(other, 'face', others)  1.18 us
    unnamed x10, local copies, waits for them, and re-layouts  0.93 us
  transfers between devices with their start and end apart: 4, of which 1 were waited for; matrix products, arithmetic and copies ran while one was open for 0% of the time, Pallas kernels for 4%

profile of v8, /device:TPU:0, one launch (start us, length us, event | category | flops | bytes accessed | tf_op | source)
XLA Modules:
  0.0 32.1 jit_solution(6181156415209101435)
XLA Ops:
  0.6 0.0 copy-start
  0.6 0.0 copy-start.1
  0.7 0.0 copy-start.4
  0.7 2.8 %shard_map.121 = (bf16[96,128]{1,0:T(8,128)(2,1)}, bf16[96,128]{1,0:T(8,128)(2,1)}, f32[344,128]{1,0:T(8,128)}) custom-call(bf16[64,64,128]{2,1,0:T(8,128)(2,1)} %diag_ref.3, bf16[64,64,128]{2,1,0:T(8,128)(2,1)} %precond_ref.1, f32[64,128]{1,0:T(8,128)} %refs_2_.1, f32[64,128]{1,0:T(8,128)} %refs_3_.2, f32[6,16,64]{2,1,0:T(8,128)} %refs_4_.1, ...), custom_call_target="tpu_custom_call" | custom-call | flops 100000000 | bytes 2550784 | tf_op jit(solution)/shard_map/pallas_call | solution.py:565
  3.5 0.5 %collective-permute-start = (bf16[96,128]{1,0:T(8,128)(2,1)}, bf16[96,128]{1,0:T(8,128)(2,1)S(1)}, u32[]{:S(2)}, u32[]{:S(2)}) collective-permute-start(bf16[96,128]{1,0:T(8,128)(2,1)} %get-tuple-element.17), channel_id=1, source_target_pairs={{0,1},{1,0},{2,3},{3,2},{4,5},{5,4},{6,7},{7,6},{8,9},{9,8},{10,11... | collective-permute-start | bytes 73736 | tf_op jit(solution)/shard_map/ppermute | solution.py:613
  4.0 2.6 %collective-permute-start.1 = (bf16[96,128]{1,0:T(8,128)(2,1)}, bf16[96,128]{1,0:T(8,128)(2,1)S(1)}, u32[]{:S(2)}, u32[]{:S(2)}) collective-permute-start(bf16[96,128]{1,0:T(8,128)(2,1)} %get-tuple-element.18), channel_id=1, source_target_pairs={{0,3},{1,2},{2,1},{3,0},{4,7},{5,6},{6,5},{7,4},{8,11},{9,10},{10,... | collective-permute-start | bytes 73736 | tf_op jit(solution)/shard_map/ppermute | solution.py:613
  6.7 0.0 copy-done
  6.7 0.0 copy-done.1
  6.7 0.0 copy-done.4
  6.7 0.0 copy-start.2
  6.7 0.9 %copy-done.2 = f32[344,128]{1,0:T(8,128)S(1)} copy-done((f32[344,128]{1,0:T(8,128)S(1)}, f32[344,128]{1,0:T(8,128)}, u32[]{:S(2)}) %copy-start.2) | copy-done | bytes 176152
  7.6 0.0 copy-start.3
  7.6 1.0 %shard_map.122 = (bf16[8,168,128]{2,1,0:T(8,128)(2,1)S(1)}, bf16[768,128]{1,0:T(8,128)(2,1)S(1)}, bf16[448,256]{1,0:T(8,128)(2,1)S(1)}, f32[64,128]{1,0:T(8,128)S(1)}) custom-call(bf16[64,64,128]{2,1,0:T(8,128)(2,1)S(1)} %copy-done.1, bf16[64,64,128]{2,1,0:T(8,128)(2,1)S(1)} %copy-done, f32[344,128]{1,0:T(8,128)S(1)} %copy-done.2, bf16[256,256]{1,0:T(8,128)(2,1)S(1)} %copy-done.4), custom_call_target="tpu_custom_call" | custom-call | flops 1000000000 | bytes 3207168 | tf_op jit(solution)/shard_map/pallas_call | solution.py:565
  8.6 0.0 collective-permute-done.first_ref
  8.6 0.0 collective-permute-done.1.second_ref
  8.6 0.0 copy-done.3
  8.7 1.2 %shard_map.123 = (f32[64,128]{1,0:T(8,128)S(1)}, f32[16,128]{1,0:T(8,128)S(1)}) custom-call(bf16[96,128]{1,0:T(8,128)(2,1)S(1)} %collective-permute-done.first_ref, bf16[96,128]{1,0:T(8,128)(2,1)S(1)} %collective-permute-done.1.second_ref, bf16[64,64,128]{2,1,0:T(8,128)(2,1)S(1)} %copy-done.1, bf16[64,64,128]{2,1,0:T(8,128)(2,1)S(1)} %copy-done, ...), custom_call_target="tpu_custom_call" | custom-call | flops 200000000 | bytes 2396160 | tf_op jit(solution)/shard_map/pallas_call | solution.py:565
  9.9 1.5 %collective-permute-start.3 = (f32[16,128]{1,0:T(8,128)S(1)}, f32[16,128]{1,0:T(8,128)S(1)}, u32[]{:S(2)}, u32[]{:S(2)}) collective-permute-start(f32[16,128]{1,0:T(8,128)S(1)} %get-tuple-element.21), channel_id=1, source_target_pairs={{0,3},{1,2},{2,1},{3,0},{4,7},{5,6},{6,5},{7,4},{8,11},{9,10},{10,... | collective-permute-start | bytes 24584 | tf_op jit(solution)/shard_map/ppermute | solution.py:613
  11.4 0.1 collective-permute-start.2
  11.5 0.4 %shard_map.124.rest_ref = f32[64,128]{1,0:T(8,128)S(1)} custom-call(bf16[64,64,128]{2,1,0:T(8,128)(2,1)S(1)} %copy-done.1, f32[344,128]{1,0:T(8,128)S(1)} %copy-done.3, f32[64,128]{1,0:T(8,128)S(1)} %get-tuple-element.22.sol_ref.refs_4_), custom_call_target="tpu_custom_call" | custom-call | flops 1000000000 | bytes 1290240 | tf_op jit(solution)/shard_map/pallas_call | solution.py:565
  11.8 1.2 %collective-permute-done.3.second_ref = f32[16,128]{1,0:T(8,128)S(1)} collective-permute-done((f32[16,128]{1,0:T(8,128)S(1)}, f32[16,128]{1,0:T(8,128)S(1)}, u32[]{:S(2)}, u32[]{:S(2)}) %collective-permute-start.3) | collective-permute-done | bytes 8224 | tf_op jit(solution)/shard_map/ppermute | solution.py:613
  13.0 0.0 collective-permute-done.2.first_ref
  13.0 0.6 %shard_map.125 = (bf16[64,128]{1,0:T(8,128)(2,1)S(1)}, bf16[8,168,128]{2,1,0:T(8,128)(2,1)S(1)}) custom-call(f32[16,128]{1,0:T(8,128)S(1)} %collective-permute-done.2.first_ref, f32[16,128]{1,0:T(8,128)S(1)} %collective-permute-done.3.second_ref, f32[64,128]{1,0:T(8,128)S(1)} %shard_map.124.rest_ref, f32[344,128]{1,0:T(8,128)S(1)} %copy-done.3, ...), custom_call_target="tpu_custom_call" | custom-call | flops 50000000 | bytes 1159168 | tf_op jit(solution)/shard_map/pallas_call | solution.py:565
  13.6 17.3 %all_to_all.5.refs_0_ = bf16[8,168,128]{2,1,0:T(8,128)(2,1)S(1)} all-to-all(bf16[8,168,128]{2,1,0:T(8,128)(2,1)S(1)} %get-tuple-element.25), channel_id=1, replica_groups=mesh['dom'=8,'face'=4] {'dom'}, dimensions={0} | all-to-all | bytes 688128 | tf_op jit(solution)/shard_map/all_to_all | solution.py:671
  30.9 1.2 %shard_map.126 = (f32[64,128]{1,0:T(8,128)}, f32[64,729]{1,0:T(8,128)}, f32[27,64]{1,0:T(8,128)}) custom-call(bf16[8,168,128]{2,1,0:T(8,128)(2,1)S(1)} %all_to_all.5.refs_0_, bf16[768,128]{1,0:T(8,128)(2,1)S(1)} %get-tuple-element.26.refs_1_, bf16[64,128]{1,0:T(8,128)(2,1)S(1)} %get-tuple-element.27.refs_2_, f32[344,128]{1,0:T(8,128)S(1)} %copy-done.3, ...), custom_call_target="tpu_custom_call" | custom-call | flops 100000000 | bytes 992256 | tf_op jit(solution)/shard_map/pallas_call | solution.py:565
Async XLA Ops:
  0.6 6.0 %copy-start = (bf16[64,64,128]{2,1,0:T(8,128)(2,1)S(1)}, bf16[64,64,128]{2,1,0:T(8,128)(2,1)}, u32[]{:S(2)}) copy-start(bf16[64,64,128]{2,1,0:T(8,128)(2,1)} %precond_ref.1) | copy-start | bytes 3145732
  0.6 6.0 %copy-start.1 = (bf16[64,64,128]{2,1,0:T(8,128)(2,1)S(1)}, bf16[64,64,128]{2,1,0:T(8,128)(2,1)}, u32[]{:S(2)}) copy-start(bf16[64,64,128]{2,1,0:T(8,128)(2,1)} %diag_ref.3) | copy-start | bytes 3145732
  0.7 6.0 %copy-start.4 = (bf16[256,256]{1,0:T(8,128)(2,1)S(1)}, bf16[256,256]{1,0:T(8,128)(2,1)}, u32[]{:S(2)}) copy-start(bf16[256,256]{1,0:T(8,128)(2,1)} %constant.2.clone.refs_9_.refs_3_) | copy-start | bytes 393220
  3.5 5.1 %collective-permute-start = (bf16[96,128]{1,0:T(8,128)(2,1)}, bf16[96,128]{1,0:T(8,128)(2,1)S(1)}, u32[]{:S(2)}, u32[]{:S(2)}) collective-permute-start(bf16[96,128]{1,0:T(8,128)(2,1)} %get-tuple-element.17), channel_id=1, source_target_pairs={{0,1},{1,0},{2,3},{3,2},{4,5},{5,4},{6,7},{7,6},{8,9},{9,8},{10,11... | collective-permute-start | bytes 73736 | tf_op jit(solution)/shard_map/ppermute | solution.py:613
  4.0 4.6 %collective-permute-start.1 = (bf16[96,128]{1,0:T(8,128)(2,1)}, bf16[96,128]{1,0:T(8,128)(2,1)S(1)}, u32[]{:S(2)}, u32[]{:S(2)}) collective-permute-start(bf16[96,128]{1,0:T(8,128)(2,1)} %get-tuple-element.18), channel_id=1, source_target_pairs={{0,3},{1,2},{2,1},{3,0},{4,7},{5,6},{6,5},{7,4},{8,11},{9,10},{10,... | collective-permute-start | bytes 73736 | tf_op jit(solution)/shard_map/ppermute | solution.py:613
  6.7 0.9 %copy-start.2 = (f32[344,128]{1,0:T(8,128)S(1)}, f32[344,128]{1,0:T(8,128)}, u32[]{:S(2)}) copy-start(f32[344,128]{1,0:T(8,128)} %get-tuple-element.19.refs_2_.pack_ref.refs_3_) | copy-start | bytes 528388
  7.6 1.1 %copy-start.3 = (f32[344,128]{1,0:T(8,128)S(1)}, f32[344,128]{1,0:T(8,128)}, u32[]{:S(2)}) copy-start(f32[344,128]{1,0:T(8,128)} %get-tuple-element.19.refs_2_.pack_ref.refs_3_) | copy-start | bytes 528388
  9.9 3.1 %collective-permute-start.3 = (f32[16,128]{1,0:T(8,128)S(1)}, f32[16,128]{1,0:T(8,128)S(1)}, u32[]{:S(2)}, u32[]{:S(2)}) collective-permute-start(f32[16,128]{1,0:T(8,128)S(1)} %get-tuple-element.21), channel_id=1, source_target_pairs={{0,3},{1,2},{2,1},{3,0},{4,7},{5,6},{6,5},{7,4},{8,11},{9,10},{10,... | collective-permute-start | bytes 24584 | tf_op jit(solution)/shard_map/ppermute | solution.py:613
  11.4 1.6 %collective-permute-start.2 = (f32[16,128]{1,0:T(8,128)S(1)}, f32[16,128]{1,0:T(8,128)S(1)}, u32[]{:S(2)}, u32[]{:S(2)}) collective-permute-start(f32[16,128]{1,0:T(8,128)S(1)} %get-tuple-element.21), channel_id=1, source_target_pairs={{0,1},{1,0},{2,3},{3,2},{4,5},{5,4},{6,7},{7,6},{8,9},{9,8},{10,11... | collective-permute-start | bytes 24584 | tf_op jit(solution)/shard_map/ppermute | solution.py:613

commit v9 on v8

--- a/solution.py
+++ b/solution.py
@@ -233,6 +233,7 @@
         self.resid = ref.at[RESID : RESID + NODES]
         self.lift = ref[LIFT : LIFT + NODES]
         self.table = ref[TABLE : TABLE + 32, 0:NODES]
+        self.edge = ref[EDGE : EDGE + 32, 0:NODES]
         self.neighbour = ref[NEIGHBOUR : NEIGHBOUR + FACES].astype(jnp.int32)
         self.orient = ref[ORIENT : ORIENT + FACES].astype(jnp.int32)
         self.owner = ref[OWNER : OWNER + 1].astype(jnp.int32)
@@ -368,7 +369,7 @@
 
 
 def middle_kernel(
-    first_ref, second_ref, diag_ref, precond_ref, pack_ref, partial_ref,
+    first_ref, second_ref, diag_ref, precond_ref, pack_ref, partial_ref, answer_ref,
     new_ref, rim_ref, sol_ref,
 ):
     count = diag_ref.shape[2]
@@ -387,8 +388,14 @@
         at = slice(32 + 16 * q, 48 + 16 * q)
         reply.extend(unfold_lanes(above[at], below[at]))
     below, above = aside(head)
-    delta = halo_lift(below, above, orient_ref, lift)
-    sol_ref[...] = partial_ref[...] + apply_blocks(precond_ref, delta)
+    edge = count // 4
+    low = jnp.where(lanes(shape) < edge, turn(below, orient_ref[2:3]), 0.0)
+    high = jnp.where(lanes(shape) >= count - edge, turn(above, orient_ref[3:4]), 0.0)
+    arrived = low + high
+    for group in range(NODES // 8):
+        parts = [answer_ref[node] * arrived for node in range(8 * group, 8 * group + 8)]
+        at = slice(8 * group, 8 * group + 8)
+        sol_ref[at] = partial_ref[at] + fold([part[:8] + part[8:] for part in parts])
     change = [block * sent for block in reply]
     change = [block[:8] + block[8:] for block in change]
     change = jnp.concatenate([fold(change[:8]), fold(change[8:])], 0)
@@ -400,8 +407,14 @@
     rim_ref[...] = pack_rim(face_traces(new_ref))
 
 
-def rest_kernel(diag_ref, pack_ref, sol_ref, rest_ref):
+def stay_hits(packed, staying, aggregates):
+    shape = (aggregates, packed.slot.shape[1])
+    return one_hot((rows(shape) == packed.slot) & (lanes(shape) < staying))
+
+
+def rest_kernel(staying, diag_ref, pack_ref, sol_ref, local_ref, rest_ref, kept_ref):
     packed = Packed(pack_ref)
+    kept_ref[...] = dot(stay_hits(packed, staying, kept_ref.shape[0]), local_ref[...], NT)
     traces = face_traces(sol_ref)
     none = jnp.zeros(traces[2].shape, F32)
     coupled = coupling(traces, none, none, packed.neighbour, packed.orient, packed.lift)
@@ -454,13 +467,31 @@
 
 def galerkin_kernel(
     staying, capacity, diag_ref, precond_ref, pack_ref, table_ref,
-    send_ref, local_ref, hits_ref, partial_ref, full_ref,
+    send_ref, local_ref, hits_ref, partial_ref, answer_ref, full_ref,
 ):
     line = restrict_line()
     count = diag_ref.shape[2]
     owner_count = send_ref.shape[0]
     packed = Packed(pack_ref)
     partial_ref[...] = packed.start[...] + apply_blocks(precond_ref, packed.resid[...])
+    edge = packed.edge
+    stack = jnp.concatenate([part for lift in (edge[0:16], edge[16:32]) for part in halves(lift)], 0)
+    none = jnp.zeros(stack.shape, BF16)
+    stack = jnp.concatenate(
+        [jnp.concatenate([stack if i == j else none for j in range(GROUP)], 1) for i in range(GROUP)], 0
+    )
+    for first in range(0, NODES, 2 * GROUP):
+        wide = [
+            precond_ref[first + GROUP * j : first + GROUP * j + GROUP].reshape(GROUP * NODES, count)
+            for j in range(2)
+        ]
+        made = dot(stack, jnp.concatenate(wide, 1), NN)
+        for j in range(2):
+            for k in range(GROUP):
+                block = made[64 * k : 64 * k + 64, count * j : count * j + count]
+                answer_ref[first + GROUP * j + k] = both_halves(
+                    (16, count), block[0:16] + block[16:32], block[32:48] + block[48:64]
+                )
     target = packed.target(staying, capacity)
     twice = jnp.concatenate([target, target], 1)
     shape = (2 * capacity, 2 * count)
@@ -506,7 +537,7 @@
 
 
 def last_kernel(
-    staying, got_ref, local_ref, low_ref, pack_ref, sol_ref,
+    staying, got_ref, kept_ref, low_ref, pack_ref, sol_ref,
     sol_out, op_out, rhs_out,
     op_ref, out_ref, sem, op_sem,
 ):
@@ -517,8 +548,7 @@
     owners, size, count = got_ref.shape
     both = size // 3
     capacity = both // 2
-    shape = (aggregates, low_ref.shape[1])
-    stay = one_hot((rows(shape) == packed.slot) & (lanes(shape) < staying))
+    stay = stay_hits(packed, staying, aggregates)
     ids = got_ref[:, 2 * both : size].astype(F32).reshape(owners * both, count)[:, count - 1 : count]
     shape = (owners * both, 2 * aggregates)
     column = lanes(shape)
@@ -536,9 +566,7 @@
         out = []
         for side in range(2):
             at = 128 * (2 * pair + side)
-            out.append(
-                total[aggregates * side : aggregates * side + aggregates] + dot(stay, local_ref[at : at + 128], NT)
-            )
+            out.append(total[aggregates * side : aggregates * side + aggregates] + kept_ref[:, at : at + 128])
         first, last = 256 * pair, min(256 * pair + 256, COARSE * COARSE)
         middle = cut if pair == 2 else first + 128
         op_ref[:, first:middle] = out[0][:, : middle - first]
@@ -632,13 +660,14 @@
         limit=FIRST_LIMIT,
     )
     first, second = exchange(to_first, to_second)
-    made, local_op, hits, partial = call(
+    made, local_op, hits, partial, answer = call(
         lambda *refs: galerkin_kernel(staying, capacity, *refs),
         [
             struct((owner_count, chunk, 128), BF16),
             struct((entries, count), BF16),
             struct((2 * capacity * owner_count, 2 * count), BF16),
             struct((NODES, count), F32),
+            struct((NODES, 16, count), F32),
         ],
         [diag_block, precond, pack, table],
         [pltpu.VMEM] * 4,
@@ -648,17 +677,17 @@
     sol, rim = call(
         middle_kernel,
         [struct((NODES, count), F32), struct((16, count), F32)],
-        [first, second, diag_block, precond, pack, partial],
-        [pltpu.VMEM] * 6,
+        [first, second, diag_block, precond, pack, partial, answer],
+        [pltpu.VMEM] * 7,
         scratch=[pltpu.VMEM((NODES, count), F32)],
         flops=200_000_000,
     )
     first, second = exchange(rim, rim)
-    (rest,) = call(
-        rest_kernel,
-        [struct((NODES, count), F32)],
-        [diag_block, pack, sol],
-        [pltpu.VMEM] * 3,
+    rest, kept = call(
+        lambda *refs: rest_kernel(staying, *refs),
+        [struct((NODES, count), F32), struct((aggregates, entries), F32)],
+        [diag_block, pack, sol, local_op],
+        [pltpu.VMEM] * 4,
         flops=1_000_000_000,
     )
     low, send = call(
@@ -677,7 +706,7 @@
     sol, coarse_op, coarse_rhs = call(
         lambda *refs: last_kernel(staying, *refs),
         outs,
-        [got, local_op, low, pack, sol],
+        [got, kept, low, pack, sol],
         [pltpu.VMEM] * 5,
         [pl.ANY] * 3,
         scratch=[pltpu.VMEM(each.shape, each.dtype) for each in outs[1:]]

time: 32.3 us -> 32.1 us (level)
  starting transfers between devices: 4.75 us -> 4.38 us
  waiting for transfers between devices: 1.18 us -> 1.53 us
    ppermute x2, starting transfers between devices: 4.16 us -> 3.8 us  [exchange(): lax.ppermute(other, 'face', others)]
    ppermute x2, waiting for transfers between devices: 1.18 us -> 1.52 us  [exchange(): lax.ppermute(other, 'face', others)]
  transfers between devices with their start and end apart: 4 -> 4, of which waited for: 1 -> 1; matrix products, arithmetic and copies ran while one was open for 0% -> 0% of each run, Pallas kernels for 4% -> 6%
where the time goes in v9:
time: 32.1 us; the launch traced here: 31.9 us
  blocking collectives  17.1 us (53%)
  Pallas kernels  7.3 us (23%)
  starting transfers between devices  4.38 us (14%)
  waiting for transfers between devices  1.53 us (5%)
  local copies, waits for them, and re-layouts  0.93 us (3%)
  between operations  0.72 us (2%)
    all_to_all x1, blocking collectives, per_device(): got = lax.all_to_all(send, 'dom', split_axis=0, concat_axis=0, tiled=True)  17.1 us
    pallas_call x6, Pallas kernels, call(): pl.pallas_call(kernel, out_shape=tuple(outs), in_specs=[pl.BlockSpec(memo...  7.3 us
    ppermute x2, starting transfers between devices, exchange(): lax.ppermute(other, 'face', others)  3.8 us
    ppermute x2, waiting for transfers between devices, exchange(): lax.ppermute(other, 'face', others)  1.52 us
    unnamed x10, local copies, waits for them, and re-layouts  0.93 us
  transfers between devices with their start and end apart: 4, of which 1 were waited for; matrix products, arithmetic and copies ran while one was open for 0% of the time, Pallas kernels for 6%

profile of v9, /device:TPU:0, one launch (start us, length us, event | category | flops | bytes accessed | tf_op | source)
XLA Modules:
  0.0 31.9 jit_solution(8785291480548112982)
XLA Ops:
  0.6 0.0 copy-start
  0.6 0.0 copy-start.1
  0.7 0.0 copy-start.4
  0.7 2.8 %shard_map.121 = (bf16[96,128]{1,0:T(8,128)(2,1)}, bf16[96,128]{1,0:T(8,128)(2,1)}, f32[344,128]{1,0:T(8,128)}) custom-call(bf16[64,64,128]{2,1,0:T(8,128)(2,1)} %refs_0_.5, bf16[64,64,128]{2,1,0:T(8,128)(2,1)} %precond_ref.1, f32[64,128]{1,0:T(8,128)} %refs_2_.1, f32[64,128]{1,0:T(8,128)} %refs_3_.2, f32[6,16,64]{2,1,0:T(8,128)} %refs_4_.1, ...), custom_call_target="tpu_custom_call" | custom-call | flops 100000000 | bytes 2550784 | tf_op jit(solution)/shard_map/pallas_call | solution.py:593
  3.5 0.5 %collective-permute-start = (bf16[96,128]{1,0:T(8,128)(2,1)}, bf16[96,128]{1,0:T(8,128)(2,1)S(1)}, u32[]{:S(2)}, u32[]{:S(2)}) collective-permute-start(bf16[96,128]{1,0:T(8,128)(2,1)} %get-tuple-element.20), channel_id=1, source_target_pairs={{0,1},{1,0},{2,3},{3,2},{4,5},{5,4},{6,7},{7,6},{8,9},{9,8},{10,11... | collective-permute-start | bytes 73736 | tf_op jit(solution)/shard_map/ppermute | solution.py:641
  4.0 2.6 %collective-permute-start.1 = (bf16[96,128]{1,0:T(8,128)(2,1)}, bf16[96,128]{1,0:T(8,128)(2,1)S(1)}, u32[]{:S(2)}, u32[]{:S(2)}) collective-permute-start(bf16[96,128]{1,0:T(8,128)(2,1)} %get-tuple-element.21), channel_id=1, source_target_pairs={{0,3},{1,2},{2,1},{3,0},{4,7},{5,6},{6,5},{7,4},{8,11},{9,10},{10,... | collective-permute-start | bytes 73736 | tf_op jit(solution)/shard_map/ppermute | solution.py:641
  6.7 0.0 copy-done
  6.7 0.0 copy-done.1
  6.7 0.0 copy-done.4
  6.7 0.0 copy-start.2
  6.7 0.9 %copy-done.2 = f32[344,128]{1,0:T(8,128)S(1)} copy-done((f32[344,128]{1,0:T(8,128)S(1)}, f32[344,128]{1,0:T(8,128)}, u32[]{:S(2)}) %copy-start.2) | copy-done | bytes 176152
  7.6 0.0 copy-start.3
  7.6 1.4 %shard_map.122 = (bf16[8,168,128]{2,1,0:T(8,128)(2,1)S(1)}, bf16[768,128]{1,0:T(8,128)(2,1)S(1)}, bf16[448,256]{1,0:T(8,128)(2,1)S(1)}, f32[64,128]{1,0:T(8,128)S(1)}, f32[64,16,128]{2,1,0:T(8,128)S(1)}) custom-call(bf16[64,64,128]{2,1,0:T(8,128)(2,1)S(1)} %copy-done.1, bf16[64,64,128]{2,1,0:T(8,128)(2,1)S(1)} %copy-done, f32[344,128]{1,0:T(8,128)S(1)} %copy-done.2, ...), custom_call_target="tpu_custom_call" | custom-call | flops 1000000000 | bytes 3731456 | tf_op jit(solution)/shard_map/pallas_call | solution.py:593
  9.0 0.0 collective-permute-done.first_ref
  9.0 0.0 collective-permute-done.1.second_ref
  9.0 0.0 copy-done.3
  9.0 0.9 %shard_map.123 = (f32[64,128]{1,0:T(8,128)S(1)}, f32[16,128]{1,0:T(8,128)S(1)}) custom-call(bf16[96,128]{1,0:T(8,128)(2,1)S(1)} %collective-permute-done.first_ref, bf16[96,128]{1,0:T(8,128)(2,1)S(1)} %collective-permute-done.1.second_ref, bf16[64,64,128]{2,1,0:T(8,128)(2,1)S(1)} %copy-done.1, bf16[64,64,128]{2,1,0:T(8,128)(2,1)S(1)} %copy-done, ...), custom_call_target="tpu_custom_call" | custom-call | flops 200000000 | bytes 2920448 | tf_op jit(solution)/shard_map/pallas_call | solution.py:593
  10.0 1.2 %collective-permute-start.3 = (f32[16,128]{1,0:T(8,128)S(1)}, f32[16,128]{1,0:T(8,128)S(1)}, u32[]{:S(2)}, u32[]{:S(2)}) collective-permute-start(f32[16,128]{1,0:T(8,128)S(1)} %get-tuple-element.25), channel_id=1, source_target_pairs={{0,3},{1,2},{2,1},{3,0},{4,7},{5,6},{6,5},{7,4},{8,11},{9,10},{10,... | collective-permute-start | bytes 24584 | tf_op jit(solution)/shard_map/ppermute | solution.py:641
  11.1 0.1 collective-permute-start.2
  11.2 0.4 %shard_map.124 = (f32[64,128]{1,0:T(8,128)S(1)}, f32[64,768]{1,0:T(8,128)S(1)}) custom-call(bf16[64,64,128]{2,1,0:T(8,128)(2,1)S(1)} %copy-done.1, f32[344,128]{1,0:T(8,128)S(1)} %copy-done.3, f32[64,128]{1,0:T(8,128)S(1)} %get-tuple-element.26.refs_2_.refs_4_, bf16[768,128]{1,0:T(8,128)(2,1)S(1)} %get-tuple-element.27.refs_3_), custom_call_target="tpu_custom_call" | custom-call | flops 1000000000 | bytes 1683456 | tf_op jit(solution)/shard_map/pallas_call | solution.py:593
  11.6 1.5 %collective-permute-done.3.second_ref = f32[16,128]{1,0:T(8,128)S(1)} collective-permute-done((f32[16,128]{1,0:T(8,128)S(1)}, f32[16,128]{1,0:T(8,128)S(1)}, u32[]{:S(2)}, u32[]{:S(2)}) %collective-permute-start.3) | collective-permute-done | bytes 8224 | tf_op jit(solution)/shard_map/ppermute | solution.py:641
  13.1 0.0 collective-permute-done.2.first_ref
  13.1 0.6 %shard_map.125 = (bf16[64,128]{1,0:T(8,128)(2,1)S(1)}, bf16[8,168,128]{2,1,0:T(8,128)(2,1)S(1)}) custom-call(f32[16,128]{1,0:T(8,128)S(1)} %collective-permute-done.2.first_ref, f32[16,128]{1,0:T(8,128)S(1)} %collective-permute-done.3.second_ref, f32[64,128]{1,0:T(8,128)S(1)} %get-tuple-element.28.rest_ref, f32[344,128]{1,0:T(8,128)S(1)} %copy-done.3, ...), custom_call_target="tpu_custom_call" | custom-call | flops 50000000 | bytes 1159168 | tf_op jit(solution)/shard_map/pallas_call | solution.py:593
  13.7 17.1 %all_to_all.5.refs_0_ = bf16[8,168,128]{2,1,0:T(8,128)(2,1)S(1)} all-to-all(bf16[8,168,128]{2,1,0:T(8,128)(2,1)S(1)} %get-tuple-element.31), channel_id=1, replica_groups=mesh['dom'=8,'face'=4] {'dom'}, dimensions={0} | all-to-all | bytes 688128 | tf_op jit(solution)/shard_map/all_to_all | solution.py:700
  30.8 1.2 %shard_map.126 = (f32[64,128]{1,0:T(8,128)}, f32[64,729]{1,0:T(8,128)}, f32[27,64]{1,0:T(8,128)}) custom-call(bf16[8,168,128]{2,1,0:T(8,128)(2,1)S(1)} %all_to_all.5.refs_0_, f32[64,768]{1,0:T(8,128)S(1)} %get-tuple-element.32.refs_1_, bf16[64,128]{1,0:T(8,128)(2,1)S(1)} %get-tuple-element.33.refs_2_, f32[344,128]{1,0:T(8,128)S(1)} %copy-done.3, ...), custom_call_target="tpu_custom_call" | custom-call | flops 100000000 | bytes 992256 | tf_op jit(solution)/shard_map/pallas_call | solution.py:593
Async XLA Ops:
  0.6 6.0 %copy-start = (bf16[64,64,128]{2,1,0:T(8,128)(2,1)S(1)}, bf16[64,64,128]{2,1,0:T(8,128)(2,1)}, u32[]{:S(2)}) copy-start(bf16[64,64,128]{2,1,0:T(8,128)(2,1)} %precond_ref.1) | copy-start | bytes 3145732
  0.6 6.0 %copy-start.1 = (bf16[64,64,128]{2,1,0:T(8,128)(2,1)S(1)}, bf16[64,64,128]{2,1,0:T(8,128)(2,1)}, u32[]{:S(2)}) copy-start(bf16[64,64,128]{2,1,0:T(8,128)(2,1)} %refs_0_.5) | copy-start | bytes 3145732
  0.7 6.0 %copy-start.4 = (bf16[256,256]{1,0:T(8,128)(2,1)S(1)}, bf16[256,256]{1,0:T(8,128)(2,1)}, u32[]{:S(2)}) copy-start(bf16[256,256]{1,0:T(8,128)(2,1)} %constant.2.clone.refs_9_.refs_3_) | copy-start | bytes 393220
  3.5 5.5 %collective-permute-start = (bf16[96,128]{1,0:T(8,128)(2,1)}, bf16[96,128]{1,0:T(8,128)(2,1)S(1)}, u32[]{:S(2)}, u32[]{:S(2)}) collective-permute-start(bf16[96,128]{1,0:T(8,128)(2,1)} %get-tuple-element.20), channel_id=1, source_target_pairs={{0,1},{1,0},{2,3},{3,2},{4,5},{5,4},{6,7},{7,6},{8,9},{9,8},{10,11... | collective-permute-start | bytes 73736 | tf_op jit(solution)/shard_map/ppermute | solution.py:641
  4.0 5.0 %collective-permute-start.1 = (bf16[96,128]{1,0:T(8,128)(2,1)}, bf16[96,128]{1,0:T(8,128)(2,1)S(1)}, u32[]{:S(2)}, u32[]{:S(2)}) collective-permute-start(bf16[96,128]{1,0:T(8,128)(2,1)} %get-tuple-element.21), channel_id=1, source_target_pairs={{0,3},{1,2},{2,1},{3,0},{4,7},{5,6},{6,5},{7,4},{8,11},{9,10},{10,... | collective-permute-start | bytes 73736 | tf_op jit(solution)/shard_map/ppermute | solution.py:641
  6.7 0.9 %copy-start.2 = (f32[344,128]{1,0:T(8,128)S(1)}, f32[344,128]{1,0:T(8,128)}, u32[]{:S(2)}) copy-start(f32[344,128]{1,0:T(8,128)} %get-tuple-element.22.refs_2_.pack_ref.refs_1_.refs_3_) | copy-start | bytes 528388
  7.6 1.4 %copy-start.3 = (f32[344,128]{1,0:T(8,128)S(1)}, f32[344,128]{1,0:T(8,128)}, u32[]{:S(2)}) copy-start(f32[344,128]{1,0:T(8,128)} %get-tuple-element.22.refs_2_.pack_ref.refs_1_.refs_3_) | copy-start | bytes 528388
  10.0 3.1 %collective-permute-start.3 = (f32[16,128]{1,0:T(8,128)S(1)}, f32[16,128]{1,0:T(8,128)S(1)}, u32[]{:S(2)}, u32[]{:S(2)}) collective-permute-start(f32[16,128]{1,0:T(8,128)S(1)} %get-tuple-element.25), channel_id=1, source_target_pairs={{0,3},{1,2},{2,1},{3,0},{4,7},{5,6},{6,5},{7,4},{8,11},{9,10},{10,... | collective-permute-start | bytes 24584 | tf_op jit(solution)/shard_map/ppermute | solution.py:641
  11.1 2.0 %collective-permute-start.2 = (f32[16,128]{1,0:T(8,128)S(1)}, f32[16,128]{1,0:T(8,128)S(1)}, u32[]{:S(2)}, u32[]{:S(2)}) collective-permute-start(f32[16,128]{1,0:T(8,128)S(1)} %get-tuple-element.25), channel_id=1, source_target_pairs={{0,1},{1,0},{2,3},{3,2},{4,5},{5,4},{6,7},{7,6},{8,9},{9,8},{10,11... | collective-permute-start | bytes 24584 | tf_op jit(solution)/shard_map/ppermute | solution.py:641

commit v10 on v9

--- a/solution.py
+++ b/solution.py
@@ -158,6 +158,20 @@
     for group in range(NODES // 8):
         out.append(fold([block_row(ref, node, tiles) for node in range(8 * group, 8 * group + 8)]))
     return jnp.concatenate(out, 0)
+
+
+def rim_change(ref, resid):
+    count = resid.shape[1]
+    tiles = resid.reshape(NODES // 8, 8, count)
+    steps = []
+    for i in range(4):
+        nodes = [16 * i + k for k in range(4)] + [16 * i + 12 + k for k in range(4)]
+        steps.append(fold([block_row(ref, node, tiles) for node in nodes]))
+    return both_halves(
+        (16, count),
+        jnp.concatenate([step[0:4] for step in steps], 0),
+        jnp.concatenate([step[4:8] for step in steps], 0),
+    )
 
 
 def pack_rim(traces):
@@ -304,16 +318,7 @@
     reply = response(precond_ref, stacked[32:64])
     for q in range(4):
         write(32 + 16 * q, reply[GROUP * q : GROUP * q + GROUP])
-    tiles = resid.reshape(NODES // 8, 8, count)
-    steps = []
-    for i in range(4):
-        nodes = [16 * i + k for k in range(4)] + [16 * i + 12 + k for k in range(4)]
-        steps.append(fold([block_row(precond_ref, node, tiles) for node in nodes]))
-    change = both_halves(
-        shape,
-        jnp.concatenate([step[0:4] for step in steps], 0),
-        jnp.concatenate([step[4:8] for step in steps], 0),
-    )
+    change = rim_change(precond_ref, resid)
     parts = []
     for values in (pack_rim(traces), pack_rim(traces) + change):
         high, low = halves(values)
@@ -370,7 +375,7 @@
 
 def middle_kernel(
     first_ref, second_ref, diag_ref, precond_ref, pack_ref, partial_ref, answer_ref,
-    new_ref, rim_ref, sol_ref,
+    sol_ref, resid_ref, rim_ref,
 ):
     count = diag_ref.shape[2]
     shape = (16, count)
@@ -403,8 +408,8 @@
     traces = face_traces(sol_ref)
     coupled = coupling(traces, below, above, neighbour_ref, orient_ref, lift)
     resid = rhs_ref[...] - (apply_blocks(diag_ref, sol_ref[...]) - coupled)
-    new_ref[...] = sol_ref[...] + apply_blocks(precond_ref, resid)
-    rim_ref[...] = pack_rim(face_traces(new_ref))
+    rim_ref[...] = pack_rim(traces) + rim_change(precond_ref, resid)
+    resid_ref[...] = resid
 
 
 def stay_hits(packed, staying, aggregates):
@@ -412,8 +417,12 @@
     return one_hot((rows(shape) == packed.slot) & (lanes(shape) < staying))
 
 
-def rest_kernel(staying, diag_ref, pack_ref, sol_ref, local_ref, rest_ref, kept_ref):
+def rest_kernel(
+    staying, diag_ref, precond_ref, pack_ref, before_ref, resid_ref, local_ref,
+    sol_ref, rest_ref, kept_ref,
+):
     packed = Packed(pack_ref)
+    sol_ref[...] = before_ref[...] + apply_blocks(precond_ref, resid_ref[...])
     kept_ref[...] = dot(stay_hits(packed, staying, kept_ref.shape[0]), local_ref[...], NT)
     traces = face_traces(sol_ref)
     none = jnp.zeros(traces[2].shape, F32)
@@ -674,20 +683,19 @@
         scratch=[pltpu.VMEM((entries, count), F32)],
         flops=1_000_000_000,
     )
-    sol, rim = call(
+    sol, resid, rim = call(
         middle_kernel,
-        [struct((NODES, count), F32), struct((16, count), F32)],
+        [struct((NODES, count), F32), struct((NODES, count), F32), struct((16, count), F32)],
         [first, second, diag_block, precond, pack, partial, answer],
         [pltpu.VMEM] * 7,
-        scratch=[pltpu.VMEM((NODES, count), F32)],
         flops=200_000_000,
     )
     first, second = exchange(rim, rim)
-    rest, kept = call(
+    sol, rest, kept = call(
         lambda *refs: rest_kernel(staying, *refs),
-        [struct((NODES, count), F32), struct((aggregates, entries), F32)],
-        [diag_block, pack, sol, local_op],
-        [pltpu.VMEM] * 4,
+        [struct((NODES, count), F32), struct((NODES, count), F32), struct((aggregates, entries), F32)],
+        [diag_block, precond, pack, sol, resid, local_op],
+        [pltpu.VMEM] * 6,
         flops=1_000_000_000,
     )
     low, send = call(

time: 32.1 us -> 31.9 us (level)
  no operation moved by 1% of the time
where the time goes in v10:
time: 31.9 us; the launch traced here: 31.7 us
  blocking collectives  17.1 us (54%)
  Pallas kernels  7.27 us (23%)
  starting transfers between devices  4.38 us (14%)
  waiting for transfers between devices  1.29 us (4%)
  local copies, waits for them, and re-layouts  0.93 us (3%)
  between operations  0.72 us (2%)
    all_to_all x1, blocking collectives, per_device(): got = lax.all_to_all(send, 'dom', split_axis=0, concat_axis=0, tiled=True)  17.1 us
    pallas_call x6, Pallas kernels, call(): pl.pallas_call(kernel, out_shape=tuple(outs), in_specs=[pl.BlockSpec(memo...  7.27 us
    ppermute x2, starting transfers between devices, exchange(): lax.ppermute(other, 'face', others)  3.8 us
    ppermute x2, waiting for transfers between devices, exchange(): lax.ppermute(other, 'face', others)  1.29 us
    unnamed x10, local copies, waits for them, and re-layouts  0.93 us
  transfers between devices with their start and end apart: 4, of which 1 were waited for; matrix products, arithmetic and copies ran while one was open for 0% of the time, Pallas kernels for 6%

profile of v10, /device:TPU:0, one launch (start us, length us, event | category | flops | bytes accessed | tf_op | source)
XLA Modules:
  0.0 31.7 jit_solution(3791027143257884048)
XLA Ops:
  0.6 0.0 copy-start
  0.6 0.0 copy-start.1
  0.7 0.0 copy-start.4
  0.7 2.8 %shard_map.121 = (bf16[96,128]{1,0:T(8,128)(2,1)}, bf16[96,128]{1,0:T(8,128)(2,1)}, f32[344,128]{1,0:T(8,128)}) custom-call(bf16[64,64,128]{2,1,0:T(8,128)(2,1)} %refs_0_.5, bf16[64,64,128]{2,1,0:T(8,128)(2,1)} %refs_1_.5, f32[64,128]{1,0:T(8,128)} %refs_2_.1, f32[64,128]{1,0:T(8,128)} %refs_3_.2, f32[6,16,64]{2,1,0:T(8,128)} %refs_4_.1, s32[6,128]{1,0:T(8,128)} %refs_5_.1, ...), custom_call_target="tpu_custom_call" | custom-call | flops 100000000 | bytes 2550784 | tf_op jit(solution)/shard_map/pallas_call | solution.py:602
  3.5 0.5 %collective-permute-start = (bf16[96,128]{1,0:T(8,128)(2,1)}, bf16[96,128]{1,0:T(8,128)(2,1)S(1)}, u32[]{:S(2)}, u32[]{:S(2)}) collective-permute-start(bf16[96,128]{1,0:T(8,128)(2,1)} %get-tuple-element.22), channel_id=1, source_target_pairs={{0,1},{1,0},{2,3},{3,2},{4,5},{5,4},{6,7},{7,6},{8,9},{9,8},{10,11... | collective-permute-start | bytes 73736 | tf_op jit(solution)/shard_map/ppermute | solution.py:650
  4.0 2.6 %collective-permute-start.1 = (bf16[96,128]{1,0:T(8,128)(2,1)}, bf16[96,128]{1,0:T(8,128)(2,1)S(1)}, u32[]{:S(2)}, u32[]{:S(2)}) collective-permute-start(bf16[96,128]{1,0:T(8,128)(2,1)} %get-tuple-element.23), channel_id=1, source_target_pairs={{0,3},{1,2},{2,1},{3,0},{4,7},{5,6},{6,5},{7,4},{8,11},{9,10},{10,... | collective-permute-start | bytes 73736 | tf_op jit(solution)/shard_map/ppermute | solution.py:650
  6.7 0.0 copy-done
  6.7 0.0 copy-done.1
  6.7 0.0 copy-done.4
  6.7 0.0 copy-start.2
  6.7 0.9 %copy-done.2 = f32[344,128]{1,0:T(8,128)S(1)} copy-done((f32[344,128]{1,0:T(8,128)S(1)}, f32[344,128]{1,0:T(8,128)}, u32[]{:S(2)}) %copy-start.2) | copy-done | bytes 176152
  7.6 0.0 copy-start.3
  7.6 1.4 %shard_map.122 = (bf16[8,168,128]{2,1,0:T(8,128)(2,1)S(1)}, bf16[768,128]{1,0:T(8,128)(2,1)S(1)}, bf16[448,256]{1,0:T(8,128)(2,1)S(1)}, f32[64,128]{1,0:T(8,128)S(1)}, f32[64,16,128]{2,1,0:T(8,128)S(1)}) custom-call(bf16[64,64,128]{2,1,0:T(8,128)(2,1)S(1)} %copy-done, bf16[64,64,128]{2,1,0:T(8,128)(2,1)S(1)} %copy-done.1, f32[344,128]{1,0:T(8,128)S(1)} %copy-done.2, ...), custom_call_target="tpu_custom_call" | custom-call | flops 1000000000 | bytes 3731456 | tf_op jit(solution)/shard_map/pallas_call | solution.py:602
  9.0 0.0 collective-permute-done.first_ref
  9.0 0.0 collective-permute-done.1.second_ref
  9.0 0.0 copy-done.3
  9.0 0.7 %shard_map.123 = (f32[64,128]{1,0:T(8,128)S(1)}, f32[64,128]{1,0:T(8,128)S(1)}, f32[16,128]{1,0:T(8,128)S(1)}) custom-call(bf16[96,128]{1,0:T(8,128)(2,1)S(1)} %collective-permute-done.first_ref, bf16[96,128]{1,0:T(8,128)(2,1)S(1)} %collective-permute-done.1.second_ref, bf16[64,64,128]{2,1,0:T(8,128)(2,1)S(1)} %copy-done, ...), custom_call_target="tpu_custom_call" | custom-call | flops 200000000 | bytes 2953216 | tf_op jit(solution)/shard_map/pallas_call | solution.py:602
  9.7 1.2 %collective-permute-start.3 = (f32[16,128]{1,0:T(8,128)S(1)}, f32[16,128]{1,0:T(8,128)S(1)}, u32[]{:S(2)}, u32[]{:S(2)}) collective-permute-start(f32[16,128]{1,0:T(8,128)S(1)} %get-tuple-element.27), channel_id=1, source_target_pairs={{0,3},{1,2},{2,1},{3,0},{4,7},{5,6},{6,5},{7,4},{8,11},{9,10},{10,... | collective-permute-start | bytes 24584 | tf_op jit(solution)/shard_map/ppermute | solution.py:650
  10.9 0.1 collective-permute-start.2
  10.9 0.6 %shard_map.124 = (f32[64,128]{1,0:T(8,128)S(1)}, f32[64,128]{1,0:T(8,128)S(1)}, f32[64,768]{1,0:T(8,128)S(1)}) custom-call(bf16[64,64,128]{2,1,0:T(8,128)(2,1)S(1)} %copy-done, bf16[64,64,128]{2,1,0:T(8,128)(2,1)S(1)} %copy-done.1, f32[344,128]{1,0:T(8,128)S(1)} %copy-done.3, f32[64,128]{1,0:T(8,128)S(1)} %get-tuple-element.28.refs_3_, ...), custom_call_target="tpu_custom_call" | custom-call | flops 1000000000 | bytes 2797568 | tf_op jit(solution)/shard_map/pallas_call | solution.py:602
  11.6 1.3 %collective-permute-done.3.second_ref = f32[16,128]{1,0:T(8,128)S(1)} collective-permute-done((f32[16,128]{1,0:T(8,128)S(1)}, f32[16,128]{1,0:T(8,128)S(1)}, u32[]{:S(2)}, u32[]{:S(2)}) %collective-permute-start.3) | collective-permute-done | bytes 8224 | tf_op jit(solution)/shard_map/ppermute | solution.py:650
  12.9 0.0 collective-permute-done.2.first_ref
  12.9 0.6 %shard_map.125 = (bf16[64,128]{1,0:T(8,128)(2,1)S(1)}, bf16[8,168,128]{2,1,0:T(8,128)(2,1)S(1)}) custom-call(f32[16,128]{1,0:T(8,128)S(1)} %collective-permute-done.2.first_ref, f32[16,128]{1,0:T(8,128)S(1)} %collective-permute-done.3.second_ref, f32[64,128]{1,0:T(8,128)S(1)} %get-tuple-element.31.rest_ref, f32[344,128]{1,0:T(8,128)S(1)} %copy-done.3, ...), custom_call_target="tpu_custom_call" | custom-call | flops 50000000 | bytes 1159168 | tf_op jit(solution)/shard_map/pallas_call | solution.py:602
  13.4 17.1 %all_to_all.5.refs_0_ = bf16[8,168,128]{2,1,0:T(8,128)(2,1)S(1)} all-to-all(bf16[8,168,128]{2,1,0:T(8,128)(2,1)S(1)} %get-tuple-element.34), channel_id=1, replica_groups=mesh['dom'=8,'face'=4] {'dom'}, dimensions={0} | all-to-all | bytes 688128 | tf_op jit(solution)/shard_map/all_to_all | solution.py:708
  30.5 1.2 %shard_map.126 = (f32[64,128]{1,0:T(8,128)}, f32[64,729]{1,0:T(8,128)}, f32[27,64]{1,0:T(8,128)}) custom-call(bf16[8,168,128]{2,1,0:T(8,128)(2,1)S(1)} %all_to_all.5.refs_0_, f32[64,768]{1,0:T(8,128)S(1)} %get-tuple-element.35.refs_1_, bf16[64,128]{1,0:T(8,128)(2,1)S(1)} %get-tuple-element.36.refs_2_, f32[344,128]{1,0:T(8,128)S(1)} %copy-done.3, ...), custom_call_target="tpu_custom_call" | custom-call | flops 100000000 | bytes 992256 | tf_op jit(solution)/shard_map/pallas_call | solution.py:602
Async XLA Ops:
  0.6 6.0 %copy-start = (bf16[64,64,128]{2,1,0:T(8,128)(2,1)S(1)}, bf16[64,64,128]{2,1,0:T(8,128)(2,1)}, u32[]{:S(2)}) copy-start(bf16[64,64,128]{2,1,0:T(8,128)(2,1)} %refs_0_.5) | copy-start | bytes 3145732
  0.6 6.0 %copy-start.1 = (bf16[64,64,128]{2,1,0:T(8,128)(2,1)S(1)}, bf16[64,64,128]{2,1,0:T(8,128)(2,1)}, u32[]{:S(2)}) copy-start(bf16[64,64,128]{2,1,0:T(8,128)(2,1)} %refs_1_.5) | copy-start | bytes 3145732
  0.7 6.0 %copy-start.4 = (bf16[256,256]{1,0:T(8,128)(2,1)S(1)}, bf16[256,256]{1,0:T(8,128)(2,1)}, u32[]{:S(2)}) copy-start(bf16[256,256]{1,0:T(8,128)(2,1)} %constant.2.clone.refs_9_.refs_3_) | copy-start | bytes 393220
  3.5 5.5 %collective-permute-start = (bf16[96,128]{1,0:T(8,128)(2,1)}, bf16[96,128]{1,0:T(8,128)(2,1)S(1)}, u32[]{:S(2)}, u32[]{:S(2)}) collective-permute-start(bf16[96,128]{1,0:T(8,128)(2,1)} %get-tuple-element.22), channel_id=1, source_target_pairs={{0,1},{1,0},{2,3},{3,2},{4,5},{5,4},{6,7},{7,6},{8,9},{9,8},{10,11... | collective-permute-start | bytes 73736 | tf_op jit(solution)/shard_map/ppermute | solution.py:650
  4.0 5.0 %collective-permute-start.1 = (bf16[96,128]{1,0:T(8,128)(2,1)}, bf16[96,128]{1,0:T(8,128)(2,1)S(1)}, u32[]{:S(2)}, u32[]{:S(2)}) collective-permute-start(bf16[96,128]{1,0:T(8,128)(2,1)} %get-tuple-element.23), channel_id=1, source_target_pairs={{0,3},{1,2},{2,1},{3,0},{4,7},{5,6},{6,5},{7,4},{8,11},{9,10},{10,... | collective-permute-start | bytes 73736 | tf_op jit(solution)/shard_map/ppermute | solution.py:650
  6.7 0.9 %copy-start.2 = (f32[344,128]{1,0:T(8,128)S(1)}, f32[344,128]{1,0:T(8,128)}, u32[]{:S(2)}) copy-start(f32[344,128]{1,0:T(8,128)} %get-tuple-element.24.refs_2_.pack_ref.refs_3_) | copy-start | bytes 528388
  7.6 1.4 %copy-start.3 = (f32[344,128]{1,0:T(8,128)S(1)}, f32[344,128]{1,0:T(8,128)}, u32[]{:S(2)}) copy-start(f32[344,128]{1,0:T(8,128)} %get-tuple-element.24.refs_2_.pack_ref.refs_3_) | copy-start | bytes 528388
  9.7 3.1 %collective-permute-start.3 = (f32[16,128]{1,0:T(8,128)S(1)}, f32[16,128]{1,0:T(8,128)S(1)}, u32[]{:S(2)}, u32[]{:S(2)}) collective-permute-start(f32[16,128]{1,0:T(8,128)S(1)} %get-tuple-element.27), channel_id=1, source_target_pairs={{0,3},{1,2},{2,1},{3,0},{4,7},{5,6},{6,5},{7,4},{8,11},{9,10},{10,... | collective-permute-start | bytes 24584 | tf_op jit(solution)/shard_map/ppermute | solution.py:650
  10.9 2.0 %collective-permute-start.2 = (f32[16,128]{1,0:T(8,128)S(1)}, f32[16,128]{1,0:T(8,128)S(1)}, u32[]{:S(2)}, u32[]{:S(2)}) collective-permute-start(f32[16,128]{1,0:T(8,128)S(1)} %get-tuple-element.27), channel_id=1, source_target_pairs={{0,1},{1,0},{2,3},{3,2},{4,5},{5,4},{6,7},{7,6},{8,9},{9,8},{10,11... | collective-permute-start | bytes 24584 | tf_op jit(solution)/shard_map/ppermute | solution.py:650

commit v11 on v10

--- a/solution.py
+++ b/solution.py
@@ -232,7 +232,8 @@
 LIFT = 3 * NODES
 EDGE = LIFT + NODES
 TABLE = EDGE + 32
-NEIGHBOUR = TABLE + 32
+SIDE = TABLE + 32
+NEIGHBOUR = SIDE + 32
 ORIENT = NEIGHBOUR + 8
 OWNER = ORIENT + 8
 RANK = OWNER + 1
@@ -248,6 +249,7 @@
         self.lift = ref[LIFT : LIFT + NODES]
         self.table = ref[TABLE : TABLE + 32, 0:NODES]
         self.edge = ref[EDGE : EDGE + 32, 0:NODES]
+        self.side = ref[SIDE : SIDE + 32]
         self.neighbour = ref[NEIGHBOUR : NEIGHBOUR + FACES].astype(jnp.int32)
         self.orient = ref[ORIENT : ORIENT + FACES].astype(jnp.int32)
         self.owner = ref[OWNER : OWNER + 1].astype(jnp.int32)
@@ -287,7 +289,10 @@
     lift = jnp.concatenate([stacked, jnp.zeros((count - FACES * 16, NODES), F32)], 0).T
     pack_ref[LIFT : LIFT + NODES] = lift
     pack_ref[EDGE : EDGE + 32, 0:NODES] = stacked[32:64]
-    pack_ref[TABLE : TABLE + 32, 0:NODES] = small_table()
+    table = small_table()
+    pack_ref[TABLE : TABLE + 32, 0:NODES] = table
+    high_side = jnp.concatenate([stacked[48:64], jnp.zeros((count - 16, NODES), F32)], 0)
+    pack_ref[SIDE : SIDE + 32] = dot_split(table, halves(high_side.T))
     pack_ref[NEIGHBOUR : NEIGHBOUR + FACES] = neighbour_ref[...].astype(F32)
     pack_ref[ORIENT : ORIENT + FACES] = orient_ref[...].astype(F32)
     owner = owner_ref[...]
@@ -418,8 +423,8 @@
 
 
 def rest_kernel(
-    staying, diag_ref, precond_ref, pack_ref, before_ref, resid_ref, local_ref,
-    sol_ref, rest_ref, kept_ref,
+    staying, diag_ref, precond_ref, pack_ref, before_ref, resid_ref, local_ref, made_ref, hits_ref,
+    sol_ref, rest_ref, kept_ref, send_ref,
 ):
     packed = Packed(pack_ref)
     sol_ref[...] = before_ref[...] + apply_blocks(precond_ref, resid_ref[...])
@@ -427,27 +432,38 @@
     traces = face_traces(sol_ref)
     none = jnp.zeros(traces[2].shape, F32)
     coupled = coupling(traces, none, none, packed.neighbour, packed.orient, packed.lift)
-    rest_ref[...] = packed.rhs[...] - (apply_blocks(diag_ref, sol_ref[...]) - coupled)
-
-
-def send_kernel(first_ref, second_ref, rest_ref, pack_ref, made_ref, hits_ref, low_ref, send_ref):
+    rest = packed.rhs[...] - (apply_blocks(diag_ref, sol_ref[...]) - coupled)
+    rest_ref[...] = rest
+    owners, size, count = made_ref.shape
+    both = size // 3
+    high, low = halves(rest)
+    low = jnp.where(lanes(low.shape) >= count - count // 4, low.astype(F32), 0.0).astype(BF16)
+    made = dot_split(packed.table, (high, low)).astype(BF16)
+    extra = dot(hits_ref[...], spread(made), NT).reshape(owners, both, count)
+    send_ref[:, 0 : 2 * both] = made_ref[:, 0 : 2 * both]
+    send_ref[:, 2 * both :] = (made_ref[:, 2 * both :].astype(F32) + extra).astype(BF16)
+
+
+def spread(made):
+    none = jnp.zeros((made.shape[1] - 16, made.shape[1]), made.dtype)
+    return jnp.concatenate(
+        [jnp.concatenate([none, made[:16]], 0), jnp.concatenate([none, made[16:]], 0)], 1
+    )
+
+
+def send_kernel(first_ref, second_ref, rest_ref, pack_ref, hits_ref, made_ref, low_ref, send_ref):
     packed = Packed(pack_ref)
     owners, size, count = made_ref.shape
     both = size // 3
+    edge = count // 4
     above, below = sides(first_ref[...], second_ref[...])
     below, above = aside(below)[0], aside(above)[1]
-    low = (rest_ref[...] + halo_lift(below, above, packed.orient, packed.lift)).astype(BF16)
-    low_ref[...] = low
-    table_high, table_low = halves(packed.table)
-    made = dot(jnp.concatenate([table_high, table_low], 0), low, NN)
-    made = (made[:32] + made[32:]).astype(BF16)
-    none = jnp.zeros((count - 16, count), BF16)
-    wide = jnp.concatenate(
-        [jnp.concatenate([none, made[:16]], 0), jnp.concatenate([none, made[16:]], 0)], 1
-    )
-    extra = dot(hits_ref[...], wide, NT).reshape(owners, both, count)
-    send_ref[:, 0 : 2 * both] = made_ref[:, 0 : 2 * both]
+    high = jnp.where(lanes(above.shape) >= count - edge, turn(above, packed.orient[3:4]), 0.0)
+    high = jnp.concatenate([high, jnp.zeros((count - 16, count), F32)], 0)
+    lifted = dot_split(packed.side, halves(high)).astype(BF16)
+    extra = dot(hits_ref[...], spread(lifted), NT).reshape(owners, both, count)
     send_ref[:, 2 * both :] = (made_ref[:, 2 * both :].astype(F32) + extra).astype(BF16)
+    low_ref[...] = (rest_ref[...] + halo_lift(below, above, packed.orient, packed.lift)).astype(BF16)
 
 
 def rank_row(owner_row, staying, owner_count):
@@ -595,7 +611,7 @@
         copy.wait()
 
 
-def call(kernel, outs, args, spaces, out_spaces=None, scratch=(), flops=0, limit=VMEM_LIMIT):
+def call(kernel, outs, args, spaces, out_spaces=None, scratch=(), flops=0, limit=VMEM_LIMIT, aliases=None):
     bytes_in = sum(a.size * a.dtype.itemsize for a in args)
     bytes_out = sum(o.size * o.dtype.itemsize for o in outs)
     out_spaces = out_spaces or [pltpu.VMEM] * len(outs)
@@ -605,6 +621,7 @@
         in_specs=[pl.BlockSpec(memory_space=space) for space in spaces],
         out_specs=tuple(pl.BlockSpec(memory_space=space) for space in out_spaces),
         scratch_shapes=list(scratch),
+        input_output_aliases=aliases or {},
         compiler_params=pltpu.CompilerParams(vmem_limit_bytes=limit),
         cost_estimate=pl.CostEstimate(
             flops=flops, bytes_accessed=bytes_in + bytes_out, transcendentals=0
@@ -691,19 +708,20 @@
         flops=200_000_000,
     )
     first, second = exchange(rim, rim)
-    sol, rest, kept = call(
+    sol, rest, kept, made = call(
         lambda *refs: rest_kernel(staying, *refs),
-        [struct((NODES, count), F32), struct((NODES, count), F32), struct((aggregates, entries), F32)],
-        [diag_block, precond, pack, sol, resid, local_op],
-        [pltpu.VMEM] * 6,
+        [struct((NODES, count), F32), struct((NODES, count), F32), struct((aggregates, entries), F32), struct(made.shape, BF16)],
+        [diag_block, precond, pack, sol, resid, local_op, made, hits],
+        [pltpu.VMEM] * 8,
         flops=1_000_000_000,
     )
     low, send = call(
         send_kernel,
         [struct((NODES, count), BF16), struct((owner_count, chunk, 128), BF16)],
-        [first, second, rest, pack, made, hits],
+        [first, second, rest, pack, hits, made],
         [pltpu.VMEM] * 6,
         flops=50_000_000,
+        aliases={5: 1},
     )
     got = lax.all_to_all(send, "dom", split_axis=0, concat_axis=0, tiled=True)
     outs = [

time: 31.9 us -> 31.8 us (level)
  waiting for transfers between devices: 1.29 us -> 0.97 us
    ppermute x2, waiting for transfers between devices: 1.29 us -> 0.96 us  [exchange(): lax.ppermute(other, 'face', others)]
  transfers between devices with their start and end apart: 4 -> 4, of which waited for: 1 -> 1; matrix products, arithmetic and copies ran while one was open for 0% -> 0% of each run, Pallas kernels for 6% -> 7%
where the time goes in v11:
time: 31.8 us; the launch traced here: 31.6 us
  blocking collectives  17.1 us (54%)
  Pallas kernels  7.49 us (24%)
  starting transfers between devices  4.37 us (14%)
  waiting for transfers between devices  0.97 us (3%)
  local copies, waits for them, and re-layouts  0.94 us (3%)
  between operations  0.72 us (2%)
    all_to_all x1, blocking collectives, per_device(): got = lax.all_to_all(send, 'dom', split_axis=0, concat_axis=0, tiled=True)  17.1 us
    pallas_call x6, Pallas kernels, call(): pl.pallas_call(kernel, out_shape=tuple(outs), in_specs=[pl.BlockSpec(memo...  7.49 us
    ppermute x2, starting transfers between devices, exchange(): lax.ppermute(other, 'face', others)  3.79 us
    ppermute x2, waiting for transfers between devices, exchange(): lax.ppermute(other, 'face', others)  0.96 us
    unnamed x10, local copies, waits for them, and re-layouts  0.94 us
  transfers between devices with their start and end apart: 4, of which 1 were waited for; matrix products, arithmetic and copies ran while one was open for 0% of the time, Pallas kernels for 7%

profile of v11, /device:TPU:0, one launch (start us, length us, event | category | flops | bytes accessed | tf_op | source)
XLA Modules:
  0.0 31.6 jit_solution(9878035694948184998)
XLA Ops:
  0.6 0.0 copy-start
  0.6 0.0 copy-start.1
  0.7 0.0 copy-start.4
  0.7 2.8 %shard_map.121 = (bf16[96,128]{1,0:T(8,128)(2,1)}, bf16[96,128]{1,0:T(8,128)(2,1)}, f32[376,128]{1,0:T(8,128)}) custom-call(bf16[64,64,128]{2,1,0:T(8,128)(2,1)} %refs_0_.5, bf16[64,64,128]{2,1,0:T(8,128)(2,1)} %refs_1_.5, f32[64,128]{1,0:T(8,128)} %refs_2_.1, f32[64,128]{1,0:T(8,128)} %refs_3_.2, f32[6,16,64]{2,1,0:T(8,128)} %refs_4_.1, s32[6,128]{1,0:T(8,128)} %refs_5_.1, ...), custom_call_target="tpu_custom_call" | custom-call | flops 100000000 | bytes 2567168 | tf_op jit(solution)/shard_map/pallas_call | solution.py:618
  3.5 0.5 %collective-permute-start = (bf16[96,128]{1,0:T(8,128)(2,1)}, bf16[96,128]{1,0:T(8,128)(2,1)S(1)}, u32[]{:S(2)}, u32[]{:S(2)}) collective-permute-start(bf16[96,128]{1,0:T(8,128)(2,1)} %get-tuple-element.23), channel_id=1, source_target_pairs={{0,1},{1,0},{2,3},{3,2},{4,5},{5,4},{6,7},{7,6},{8,9},{9,8},{10,11... | collective-permute-start | bytes 73736 | tf_op jit(solution)/shard_map/ppermute | solution.py:667
  4.0 2.6 %collective-permute-start.1 = (bf16[96,128]{1,0:T(8,128)(2,1)}, bf16[96,128]{1,0:T(8,128)(2,1)S(1)}, u32[]{:S(2)}, u32[]{:S(2)}) collective-permute-start(bf16[96,128]{1,0:T(8,128)(2,1)} %get-tuple-element.24), channel_id=1, source_target_pairs={{0,3},{1,2},{2,1},{3,0},{4,7},{5,6},{6,5},{7,4},{8,11},{9,10},{10,... | collective-permute-start | bytes 73736 | tf_op jit(solution)/shard_map/ppermute | solution.py:667
  6.7 0.0 copy-done
  6.7 0.0 copy-done.1
  6.7 0.0 copy-done.4
  6.7 0.0 copy-start.2
  6.7 0.9 %copy-done.2 = f32[376,128]{1,0:T(8,128)S(1)} copy-done((f32[376,128]{1,0:T(8,128)S(1)}, f32[376,128]{1,0:T(8,128)}, u32[]{:S(2)}) %copy-start.2) | copy-done | bytes 192536
  7.6 0.0 copy-start.3
  7.6 1.4 %shard_map.122 = (bf16[8,168,128]{2,1,0:T(8,128)(2,1)S(1)}, bf16[768,128]{1,0:T(8,128)(2,1)S(1)}, bf16[448,256]{1,0:T(8,128)(2,1)S(1)}, f32[64,128]{1,0:T(8,128)S(1)}, f32[64,16,128]{2,1,0:T(8,128)S(1)}) custom-call(bf16[64,64,128]{2,1,0:T(8,128)(2,1)S(1)} %copy-done, bf16[64,64,128]{2,1,0:T(8,128)(2,1)S(1)} %copy-done.1, f32[376,128]{1,0:T(8,128)S(1)} %copy-done.2, ...), custom_call_target="tpu_custom_call" | custom-call | flops 1000000000 | bytes 3747840 | tf_op jit(solution)/shard_map/pallas_call | solution.py:618
  9.0 0.0 collective-permute-done.first_ref
  9.0 0.0 collective-permute-done.1.second_ref
  9.0 0.0 copy-done.3
  9.0 0.7 %shard_map.123 = (f32[64,128]{1,0:T(8,128)S(1)}, f32[64,128]{1,0:T(8,128)S(1)}, f32[16,128]{1,0:T(8,128)S(1)}) custom-call(bf16[96,128]{1,0:T(8,128)(2,1)S(1)} %collective-permute-done.first_ref, bf16[96,128]{1,0:T(8,128)(2,1)S(1)} %collective-permute-done.1.second_ref, bf16[64,64,128]{2,1,0:T(8,128)(2,1)S(1)} %copy-done, ...), custom_call_target="tpu_custom_call" | custom-call | flops 200000000 | bytes 2969600 | tf_op jit(solution)/shard_map/pallas_call | solution.py:618
  9.7 1.1 %collective-permute-start.3 = (f32[16,128]{1,0:T(8,128)S(1)}, f32[16,128]{1,0:T(8,128)S(1)}, u32[]{:S(2)}, u32[]{:S(2)}) collective-permute-start(f32[16,128]{1,0:T(8,128)S(1)} %get-tuple-element.28), channel_id=1, source_target_pairs={{0,3},{1,2},{2,1},{3,0},{4,7},{5,6},{6,5},{7,4},{8,11},{9,10},{10,... | collective-permute-start | bytes 24584 | tf_op jit(solution)/shard_map/ppermute | solution.py:667
  10.9 0.1 collective-permute-start.2
  10.9 1.0 %shard_map.124 = (f32[64,128]{1,0:T(8,128)S(1)}, f32[64,128]{1,0:T(8,128)S(1)}, f32[64,768]{1,0:T(8,128)S(1)}, bf16[8,168,128]{2,1,0:T(8,128)(2,1)S(1)}) custom-call(bf16[64,64,128]{2,1,0:T(8,128)(2,1)S(1)} %copy-done, bf16[64,64,128]{2,1,0:T(8,128)(2,1)S(1)} %copy-done.1, f32[376,128]{1,0:T(8,128)S(1)} %copy-done.3, ...), custom_call_target="tpu_custom_call" | custom-call | flops 1000000000 | bytes 3731456 | tf_op jit(solution)/shard_map/pallas_call | solution.py:618
  11.9 1.0 %collective-permute-done.3.second_ref = f32[16,128]{1,0:T(8,128)S(1)} collective-permute-done((f32[16,128]{1,0:T(8,128)S(1)}, f32[16,128]{1,0:T(8,128)S(1)}, u32[]{:S(2)}, u32[]{:S(2)}) %collective-permute-start.3) | collective-permute-done | bytes 8224 | tf_op jit(solution)/shard_map/ppermute | solution.py:667
  12.9 0.0 collective-permute-done.2.first_ref
  12.9 0.4 %shard_map.125 = (bf16[64,128]{1,0:T(8,128)(2,1)S(1)}, bf16[8,168,128]{2,1,0:T(8,128)(2,1)S(1)}) custom-call(f32[16,128]{1,0:T(8,128)S(1)} %collective-permute-done.2.first_ref, f32[16,128]{1,0:T(8,128)S(1)} %collective-permute-done.3.second_ref, f32[64,128]{1,0:T(8,128)S(1)} %get-tuple-element.34.rest_ref, ...), custom_call_target="tpu_custom_call", output_to_operand_aliasing={{1}: (5, {})} | custom-call | flops 50000000 | bytes 1175552 | tf_op jit(solution)/shard_map/pallas_call | solution.py:618
  13.3 17.1 %all_to_all.5.refs_0_ = bf16[8,168,128]{2,1,0:T(8,128)(2,1)S(1)} all-to-all(bf16[8,168,128]{2,1,0:T(8,128)(2,1)S(1)} %get-tuple-element.36), channel_id=1, replica_groups=mesh['dom'=8,'face'=4] {'dom'}, dimensions={0} | all-to-all | bytes 688128 | tf_op jit(solution)/shard_map/all_to_all | solution.py:726
  30.4 1.2 %shard_map.126 = (f32[64,128]{1,0:T(8,128)}, f32[64,729]{1,0:T(8,128)}, f32[27,64]{1,0:T(8,128)}) custom-call(bf16[8,168,128]{2,1,0:T(8,128)(2,1)S(1)} %all_to_all.5.refs_0_, f32[64,768]{1,0:T(8,128)S(1)} %get-tuple-element.37.refs_1_, bf16[64,128]{1,0:T(8,128)(2,1)S(1)} %get-tuple-element.38.refs_2_, f32[376,128]{1,0:T(8,128)S(1)} %copy-done.3, ...), custom_call_target="tpu_custom_call" | custom-call | flops 100000000 | bytes 1008640 | tf_op jit(solution)/shard_map/pallas_call | solution.py:618
Async XLA Ops:
  0.6 6.0 %copy-start = (bf16[64,64,128]{2,1,0:T(8,128)(2,1)S(1)}, bf16[64,64,128]{2,1,0:T(8,128)(2,1)}, u32[]{:S(2)}) copy-start(bf16[64,64,128]{2,1,0:T(8,128)(2,1)} %refs_0_.5) | copy-start | bytes 3145732
  0.6 6.0 %copy-start.1 = (bf16[64,64,128]{2,1,0:T(8,128)(2,1)S(1)}, bf16[64,64,128]{2,1,0:T(8,128)(2,1)}, u32[]{:S(2)}) copy-start(bf16[64,64,128]{2,1,0:T(8,128)(2,1)} %refs_1_.5) | copy-start | bytes 3145732
  0.7 6.0 %copy-start.4 = (bf16[256,256]{1,0:T(8,128)(2,1)S(1)}, bf16[256,256]{1,0:T(8,128)(2,1)}, u32[]{:S(2)}) copy-start(bf16[256,256]{1,0:T(8,128)(2,1)} %constant.2.clone.refs_9_.refs_3_) | copy-start | bytes 393220
  3.5 5.5 %collective-permute-start = (bf16[96,128]{1,0:T(8,128)(2,1)}, bf16[96,128]{1,0:T(8,128)(2,1)S(1)}, u32[]{:S(2)}, u32[]{:S(2)}) collective-permute-start(bf16[96,128]{1,0:T(8,128)(2,1)} %get-tuple-element.23), channel_id=1, source_target_pairs={{0,1},{1,0},{2,3},{3,2},{4,5},{5,4},{6,7},{7,6},{8,9},{9,8},{10,11... | collective-permute-start | bytes 73736 | tf_op jit(solution)/shard_map/ppermute | solution.py:667
  4.0 5.0 %collective-permute-start.1 = (bf16[96,128]{1,0:T(8,128)(2,1)}, bf16[96,128]{1,0:T(8,128)(2,1)S(1)}, u32[]{:S(2)}, u32[]{:S(2)}) collective-permute-start(bf16[96,128]{1,0:T(8,128)(2,1)} %get-tuple-element.24), channel_id=1, source_target_pairs={{0,3},{1,2},{2,1},{3,0},{4,7},{5,6},{6,5},{7,4},{8,11},{9,10},{10,... | collective-permute-start | bytes 73736 | tf_op jit(solution)/shard_map/ppermute | solution.py:667
  6.7 0.9 %copy-start.2 = (f32[376,128]{1,0:T(8,128)S(1)}, f32[376,128]{1,0:T(8,128)}, u32[]{:S(2)}) copy-start(f32[376,128]{1,0:T(8,128)} %get-tuple-element.25.refs_2_.pack_ref.refs_3_) | copy-start | bytes 577540
  7.6 1.4 %copy-start.3 = (f32[376,128]{1,0:T(8,128)S(1)}, f32[376,128]{1,0:T(8,128)}, u32[]{:S(2)}) copy-start(f32[376,128]{1,0:T(8,128)} %get-tuple-element.25.refs_2_.pack_ref.refs_3_) | copy-start | bytes 577540
  9.7 3.1 %collective-permute-start.3 = (f32[16,128]{1,0:T(8,128)S(1)}, f32[16,128]{1,0:T(8,128)S(1)}, u32[]{:S(2)}, u32[]{:S(2)}) collective-permute-start(f32[16,128]{1,0:T(8,128)S(1)} %get-tuple-element.28), channel_id=1, source_target_pairs={{0,3},{1,2},{2,1},{3,0},{4,7},{5,6},{6,5},{7,4},{8,11},{9,10},{10,... | collective-permute-start | bytes 24584 | tf_op jit(solution)/shard_map/ppermute | solution.py:667
  10.9 2.0 %collective-permute-start.2 = (f32[16,128]{1,0:T(8,128)S(1)}, f32[16,128]{1,0:T(8,128)S(1)}, u32[]{:S(2)}, u32[]{:S(2)}) collective-permute-start(f32[16,128]{1,0:T(8,128)S(1)} %get-tuple-element.28), channel_id=1, source_target_pairs={{0,1},{1,0},{2,3},{3,2},{4,5},{5,4},{6,7},{7,6},{8,9},{9,8},{10,11... | collective-permute-start | bytes 24584 | tf_op jit(solution)/shard_map/ppermute | solution.py:667
